TPU v7x, 128 devices: a whole 4x4x4 slice. The times are simulated.
128 devices in a mesh: views: 4 (over x), tiles: 32 (over z, y, core).
Axes of the slice: x: 4, y: 4, z: 4, core: 2. Of those that a mesh axis runs over, the one named last changes fastest.
Arguments:
- params: float32 [59, 65536], P(None, ('views', 'tiles')), as said below
- first_moment: float32 [59, 65536], P(None, ('views', 'tiles')), may hold values from -6 to 6
- second_moment: float32 [59, 65536], P(None, ('views', 'tiles')), may hold values from 0.5 to 20
- cameras: float32 [4, 6], replicated, may hold values from -0.02 to 0.02
- target: float32 [4, 512, 3, 256], P('views', 'tiles'), may hold values from 0 to 1
- lists: int32 [4, 512, 256], P('views', 'tiles'), may hold values from 0 to 65535, as said below
- lengths: int32 [4, 512], P('views', 'tiles'), may hold values from 32 to 256
Outputs:
- new_params: float32 [59, 65536], P(None, ('views', 'tiles'))
- new_first: float32 [59, 65536], P(None, ('views', 'tiles'))
- new_second: float32 [59, 65536], P(None, ('views', 'tiles'))
Inputs may be any that keep to these rules, and one draw needn't show every extreme that they name: Each entry names a Gaussian by its column in params. The lists of the 16 tiles that one device holds (live entries or not) have exactly 32 entries in the columns of each device's shard of params. `params`: the quaternion's first entry is at least 0.6, the means lie in front of every camera, and the opacity logits are at most -2.
All inputs are finite; a program needn't handle non-finite values.
Results may differ from a plain program's by a relative error of at most 0.0003.
Values sent between devices are 32-bit elements; how exact they have to be, the bound alone decides.
No kernel may reach another device: no remote copies, remote signals or barrier semaphores. Data moves between devices by JAX's collectives and lax.ppermute only.
A program may use at most 128 MiB of HBM per device.

v0:
```python
import jax
import jax.numpy as jnp
import numpy as np
from jax import lax
from jax.sharding import PartitionSpec as P

TILE_SIDE = 16
TILE_COLS = 32
ADAM_STEP = 1000


sh_zero = 0.28209479177387814
sh_first = 0.4886025119029199
sh_second = (
    1.0925484305920792,
    -1.0925484305920792,
    0.31539156525252005,
    -1.0925484305920792,
    0.5462742152960396,
)
sh_third = (
    -0.5900435899266435,
    2.890611442640554,
    -0.4570457994644658,
    0.3731763325901154,
    -0.4570457994644658,
    1.445305721320277,
    -0.5900435899266435,
)
beta_one = 0.9
beta_two = 0.999
adam_eps = 1e-15
learning = np.concatenate(
    [
        np.full(3, 0.00016),
        np.full(3, 0.005),
        np.full(4, 0.001),
        np.full(1, 0.05),
        np.full(3, 0.0025),
        np.full(45, 0.000125),
    ]
).astype(np.float32)[:, None]


def matmul_three(left, right):
    return [
        [
            left[row_at][0] * right[0][col_at]
            + left[row_at][1] * right[1][col_at]
            + left[row_at][2] * right[2][col_at]
            for col_at in range(3)
        ]
        for row_at in range(3)
    ]


def camera_rotation(camera):
    cos_a, sin_a = (jnp.cos(camera[0]), jnp.sin(camera[0]))
    cos_b, sin_b = (jnp.cos(camera[1]), jnp.sin(camera[1]))
    cos_c, sin_c = (jnp.cos(camera[2]), jnp.sin(camera[2]))
    around_x = [[1.0, 0.0, 0.0], [0.0, cos_a, -sin_a], [0.0, sin_a, cos_a]]
    around_y = [[cos_b, 0.0, sin_b], [0.0, 1.0, 0.0], [-sin_b, 0.0, cos_b]]
    around_z = [[cos_c, -sin_c, 0.0], [sin_c, cos_c, 0.0], [0.0, 0.0, 1.0]]
    return matmul_three(around_z, matmul_three(around_y, around_x))


def sh_basis(along_x, along_y, along_z):
    square_x, square_y, square_z = (along_x * along_x, along_y * along_y, along_z * along_z)
    both_xy, both_yz, both_xz = (along_x * along_y, along_y * along_z, along_x * along_z)
    return [
        sh_zero + 0.0 * along_x,
        -sh_first * along_y,
        sh_first * along_z,
        -sh_first * along_x,
        sh_second[0] * both_xy,
        sh_second[1] * both_yz,
        sh_second[2] * (2.0 * square_z - square_x - square_y),
        sh_second[3] * both_xz,
        sh_second[4] * (square_x - square_y),
        sh_third[0] * along_y * (3.0 * square_x - square_y),
        sh_third[1] * both_xy * along_z,
        sh_third[2] * along_y * (4.0 * square_z - square_x - square_y),
        sh_third[3] * along_z * (2.0 * square_z - 3.0 * square_x - 3.0 * square_y),
        sh_third[4] * along_x * (4.0 * square_z - square_x - square_y),
        sh_third[5] * along_z * (square_x - square_y),
        sh_third[6] * along_x * (square_x - 3.0 * square_y),
    ]


def project(params, camera, focal_len, center_x, center_y):
    rotation = camera_rotation(camera)
    means = [params[0], params[1], params[2]]
    point = [
        rotation[axis_at][0] * means[0]
        + rotation[axis_at][1] * means[1]
        + rotation[axis_at][2] * means[2]
        + camera[3 + axis_at]
        for axis_at in range(3)
    ]
    inverse_z = 1.0 / point[2]
    screen_u = focal_len * point[0] * inverse_z + center_x
    screen_v = focal_len * point[1] * inverse_z + center_y
    scales = jnp.exp(params[3:6])
    unit_quat = params[6:10] * lax.rsqrt(jnp.sum(params[6:10] * params[6:10], axis=0))
    real_part, imag_x, imag_y, imag_z = (unit_quat[0], unit_quat[1], unit_quat[2], unit_quat[3])
    spin = [
        [
            1.0 - 2.0 * (imag_y * imag_y + imag_z * imag_z),
            2.0 * (imag_x * imag_y - real_part * imag_z),
            2.0 * (imag_x * imag_z + real_part * imag_y),
        ],
        [
            2.0 * (imag_x * imag_y + real_part * imag_z),
            1.0 - 2.0 * (imag_x * imag_x + imag_z * imag_z),
            2.0 * (imag_y * imag_z - real_part * imag_x),
        ],
        [
            2.0 * (imag_x * imag_z - real_part * imag_y),
            2.0 * (imag_y * imag_z + real_part * imag_x),
            1.0 - 2.0 * (imag_x * imag_x + imag_y * imag_y),
        ],
    ]
    turned = matmul_three(rotation, spin)
    shaped = [
        [turned[row_at][col_at] * scales[col_at] for col_at in range(3)] for row_at in range(3)
    ]
    near_x = [
        focal_len * inverse_z * shaped[0][col_at]
        - focal_len * point[0] * inverse_z * inverse_z * shaped[2][col_at]
        for col_at in range(3)
    ]
    near_y = [
        focal_len * inverse_z * shaped[1][col_at]
        - focal_len * point[1] * inverse_z * inverse_z * shaped[2][col_at]
        for col_at in range(3)
    ]
    cov_a = near_x[0] * near_x[0] + near_x[1] * near_x[1] + near_x[2] * near_x[2] + 0.3
    cov_b = near_x[0] * near_y[0] + near_x[1] * near_y[1] + near_x[2] * near_y[2]
    cov_c = near_y[0] * near_y[0] + near_y[1] * near_y[1] + near_y[2] * near_y[2] + 0.3
    determinant = cov_a * cov_c - cov_b * cov_b
    offset = [
        means[axis_at]
        + rotation[0][axis_at] * camera[3]
        + rotation[1][axis_at] * camera[4]
        + rotation[2][axis_at] * camera[5]
        for axis_at in range(3)
    ]
    inverse_len = lax.rsqrt(offset[0] * offset[0] + offset[1] * offset[1] + offset[2] * offset[2])
    basis = sh_basis(offset[0] * inverse_len, offset[1] * inverse_len, offset[2] * inverse_len)
    colors = [
        0.5 + sum((basis[coef_at] * params[11 + 3 * coef_at + channel] for coef_at in range(16)))
        for channel in range(3)
    ]
    opacity = jax.nn.sigmoid(params[10])
    return jnp.stack(
        [
            screen_u,
            screen_v,
            cov_c / determinant,
            -cov_b / determinant,
            cov_a / determinant,
            opacity,
            colors[0],
            colors[1],
            colors[2],
        ]
    )


def composite(picked, lengths, target, first_tile):
    tile_count = picked.shape[1]
    list_size = picked.shape[2]
    tile_ids = first_tile + jnp.arange(tile_count, dtype=jnp.int32)
    pixel_ids = jnp.arange(TILE_SIDE * TILE_SIDE, dtype=jnp.int32)
    pixel_x = (tile_ids % TILE_COLS * TILE_SIDE)[:, None] + (pixel_ids % TILE_SIDE)[None, :]
    pixel_y = (tile_ids // TILE_COLS * TILE_SIDE)[:, None] + (pixel_ids // TILE_SIDE)[None, :]
    delta_x = pixel_x.astype(jnp.float32)[:, None, :] + 0.5 - picked[0][:, :, None]
    delta_y = pixel_y.astype(jnp.float32)[:, None, :] + 0.5 - picked[1][:, :, None]
    quadric = (
        picked[2][:, :, None] * delta_x * delta_x
        + 2.0 * picked[3][:, :, None] * delta_x * delta_y
        + picked[4][:, :, None] * delta_y * delta_y
    )
    live_mask = jnp.arange(list_size, dtype=jnp.int32)[None, :] < lengths[:, None]
    alphas = jnp.where(live_mask[:, :, None], picked[5][:, :, None] * jnp.exp(-0.5 * quadric), 0.0)
    log_keep = jnp.log1p(-alphas)
    weight = jnp.exp(jnp.cumsum(log_keep, axis=1) - log_keep) * alphas
    render = jnp.stack(
        [jnp.sum(weight * picked[6 + channel][:, :, None], axis=1) for channel in range(3)], axis=1
    )
    return jnp.sum(jnp.abs(render - target))


def adam_update(params, first_moment, second_moment, gradient):
    new_first = beta_one * first_moment + (1.0 - beta_one) * gradient
    new_second = beta_two * second_moment + (1.0 - beta_two) * gradient * gradient
    step_size = learning * (new_first / (1.0 - beta_one**ADAM_STEP))
    new_params = params - step_size / (
        jnp.sqrt(new_second / (1.0 - beta_two**ADAM_STEP)) + adam_eps
    )
    return (new_params, new_first, new_second)


def select_rows(piece, positions):
    width_here = piece.shape[1]
    inside = (positions >= 0) & (positions < width_here)
    values = jnp.take(piece, jnp.clip(positions, 0, width_here - 1), axis=1)
    return jnp.where(inside[None, :], values, 0.0)


def spread_rows(row_grads, positions, block_rows):
    width_here = block_rows * 128
    inside = (positions >= 0) & (positions < width_here)
    dense_rows = jnp.zeros((row_grads.shape[0], width_here), jnp.float32)
    dense_rows = dense_rows.at[:, jnp.clip(positions, 0, width_here - 1)].add(
        jnp.where(inside[None, :], row_grads, 0.0)
    )
    return dense_rows.reshape(row_grads.shape[0], block_rows, 128).transpose(1, 0, 2)


def per_device(params, first_moment, second_moment, cameras, target, lists, lengths):
    view_count = lax.axis_size("views")
    tile_groups = lax.axis_size("tiles")
    my_view = lax.axis_index("views")
    my_tiles = lax.axis_index("tiles")
    owned = params.shape[1]
    tile_dev = target.shape[1]
    list_size = lists.shape[2]
    width = TILE_COLS * TILE_SIDE
    height = tile_dev * tile_groups // TILE_COLS * TILE_SIDE
    focal_len = float(width)

    def all_views(values):
        return jnp.stack(
            [
                project(values, cameras[camera_at], focal_len, 0.5 * width, 0.5 * height)
                for camera_at in range(view_count)
            ]
        )

    projected, pullback = jax.vjp(all_views, params)
    entries = lists[0].reshape(-1)
    picked = select_rows(
        lax.dynamic_index_in_dim(
            lax.all_gather(projected, ("views", "tiles"), axis=2, tiled=True),
            my_view,
            0,
            keepdims=False,
        ),
        entries,
    )
    per_block = 4
    block_count = tile_dev // per_block
    blocks = (
        picked.reshape(-1, block_count, per_block, list_size).transpose(1, 0, 2, 3),
        lengths[0].reshape(block_count, per_block),
        target[0].reshape(block_count, per_block, 3, -1),
        my_tiles * tile_dev + jnp.arange(block_count, dtype=jnp.int32) * per_block,
    )

    def block_gradient(block):
        chosen, block_len, block_target, first_tile = block
        _, pull_block = jax.vjp(
            lambda inner: composite(inner, block_len, block_target, first_tile), chosen
        )
        return pull_block(jnp.ones((), jnp.float32))[0]

    row_grads = (
        lax.map(block_gradient, blocks).transpose(1, 0, 2, 3).reshape(projected.shape[1], -1)
    )
    selector = (jnp.arange(view_count) == my_view).astype(jnp.float32)
    shares = lax.psum_scatter(
        spread_rows(row_grads, entries, owned // 128 * lax.axis_size(("views", "tiles")))[:, None]
        * selector[None, :, None, None],
        ("views", "tiles"),
        scatter_dimension=0,
        tiled=True,
    )
    owner_grads = shares.transpose(1, 2, 0, 3).reshape(view_count, -1, owned)
    gradient = pullback(owner_grads)[0]
    return adam_update(params, first_moment, second_moment, gradient)


def solution(mesh):
    placed = (
        P(None, ("views", "tiles")),
        P(None, ("views", "tiles")),
        P(None, ("views", "tiles")),
        P(),
        P("views", "tiles", None, None),
        P("views", "tiles", None),
        P("views", "tiles"),
    )
    return jax.shard_map(
        per_device,
        mesh=mesh,
        in_specs=placed,
        out_specs=(
            P(None, ("views", "tiles")),
            P(None, ("views", "tiles")),
            P(None, ("views", "tiles")),
        ),
        check_vma=False,
    )
```

profile of v0, /device:TPU:1, one launch (start us, length us, event | category | flops | bytes accessed | tf_op | source)
XLA Modules:
  0.0 631.5 jit_solution(7285283560596323478)
XLA Ops:
  69.9 3.5 fusion.300
  77.6 3.5 fusion.302
  93.3 79.9 %all-gather.2.cloned.1.call-done = f32[4,9,65536]{2,1,0:T(8,128)} async-done(((f32[4,9,512]{2,1,0:T(8,128)}), f32[4,9,65536]{2,1,0:T(8,128)}) %all-gather.2.cloned.1.call-update) | async-done | bytes 9437200 | tf_op jit(solution)/shard_map/all_gather | solution.py:245
  173.2 4.4 constant_dynamic-slice_fusion.9
  177.6 17.0 %copy.51 = f32[1,9,65536]{1,2,0:T(8,128)} copy(f32[1,9,65536]{2,1,0:T(8,128)} %constant_dynamic-slice_fusion.9) | data formatting | bytes 4718592 | tf_op jit(solution)/shard_map/jit(dynamic_index_in_dim)/dynamic_slice | solution.py:244
  194.5 21.3 %gather_fusion = f32[4096,9]{1,0:T(8,128)S(1)} fusion(f32[9,65536]{0,1:T(8,128)} %bitcast.224, s32[4096]{0:T(1024)S(1)} %broadcast_clamp_fusion), kind=kCustom, calls=%fused_computation | custom fusion | bytes 311296 | tf_op jit(solution)/shard_map/jit(_take)/gather | solution.py:207
  217.2 152.1 %while.13 = (s32[]{:T(128)}, f32[4,9,4,256]{3,2,1,0:T(4,128)}, s32[4,4]{1,0:T(4,128)}, f32[4,9,4,256]{3,2,1,0:T(4,128)}, s32[4]{0:T(128)}, /*index=5*/f32[4,4,3,...) while((s32[]{:T(128)}, f32[4,9,4,256]{3,2,1,0:T(4,128)}, ...), condition=%wide.region_18.19_spmd, body=%wide.region_1.18_spmd.sunk | while | flops 97887840 | bytes 26980316 | solution.py:269
  221.8 4.4 fusion.321
  233.2 12.4 %fusion.323 = f32[4,256,2,128]{1,2,3,0:T(2,128)S(1)} fusion(f32[4,256,2,128]{1,2,3,0:T(2,128)S(1)} %broadcast_add_fusion.12, f32[4,256,2,128]{1,2,3,0:T(2,128)S(1)} %fusion.321, f32[4,2,128]{1,2,0:T(8,128)S(1)} %copy.79, f32[4,256]{1,0:T(4,128)S(1)} %get-tuple-element.862, f32[4,2,128]{1,2,0:T(8,128)} %copy.80, ...), kind=kOutput, calls=%fused_computation.50.clone.1 | output fusion | flops 35651584 | bytes 3170304 | tf_op jit(solution)/shard_map/reduce-window.18
  248.3 3.8 multiply_reduce_fusion.15
  259.8 4.4 fusion.321
  271.2 12.4 %fusion.323 = f32[4,256,2,128]{1,2,3,0:T(2,128)S(1)} fusion(f32[4,256,2,128]{1,2,3,0:T(2,128)S(1)} %broadcast_add_fusion.12, f32[4,256,2,128]{1,2,3,0:T(2,128)S(1)} %fusion.321, f32[4,2,128]{1,2,0:T(8,128)S(1)} %copy.79, f32[4,256]{1,0:T(4,128)S(1)} %get-tuple-element.862, f32[4,2,128]{1,2,0:T(8,128)} %copy.80, ...), kind=kOutput, calls=%fused_computation.50.clone.1 | output fusion | flops 35651584 | bytes 3170304 | tf_op jit(solution)/shard_map/reduce-window.18
  286.4 3.8 multiply_reduce_fusion.15
  297.9 4.4 fusion.321
  309.2 12.4 %fusion.323 = f32[4,256,2,128]{1,2,3,0:T(2,128)S(1)} fusion(f32[4,256,2,128]{1,2,3,0:T(2,128)S(1)} %broadcast_add_fusion.12, f32[4,256,2,128]{1,2,3,0:T(2,128)S(1)} %fusion.321, f32[4,2,128]{1,2,0:T(8,128)S(1)} %copy.79, f32[4,256]{1,0:T(4,128)S(1)} %get-tuple-element.862, f32[4,2,128]{1,2,0:T(8,128)} %copy.80, ...), kind=kOutput, calls=%fused_computation.50.clone.1 | output fusion | flops 35651584 | bytes 3170304 | tf_op jit(solution)/shard_map/reduce-window.18
  324.4 3.8 multiply_reduce_fusion.15
  335.9 4.4 fusion.321
  347.2 12.4 %fusion.323 = f32[4,256,2,128]{1,2,3,0:T(2,128)S(1)} fusion(f32[4,256,2,128]{1,2,3,0:T(2,128)S(1)} %broadcast_add_fusion.12, f32[4,256,2,128]{1,2,3,0:T(2,128)S(1)} %fusion.321, f32[4,2,128]{1,2,0:T(8,128)S(1)} %copy.79, f32[4,256]{1,0:T(4,128)S(1)} %get-tuple-element.862, f32[4,2,128]{1,2,0:T(8,128)} %copy.80, ...), kind=kOutput, calls=%fused_computation.50.clone.1 | output fusion | flops 35651584 | bytes 3170304 | tf_op jit(solution)/shard_map/reduce-window.18
  362.4 3.8 multiply_reduce_fusion.15
  371.7 35.6 %scatter_custom_fusion = f32[9,65536]{0,1:T(8,128)} fusion(s32[4096]{0:T(1024)} %bitcast.265, f32[4096,9]{1,0:T(8,128)S(1)} %copy.55, f32[]{:T(128)} %constant.226.clone.1), kind=kCustom, calls=%fused_computation.120 | custom fusion | flops 36864 | bytes 2359808 | tf_op jit(solution)/shard_map/scatter-add | solution.py:215
  407.3 18.1 %copy.56 = f32[512,9,128]{2,0,1:T(8,128)S(1)} copy(f32[512,9,128]{1,2,0:T(8,128)} %bitcast.223) | data formatting | bytes 4718592 | tf_op jit(solution)/shard_map/transpose | solution.py:218
  425.8 4.7 broadcast_multiply_fusion
  430.5 163.1 %all-reduce.284.cloned.1.call-done = f32[512,4,9,128]{3,0,2,1:T(8,128)} async-done(((f32[512,4,9,128]{3,0,2,1:T(8,128)}), f32[512,4,9,128]{3,0,2,1:T(8,128)}) %all-reduce.284.cloned.1.call-update) | async-done | bytes 9437200
  621.0 3.7 divide_subtract_fusion
  (557 shorter events, 138.0 us)
Async XLA Ops:
  7.2 166.0 %all-gather.2.cloned.1.call-start = ((), (), s32[]{:S(2)}) async-start(), calls=%async_computation | async-start | bytes 16908288 | tf_op jit(solution)/shard_map/all_gather | solution.py:245
  86.3 507.3 %all-reduce.284.cloned.1.call-start = ((), (), s32[]{:S(2)}) async-start(), calls=%async_computation.1 | async-start | bytes 18874368
  425.5 190.4 %copy-start.14 = (f32[1,512]{1,0:T(1,128)S(1)}, f32[1,512]{1,0:T(1,128)}, u32[]{:S(2)}) copy-start(f32[1,512]{1,0:T(1,128)} %copy-done.13) | copy-start | bytes 6148
  425.5 190.4 %copy-start.16 = (f32[1,512]{1,0:T(1,128)S(1)}, f32[1,512]{1,0:T(1,128)}, u32[]{:S(2)}) copy-start(f32[1,512]{1,0:T(1,128)} %copy-done.15) | copy-start | bytes 6148
  425.5 190.4 %copy-start.18 = (f32[1,512]{1,0:T(1,128)S(1)}, f32[1,512]{1,0:T(1,128)}, u32[]{:S(2)}) copy-start(f32[1,512]{1,0:T(1,128)} %copy-done.17) | copy-start | bytes 6148
  425.5 190.4 %copy-start.56 = (f32[1,512]{1,0:T(1,128)S(1)}, f32[1,512]{1,0:T(1,128)}, u32[]{:S(2)}) copy-start(f32[1,512]{1,0:T(1,128)} %copy-done.55) | copy-start | bytes 6148
  425.6 191.3 %copy-start.54 = (f32[1,512]{1,0:T(1,128)S(1)}, f32[1,512]{1,0:T(1,128)}, u32[]{:S(2)}) copy-start(f32[1,512]{1,0:T(1,128)} %get-tuple-element.313) | copy-start | bytes 6148
  425.6 192.4 %copy-start.8 = (f32[1,512]{1,0:T(1,128)S(1)}, f32[1,512]{1,0:T(1,128)}, u32[]{:S(2)}) copy-start(f32[1,512]{1,0:T(1,128)} %copy-done.7) | copy-start | bytes 6148
  425.6 192.4 %copy-start.10 = (f32[1,512]{1,0:T(1,128)S(1)}, f32[1,512]{1,0:T(1,128)}, u32[]{:S(2)}) copy-start(f32[1,512]{1,0:T(1,128)} %copy-done.9) | copy-start | bytes 6148
  425.6 192.4 %copy-start.12 = (f32[1,512]{1,0:T(1,128)S(1)}, f32[1,512]{1,0:T(1,128)}, u32[]{:S(2)}) copy-start(f32[1,512]{1,0:T(1,128)} %copy-done.11) | copy-start | bytes 6148
  425.7 192.4 %copy-start.33 = (f32[1,512]{1,0:T(1,128)S(1)}, f32[1,512]{1,0:T(1,128)}, u32[]{:S(2)}) copy-start(f32[1,512]{1,0:T(1,128)} %copy-done.32) | copy-start | bytes 6148
  425.7 192.4 %copy-start.35 = (f32[1,512]{1,0:T(1,128)S(1)}, f32[1,512]{1,0:T(1,128)}, u32[]{:S(2)}) copy-start(f32[1,512]{1,0:T(1,128)} %copy-done.34) | copy-start | bytes 6148
  425.7 192.4 %copy-start.37 = (f32[1,512]{1,0:T(1,128)S(1)}, f32[1,512]{1,0:T(1,128)}, u32[]{:S(2)}) copy-start(f32[1,512]{1,0:T(1,128)} %copy-done.36) | copy-start | bytes 6148
  425.7 192.4 %copy-start.39 = (f32[1,512]{1,0:T(1,128)S(1)}, f32[1,512]{1,0:T(1,128)}, u32[]{:S(2)}) copy-start(f32[1,512]{1,0:T(1,128)} %copy-done.38) | copy-start | bytes 6148
  425.7 192.4 %copy-start.41 = (f32[1,512]{1,0:T(1,128)S(1)}, f32[1,512]{1,0:T(1,128)}, u32[]{:S(2)}) copy-start(f32[1,512]{1,0:T(1,128)} %copy-done.40) | copy-start | bytes 6148
  425.7 192.4 %copy-start.43 = (f32[1,512]{1,0:T(1,128)S(1)}, f32[1,512]{1,0:T(1,128)}, u32[]{:S(2)}) copy-start(f32[1,512]{1,0:T(1,128)} %copy-done.42) | copy-start | bytes 6148
  425.7 192.4 %copy-start.45 = (f32[1,512]{1,0:T(1,128)S(1)}, f32[1,512]{1,0:T(1,128)}, u32[]{:S(2)}) copy-start(f32[1,512]{1,0:T(1,128)} %copy-done.44) | copy-start | bytes 6148
  425.7 192.4 %copy-start.47 = (f32[1,512]{1,0:T(1,128)S(1)}, f32[1,512]{1,0:T(1,128)}, u32[]{:S(2)}) copy-start(f32[1,512]{1,0:T(1,128)} %copy-done.46) | copy-start | bytes 6148
  425.7 192.4 %copy-start.49 = (f32[1,512]{1,0:T(1,128)S(1)}, f32[1,512]{1,0:T(1,128)}, u32[]{:S(2)}) copy-start(f32[1,512]{1,0:T(1,128)} %copy-done.48) | copy-start | bytes 6148
  425.7 192.4 %copy-start.51 = (f32[1,512]{1,0:T(1,128)S(1)}, f32[1,512]{1,0:T(1,128)}, u32[]{:S(2)}) copy-start(f32[1,512]{1,0:T(1,128)} %copy-done.50) | copy-start | bytes 6148
  425.8 192.4 %copy-start.53 = (f32[1,512]{1,0:T(1,128)S(1)}, f32[1,512]{1,0:T(1,128)}, u32[]{:S(2)}) copy-start(f32[1,512]{1,0:T(1,128)} %copy-done.52) | copy-start | bytes 6148
  425.8 193.2 %copy-start.31 = (f32[1,512]{1,0:T(1,128)S(1)}, f32[1,512]{1,0:T(1,128)}, u32[]{:S(2)}) copy-start(f32[1,512]{1,0:T(1,128)} %get-tuple-element.257) | copy-start | bytes 6148
  430.5 190.5 %copy-start.2 = (f32[59,512]{1,0:T(8,128)S(1)}, f32[59,512]{1,0:T(8,128)}, u32[]{:S(2)}) copy-start(f32[59,512]{1,0:T(8,128)} %param.11) | copy-start | bytes 362500
  430.5 190.5 %copy-start.3 = (f32[59,512]{1,0:T(8,128)S(1)}, f32[59,512]{1,0:T(8,128)}, u32[]{:S(2)}) copy-start(f32[59,512]{1,0:T(8,128)} %param.12) | copy-start | bytes 362500
  (102 other events, 4319.9 us)
Sparse Core Ops, SparseCore 0:
  86.4 86.6 all-gather.1
  430.6 162.9 all-reduce.283
where the time goes:
time: 636 us; the launch traced here: 631 us
  waiting for transfers between devices  243 us (38%)
  other arithmetic  234 us (37%)
  local copies, waits for them, and re-layouts  97.6 us (15%)
  between operations  55.4 us (9%)
    unnamed x3, waiting for transfers between devices  163 us
    all_gather x1, waiting for transfers between devices, per_device(): lax.all_gather(projected, ('views', 'tiles'), axis=2, tiled=True)  79.9 us
    another operation x24, other arithmetic  63.9 us
    scatter-add x1, other arithmetic, spread_rows(): dense_rows.at[:, jnp.clip(positions, 0, width_here - 1)]  35.6 us
    gather x2, local copies, waits for them, and re-layouts, select_rows(): values = jnp.take(piece, jnp.clip(positions, 0, width_here - 1), axis=1)  21.9 us
    dynamic_slice x2, local copies, waits for them, and re-layouts, per_device(): lax.dynamic_index_in_dim(lax.all_gather(projected, ('views', 'tiles'), ax...  21.4 us
    transpose x1, local copies, waits for them, and re-layouts, spread_rows(): dense_rows.reshape(row_grads.shape[0], block_rows, 128).transpose(1, 0, 2)  18.1 us
    select_n x4, other arithmetic, composite(): jnp.where(live_mask[:, :, None], picked[5][:, :, None] * jnp.exp(-0.5 * q...  17.7 us
  transfers between devices with their start and end apart: 2, of which 2 were waited for; matrix products, arithmetic and copies ran while one was open for 1% of the time, Pallas kernels for 0%

commit v1 on v0

v1 whole, which is shorter than its diff:
```python
import jax
import jax.numpy as jnp
import numpy as np
from jax import lax
from jax.experimental import pallas as pl
from jax.experimental.pallas import tpu as pltpu
from jax.sharding import PartitionSpec as P

TILE_SIDE = 16
TILE_COLS = 32
ADAM_STEP = 1000
GROUP = 8
LANES = 128
VIEWS = 4
SLOTS = 32
FEATURES = 9
AXES = ("views", "tiles")

f32 = jnp.float32
bf16 = jnp.bfloat16
i32 = jnp.int32

sh_zero = 0.28209479177387814
sh_first = 0.4886025119029199
sh_second = (
    1.0925484305920792,
    -1.0925484305920792,
    0.31539156525252005,
    -1.0925484305920792,
    0.5462742152960396,
)
sh_third = (
    -0.5900435899266435,
    2.890611442640554,
    -0.4570457994644658,
    0.3731763325901154,
    -0.4570457994644658,
    1.445305721320277,
    -0.5900435899266435,
)
beta_one = 0.9
beta_two = 0.999
adam_eps = 1e-15


def matmul_three(left, right):
    return [
        [
            left[row_at][0] * right[0][col_at]
            + left[row_at][1] * right[1][col_at]
            + left[row_at][2] * right[2][col_at]
            for col_at in range(3)
        ]
        for row_at in range(3)
    ]


def rotation_entries(cos, sin):
    cos_a, cos_b, cos_c = cos
    sin_a, sin_b, sin_c = sin
    return [
        [cos_c * cos_b, cos_c * sin_b * sin_a - sin_c * cos_a, cos_c * sin_b * cos_a + sin_c * sin_a],
        [sin_c * cos_b, sin_c * sin_b * sin_a + cos_c * cos_a, sin_c * sin_b * cos_a - cos_c * sin_a],
        [-sin_b, cos_b * sin_a, cos_b * cos_a],
    ]


def sh_basis(along_x, along_y, along_z):
    square_x, square_y, square_z = (along_x * along_x, along_y * along_y, along_z * along_z)
    both_xy, both_yz, both_xz = (along_x * along_y, along_y * along_z, along_x * along_z)
    return [
        sh_zero + 0.0 * along_x,
        -sh_first * along_y,
        sh_first * along_z,
        -sh_first * along_x,
        sh_second[0] * both_xy,
        sh_second[1] * both_yz,
        sh_second[2] * (2.0 * square_z - square_x - square_y),
        sh_second[3] * both_xz,
        sh_second[4] * (square_x - square_y),
        sh_third[0] * along_y * (3.0 * square_x - square_y),
        sh_third[1] * both_xy * along_z,
        sh_third[2] * along_y * (4.0 * square_z - square_x - square_y),
        sh_third[3] * along_z * (2.0 * square_z - 3.0 * square_x - 3.0 * square_y),
        sh_third[4] * along_x * (4.0 * square_z - square_x - square_y),
        sh_third[5] * along_z * (square_x - square_y),
        sh_third[6] * along_x * (square_x - 3.0 * square_y),
    ]


def project(params, rotation, shift, focal_len, center_x, center_y):
    means = params[:3]
    point = [
        rotation[axis_at][0] * means[0]
        + rotation[axis_at][1] * means[1]
        + rotation[axis_at][2] * means[2]
        + shift[axis_at]
        for axis_at in range(3)
    ]
    inverse_z = 1.0 / point[2]
    screen_u = focal_len * point[0] * inverse_z + center_x
    screen_v = focal_len * point[1] * inverse_z + center_y
    scales = [jnp.exp(params[3 + axis_at]) for axis_at in range(3)]
    quat = params[6:10]
    inverse_norm = lax.rsqrt(
        quat[0] * quat[0] + quat[1] * quat[1] + quat[2] * quat[2] + quat[3] * quat[3]
    )
    real_part, imag_x, imag_y, imag_z = [part * inverse_norm for part in quat]
    spin = [
        [
            1.0 - 2.0 * (imag_y * imag_y + imag_z * imag_z),
            2.0 * (imag_x * imag_y - real_part * imag_z),
            2.0 * (imag_x * imag_z + real_part * imag_y),
        ],
        [
            2.0 * (imag_x * imag_y + real_part * imag_z),
            1.0 - 2.0 * (imag_x * imag_x + imag_z * imag_z),
            2.0 * (imag_y * imag_z - real_part * imag_x),
        ],
        [
            2.0 * (imag_x * imag_z - real_part * imag_y),
            2.0 * (imag_y * imag_z + real_part * imag_x),
            1.0 - 2.0 * (imag_x * imag_x + imag_y * imag_y),
        ],
    ]
    turned = matmul_three(rotation, spin)
    shaped = [
        [turned[row_at][col_at] * scales[col_at] for col_at in range(3)] for row_at in range(3)
    ]
    near_x = [
        focal_len * inverse_z * shaped[0][col_at]
        - focal_len * point[0] * inverse_z * inverse_z * shaped[2][col_at]
        for col_at in range(3)
    ]
    near_y = [
        focal_len * inverse_z * shaped[1][col_at]
        - focal_len * point[1] * inverse_z * inverse_z * shaped[2][col_at]
        for col_at in range(3)
    ]
    cov_a = near_x[0] * near_x[0] + near_x[1] * near_x[1] + near_x[2] * near_x[2] + 0.3
    cov_b = near_x[0] * near_y[0] + near_x[1] * near_y[1] + near_x[2] * near_y[2]
    cov_c = near_y[0] * near_y[0] + near_y[1] * near_y[1] + near_y[2] * near_y[2] + 0.3
    determinant = cov_a * cov_c - cov_b * cov_b
    offset = [
        means[axis_at]
        + rotation[0][axis_at] * shift[0]
        + rotation[1][axis_at] * shift[1]
        + rotation[2][axis_at] * shift[2]
        for axis_at in range(3)
    ]
    inverse_len = lax.rsqrt(offset[0] * offset[0] + offset[1] * offset[1] + offset[2] * offset[2])
    basis = sh_basis(offset[0] * inverse_len, offset[1] * inverse_len, offset[2] * inverse_len)
    colors = [
        0.5 + sum((basis[coef_at] * params[11 + 3 * coef_at + channel] for coef_at in range(16)))
        for channel in range(3)
    ]
    log_opacity = params[10] - jnp.log1p(jnp.exp(params[10]))
    return [
        screen_u,
        screen_v,
        cov_c / determinant,
        -cov_b / determinant,
        cov_a / determinant,
        log_opacity,
        colors[0],
        colors[1],
        colors[2],
    ]


def camera_terms(cameras_ref, owned):
    cameras = cameras_ref[...]
    cos, sin = jnp.cos(cameras), jnp.sin(cameras)

    def column(values, at):
        return jnp.broadcast_to(values[:, at : at + 1], (VIEWS, owned))

    rotation = rotation_entries(
        [column(cos, at) for at in range(3)], [column(sin, at) for at in range(3)]
    )
    return rotation, [column(cameras, 3 + at) for at in range(3)]


def iota(shape, dim):
    return lax.broadcasted_iota(i32, shape, dim)


def dot(left, right, left_dim, right_dim):
    return lax.dot_general(
        left, right, (((left_dim,), (right_dim,)), ((), ())), preferred_element_type=f32
    )


def pieces(values, count):
    out = []
    for at in range(count):
        part = values.astype(bf16)
        out.append(part)
        if at + 1 < count:
            values = values - part.astype(f32)
    return out


def rank_kernel(owned, entries_ref, rank_ref, request_ref):
    chunks = entries_ref.shape[0]
    entries = entries_ref[...]
    owner = lax.rem(lax.div(entries, owned), LANES)
    column = lax.rem(entries, owned)
    low = lax.rem(column, 256).astype(f32)
    high = lax.div(column, 256).astype(f32)
    before = jnp.where(iota((LANES, LANES), 0) < iota((LANES, LANES), 1), 1.0, 0.0)
    adder = jnp.concatenate([before, jnp.ones((LANES, LANES), f32)], axis=1).astype(bf16)
    owner_id = iota((LANES, LANES), 0)
    slot_id = iota((SLOTS, LANES), 0)
    base = jnp.zeros((LANES, LANES), f32)
    requests = jnp.zeros((LANES, 2 * SLOTS), f32)
    for at in range(chunks):
        hot = owner_id == owner[at : at + 1, :]
        hot_one = jnp.where(hot, 1.0, 0.0).astype(bf16)
        counts = dot(hot_one, adder, 1, 0)
        rank = jnp.sum(
            jnp.where(hot, counts[:, :LANES] + base, 0.0), axis=0, keepdims=True
        ).astype(i32)
        base = base + counts[:, LANES:]
        rank_ref[at : at + 1, :] = rank
        slot = slot_id == rank
        wanted = jnp.concatenate(
            [
                jnp.where(slot, low[at : at + 1, :], 0.0),
                jnp.where(slot, high[at : at + 1, :], 0.0),
            ],
            axis=0,
        ).astype(bf16)
        requests = requests + dot(hot_one, wanted, 1, 1)
    request_ref[...] = requests[:, :SLOTS] + 256.0 * requests[:, SLOTS:]


def flipped_requests(asked_ref):
    asked = asked_ref[...]
    wide = jnp.concatenate([asked, jnp.zeros((LANES, LANES - SLOTS), f32)], axis=1)
    return wide.T[:SLOTS, :].astype(i32)


def answer_kernel(frame, params_ref, cameras_ref, asked_ref, rows_ref):
    owned = params_ref.shape[1]
    rotation, shift = camera_terms(cameras_ref, owned)
    params = [jnp.broadcast_to(params_ref[at : at + 1, :], (VIEWS, owned)) for at in range(59)]
    projected = project(params, rotation, shift, *frame)
    asked = flipped_requests(asked_ref)
    chunk_of = lax.div(asked, LANES)
    lane_of = lax.rem(asked, LANES)
    view_of = lax.div(iota((SLOTS, LANES), 1), LANES // VIEWS)
    chosen = [jnp.zeros((SLOTS, LANES), f32) for _ in range(FEATURES)]
    for view in range(VIEWS):
        for chunk in range(owned // LANES):
            mask = (view_of == view) & (chunk_of == chunk)
            for at in range(FEATURES):
                source = jnp.broadcast_to(
                    projected[at][view : view + 1, chunk * LANES : (chunk + 1) * LANES],
                    (SLOTS, LANES),
                )
                found = jnp.take_along_axis(source, lane_of, axis=1, mode="promise_in_bounds")
                chosen[at] = jnp.where(mask, found, chosen[at])
    for part in range(3):
        stack = chosen[4 * part : 4 * part + 4]
        while len(stack) < 4:
            stack.append(jnp.zeros((SLOTS, LANES), f32))
        rows_ref[:, part * LANES : (part + 1) * LANES] = jnp.concatenate(stack, axis=0).T


def tile_kernel(
    owned,
    entries_ref,
    rank_ref,
    rows_ref,
    target_ref,
    grads_ref,
    source_ref,
    coef_ref,
    color_ref,
    alpha_ref,
    weight_ref,
    moment_ref,
    grad_ref,
):
    chunks = entries_ref.shape[0]
    groups = 2
    per_group = chunks // groups
    pixels = TILE_SIDE * TILE_SIDE
    steps = LANES // GROUP
    first_tile = lax.axis_index("tiles") * (groups * GROUP)

    for part in range(3):
        source_ref[part * LANES : (part + 1) * LANES, :] = rows_ref[
            :, part * LANES : (part + 1) * LANES
        ].T
    entries = entries_ref[...]
    owner = lax.rem(lax.div(entries, owned), LANES)
    live = entries < owned * LANES
    rank = rank_ref[...]
    shape = (chunks, LANES)
    chosen = [jnp.zeros(shape, f32) for _ in range(FEATURES)]
    for slot in range(SLOTS):
        mask = rank == slot
        for at in range(FEATURES):
            row = at * SLOTS + slot
            source = jnp.broadcast_to(source_ref[row : row + 1, :], shape)
            found = jnp.take_along_axis(source, owner, axis=1, mode="promise_in_bounds")
            chosen[at] = jnp.where(mask, found, chosen[at])

    tile = first_tile + lax.div(iota(shape, 0), per_group) * GROUP + lax.rem(iota(shape, 1), GROUP)
    middle_x = (lax.rem(tile, TILE_COLS) * TILE_SIDE + TILE_SIDE // 2).astype(f32)
    middle_y = (lax.div(tile, TILE_COLS) * TILE_SIDE + TILE_SIDE // 2).astype(f32)
    at_u = chosen[0] - middle_x
    at_v = chosen[1] - middle_y
    conic_a, conic_b, conic_c = chosen[2], chosen[3], chosen[4]
    by_u = conic_a * at_u + conic_b * at_v
    by_v = conic_b * at_u + conic_c * at_v
    coefs = [
        jnp.where(live, chosen[5] - 0.5 * (at_u * by_u + at_v * by_v), -1e4),
        jnp.where(live, by_u, 0.0),
        jnp.where(live, by_v, 0.0),
        jnp.where(live, -0.5 * conic_a, 0.0),
        jnp.where(live, -conic_b, 0.0),
        jnp.where(live, -0.5 * conic_c, 0.0),
    ]
    for at in range(8):
        split = pieces(coefs[at], 3) if at < 6 else [jnp.zeros(shape, bf16)] * 3
        for part in range(3):
            row = (part * 8 + at) * chunks
            coef_ref[row : row + chunks, :] = split[part].astype(f32)
    for at in range(3):
        split = pieces(chosen[6 + at], 3)
        for part in range(3):
            row = (part * 3 + at) * chunks
            color_ref[row : row + chunks, :] = split[part].astype(f32)

    pixel = iota((8, pixels), 1)
    row8 = iota((8, pixels), 0)
    off_x = lax.rem(pixel, TILE_SIDE).astype(f32) - 7.5
    off_y = lax.div(pixel, TILE_SIDE).astype(f32) - 7.5
    base = jnp.where(row8 == 0, 1.0, 0.0)
    for at, values in enumerate([off_x, off_y, off_x * off_x, off_x * off_y, off_y * off_y]):
        base = jnp.where(row8 == at + 1, values, base)
    base_one = base.astype(bf16)
    base_three = jnp.concatenate([base, base, base], axis=0).astype(bf16)
    same_tile = lax.rem(iota((GROUP, LANES), 1), GROUP) == iota((GROUP, LANES), 0)

    def color_rows(chunk):
        rows = []
        for part in range(9):
            row = color_ref[pl.ds(part * chunks + chunk, 1), :]
            rows.append(jnp.where(same_tile, jnp.broadcast_to(row, (GROUP, LANES)), 0.0))
        return jnp.concatenate(rows, axis=0).astype(bf16)

    def forward(at, carry):
        out = []
        for group in range(groups):
            clear, render = carry[group]
            chunk = group * per_group + at
            coef = coef_ref[pl.ds(chunk, 24, stride=chunks), :].astype(bf16)
            alpha = jnp.exp(dot(coef, base_three, 0, 0))
            start = pl.multiple_of(chunk * LANES, LANES)
            alpha_ref[pl.ds(start, LANES), :] = alpha
            weights = []
            for step in range(steps):
                weight = alpha[step * GROUP : (step + 1) * GROUP, :] * clear
                clear = clear - weight
                weights.append(weight)
            weight = jnp.concatenate(weights, axis=0)
            weight_ref[pl.ds(start, LANES), :] = weight
            colors = color_rows(chunk)
            high, middle, low = pieces(weight, 3)
            render = render + (
                dot(colors, high, 1, 0)
                + jnp.concatenate(
                    [dot(colors[:48], middle, 1, 0), jnp.zeros((24, pixels), f32)], axis=0
                )
            )
            render = render + jnp.concatenate(
                [dot(colors[:24], low, 1, 0), jnp.zeros((48, pixels), f32)], axis=0
            )
            out.append((clear, render))
        return tuple(out)

    start_state = (jnp.ones((GROUP, pixels), f32), jnp.zeros((72, pixels), f32))
    done = lax.fori_loop(0, per_group, forward, (start_state,) * groups)

    signs = []
    for group in range(groups):
        render = done[group][1]
        render = render[:24] + (render[24:48] + render[48:])
        rows = []
        for at in range(3):
            gap = (
                render[at * GROUP : (at + 1) * GROUP, :]
                - target_ref[group * GROUP : (group + 1) * GROUP, at, :]
            )
            rows.append(jnp.where(gap > 0.0, 1.0, jnp.where(gap < 0.0, -1.0, 0.0)))
        signs.append(jnp.concatenate(rows, axis=0))

    def backward(back, carry):
        at = per_group - 1 - back
        out = []
        for group in range(groups):
            behind = carry[group]
            chunk = group * per_group + at
            start = pl.multiple_of(chunk * LANES, LANES)
            sign = signs[group].astype(bf16)
            sign_three = jnp.concatenate([signs[group]] * 3, axis=0).astype(bf16)
            pull = dot(color_rows(chunk), sign_three, 0, 0)
            alpha = alpha_ref[pl.ds(start, LANES), :]
            weight = weight_ref[pl.ds(start, LANES), :]
            by_alpha = [None] * steps
            for step in reversed(range(steps)):
                rows = slice(step * GROUP, (step + 1) * GROUP)
                gap = pull[rows, :] - behind
                by_alpha[step] = weight[rows, :] * gap
                behind = behind + alpha[rows, :] * gap
            high, low = pieces(jnp.concatenate(by_alpha, axis=0), 2)
            moments = dot(base_one, high, 1, 1) + dot(base_one, low, 1, 1)
            high, low = pieces(weight, 2)
            by_color = dot(sign, high, 1, 1) + dot(sign, low, 1, 1)
            row = pl.multiple_of(chunk * 16, 16)
            moment_ref[pl.ds(row, 8), :] = moments
            for channel in range(3):
                moment_ref[pl.ds(row + 8 + channel, 1), :] = jnp.sum(
                    jnp.where(same_tile, by_color[channel * GROUP : (channel + 1) * GROUP], 0.0),
                    axis=0,
                    keepdims=True,
                )
            out.append(behind)
        return tuple(out)

    lax.fori_loop(0, per_group, backward, (jnp.zeros((GROUP, pixels), f32),) * groups)

    sums = [moment_ref[pl.ds(at, chunks, stride=16), :] for at in range(6)]
    sum_x = sums[1] - at_u * sums[0]
    sum_y = sums[2] - at_v * sums[0]
    sum_xx = sums[3] - 2.0 * at_u * sums[1] + at_u * at_u * sums[0]
    sum_xy = sums[4] - at_u * sums[2] - at_v * sum_x
    sum_yy = sums[5] - 2.0 * at_v * sums[2] + at_v * at_v * sums[0]
    grads = [
        conic_a * sum_x + conic_b * sum_y,
        conic_b * sum_x + conic_c * sum_y,
        -0.5 * sum_xx,
        -sum_xy,
        -0.5 * sum_yy,
        sums[0],
    ] + [moment_ref[pl.ds(8 + at, chunks, stride=16), :] for at in range(3)]
    for at in range(FEATURES):
        grad_ref[at * chunks : (at + 1) * chunks, :] = jnp.where(live, grads[at], 0.0)

    owner_id = iota((LANES, LANES), 0)
    slot_id = iota((SLOTS, LANES), 0)

    def scatter(chunk, total):
        own = lax.rem(lax.div(entries_ref[pl.ds(chunk, 1), :], owned), LANES)
        hot = jnp.where(owner_id == own, 1.0, 0.0).astype(bf16)
        slot = slot_id == rank_ref[pl.ds(chunk, 1), :]
        rows = []
        for at in range(FEATURES):
            row = grad_ref[pl.ds(at * chunks + chunk, 1), :]
            rows.append(jnp.where(slot, jnp.broadcast_to(row, (SLOTS, LANES)), 0.0))
        high, low = pieces(jnp.concatenate(rows, axis=0), 2)
        return total + (dot(hot, high, 1, 1) + dot(hot, low, 1, 1))

    total = lax.fori_loop(0, chunks, scatter, jnp.zeros((LANES, FEATURES * SLOTS), f32))
    grads_ref[...] = jnp.concatenate(
        [total, jnp.zeros((LANES, 3 * LANES - FEATURES * SLOTS), f32)], axis=1
    )


def update_kernel(
    frame,
    params_ref,
    first_ref,
    second_ref,
    cameras_ref,
    asked_ref,
    grads_ref,
    rates_ref,
    new_params_ref,
    new_first_ref,
    new_second_ref,
    source_ref,
    dense_ref,
    gradient_ref,
):
    owned = params_ref.shape[1]
    asked = flipped_requests(asked_ref)
    for part in range(3):
        source_ref[part * LANES : (part + 1) * LANES, :] = grads_ref[
            :, part * LANES : (part + 1) * LANES
        ].T
    source_ref[3 * LANES :, :] = jnp.zeros((LANES, LANES), f32)
    view_of = lax.div(iota((16, LANES), 1), LANES // VIEWS)
    column_id = iota((owned, LANES), 0)
    dense = jnp.zeros((2 * VIEWS * 16, owned), f32)
    for slot in range(SLOTS):
        hot = jnp.where(column_id == asked[slot : slot + 1, :], 1.0, 0.0).astype(bf16)
        values = source_ref[pl.ds(slot, 16, stride=SLOTS), :]
        values = jnp.concatenate(
            [jnp.where(view_of == view, values, 0.0) for view in range(VIEWS)], axis=0
        )
        high, low = pieces(values, 2)
        dense = dense + dot(jnp.concatenate([high, low], axis=0), hot, 1, 1)
    dense = dense[: VIEWS * 16] + dense[VIEWS * 16 :]
    spans = range(owned // LANES)
    for span in spans:
        dense_ref[span * VIEWS * 16 : (span + 1) * VIEWS * 16, :] = dense[
            :, span * LANES : (span + 1) * LANES
        ]
    cotangents = [
        jnp.concatenate(
            [dense_ref[pl.ds(span * VIEWS * 16 + at, VIEWS, stride=16), :] for span in spans], axis=1
        )
        for at in range(FEATURES)
    ]

    rotation, shift = camera_terms(cameras_ref, owned)
    params = [jnp.broadcast_to(params_ref[at : at + 1, :], (VIEWS, owned)) for at in range(59)]
    _, pullback = jax.vjp(lambda values: project(values, rotation, shift, *frame), params)
    by_params = pullback(cotangents)[0]
    for at in range(59):
        gradient_ref[at : at + 1, :] = jnp.sum(by_params[at], axis=0, keepdims=True)
    gradient = gradient_ref[:59, :]
    new_first = beta_one * first_ref[...] + (1.0 - beta_one) * gradient
    new_second = beta_two * second_ref[...] + (1.0 - beta_two) * gradient * gradient
    new_first_ref[...] = new_first
    new_second_ref[...] = new_second
    step_size = rates_ref[...] * (new_first / (1.0 - beta_one**ADAM_STEP))
    new_params_ref[...] = params_ref[...] - step_size / (
        jnp.sqrt(new_second / (1.0 - beta_two**ADAM_STEP)) + adam_eps
    )


learning = np.concatenate(
    [
        np.full(3, 0.00016),
        np.full(3, 0.005),
        np.full(4, 0.001),
        np.full(1, 0.05),
        np.full(3, 0.0025),
        np.full(45, 0.000125),
    ]
).astype(np.float32)[:, None]


def per_device(params, first_moment, second_moment, cameras, target, lists, lengths):
    owned = params.shape[1]
    list_size = lists.shape[2]
    tile_dev = lists.shape[1]
    entry_count = tile_dev * list_size
    chunks = entry_count // LANES
    width = TILE_COLS * TILE_SIDE
    height = tile_dev * lax.axis_size("tiles") // TILE_COLS * TILE_SIDE
    frame = (float(width), 0.5 * width, 0.5 * height)
    limits = pltpu.CompilerParams(vmem_limit_bytes=48 * 1024 * 1024)

    dead = jnp.arange(list_size, dtype=i32)[None, :] >= lengths[0][:, None]
    entries = lists[0] + jnp.where(dead, owned * LANES, 0)
    entries = (
        entries.reshape(tile_dev // GROUP, GROUP, list_size).transpose(0, 2, 1).reshape(chunks, LANES)
    )

    def full(shape, dtype=f32):
        return jax.ShapeDtypeStruct(shape, dtype)

    rank, requests = pl.pallas_call(
        lambda *refs: rank_kernel(owned, *refs),
        out_shape=(full((chunks, LANES), i32), full((LANES, SLOTS))),
        compiler_params=limits,
        name="rank",
    )(entries)
    asked = lax.all_to_all(requests, AXES, 0, 0, tiled=True)
    answers = pl.pallas_call(
        lambda *refs: answer_kernel(frame, *refs),
        out_shape=full((LANES, 3 * LANES)),
        compiler_params=limits,
        name="answer",
    )(params, cameras, asked)
    rows = lax.all_to_all(answers, AXES, 0, 0, tiled=True)
    row_grads = pl.pallas_call(
        lambda *refs: tile_kernel(owned, *refs),
        out_shape=full((LANES, 3 * LANES)),
        scratch_shapes=[
            pltpu.VMEM((3 * LANES, LANES), f32),
            pltpu.VMEM((24 * chunks, LANES), f32),
            pltpu.VMEM((9 * chunks, LANES), f32),
            pltpu.VMEM((entry_count, TILE_SIDE * TILE_SIDE), f32),
            pltpu.VMEM((entry_count, TILE_SIDE * TILE_SIDE), f32),
            pltpu.VMEM((16 * chunks, LANES), f32),
            pltpu.VMEM((FEATURES * chunks, LANES), f32),
        ],
        compiler_params=limits,
        name="tiles",
    )(entries, rank, rows, target[0])
    shares = lax.all_to_all(row_grads, AXES, 0, 0, tiled=True)
    return pl.pallas_call(
        lambda *refs: update_kernel(frame, *refs),
        out_shape=(full(params.shape),) * 3,
        scratch_shapes=[
            pltpu.VMEM((4 * LANES, LANES), f32),
            pltpu.VMEM((VIEWS * 16 * (owned // LANES), LANES), f32),
            pltpu.VMEM((64, owned), f32),
        ],
        compiler_params=limits,
        name="update",
    )(params, first_moment, second_moment, cameras, asked, shares, jnp.asarray(learning))


def solution(mesh):
    placed = (
        P(None, AXES),
        P(None, AXES),
        P(None, AXES),
        P(),
        P("views", "tiles", None, None),
        P("views", "tiles", None),
        P("views", "tiles"),
    )
    return jax.shard_map(
        per_device,
        mesh=mesh,
        in_specs=placed,
        out_specs=(P(None, AXES),) * 3,
        check_vma=False,
    )
```

time: 636 us -> 92.7 us (0.15)
  other arithmetic: 234 us -> 0.7 us
  waiting for transfers between devices: 243 us -> 10.3 us
  local copies, waits for them, and re-layouts: 97.6 us -> 3.83 us
  between operations: 55.4 us -> 0.73 us
  Pallas kernels: 0 us -> 36.7 us
  blocking collectives: 0 us -> 35.5 us
    unnamed x3 -> x0, waiting for transfers between devices: 163 us -> none
    all_gather x1 -> x0, waiting for transfers between devices: 79.9 us -> none  [per_device(): lax.all_gather(projected, ('views', 'tiles'), axis=2, tiled=True)]
    another operation x25 -> x0, other arithmetic: 64.5 us -> none
    reduce_sum x14 -> x0, other arithmetic: 37.4 us -> none  [the longest x4 15.1 us: composite(): weight * picked[6 + channel][:, :, None]]
    pallas_call x0 -> x4, Pallas kernels: none -> 36.7 us  [the longest x1 29.6 us: per_device(): pl.pallas_call(lambda *refs: tile_kernel(owned, *refs), out_shape=full((L...]
    scatter-add x1 -> x0, other arithmetic: 35.6 us -> none  [spread_rows(): dense_rows.at[:, jnp.clip(positions, 0, width_here - 1)]]
    all_to_all x0 -> x2, blocking collectives: none -> 35.5 us  [the longest x1 20.8 us: per_device(): asked = lax.all_to_all(requests, AXES, 0, 0, tiled=True)]
    dynamic_slice x6 -> x0, local copies, waits for them, and re-layouts: 26.4 us -> none  [the longest x2 21.4 us: per_device(): lax.dynamic_index_in_dim(lax.all_gather(projected, ('views', 'tiles'), ax...]
  transfers between devices with their start and end apart: 2 -> 1, of which waited for: 2 -> 1; matrix products, arithmetic and copies ran while one was open for 1% -> 0% of each run, Pallas kernels for 0% -> 0%
where the time goes in v1:
time: 92.7 us; the launch traced here: 92.4 us
  Pallas kernels  36.7 us (40%)
  blocking collectives  35.5 us (38%)
  waiting for transfers between devices  10.3 us (11%)
  starting transfers between devices  4.62 us (5%)
  local copies, waits for them, and re-layouts  3.83 us (4%)
    pallas_call x1, Pallas kernels, per_device(): pl.pallas_call(lambda *refs: tile_kernel(owned, *refs), out_shape=full((L...  29.6 us
    all_to_all x1, blocking collectives, per_device(): asked = lax.all_to_all(requests, AXES, 0, 0, tiled=True)  20.8 us
    all_to_all x1, blocking collectives, per_device(): shares = lax.all_to_all(row_grads, AXES, 0, 0, tiled=True)  14.7 us
    all_to_all x1, waiting for transfers between devices, per_device(): rows = lax.all_to_all(answers, AXES, 0, 0, tiled=True)  10.3 us
    all_to_all x1, starting transfers between devices, per_device(): rows = lax.all_to_all(answers, AXES, 0, 0, tiled=True)  4.62 us
    pallas_call x1, Pallas kernels, per_device(): pl.pallas_call(lambda *refs: update_kernel(frame, *refs), out_shape=(full...  2.97 us
    pallas_call x1, Pallas kernels, per_device(): pl.pallas_call(lambda *refs: rank_kernel(owned, *refs), out_shape=(full((...  2.29 us
  transfers between devices with their start and end apart: 1, of which 1 were waited for; matrix products, arithmetic and copies ran while one was open for 0% of the time, Pallas kernels for 0%

profile of v1, /device:TPU:1, one launch (start us, length us, event | category | flops | bytes accessed | tf_op | source)
XLA Modules:
  0.0 92.4 jit_solution(2823949107828640352)
XLA Ops:
  0.6 0.0 copy-start.6
  0.6 0.5 broadcast.10
  1.2 0.1 copy-done.6
  1.3 0.7 reduce.3
  1.9 0.1 ge.17
  2.0 0.8 copy.15
  2.9 0.1 reshape.26.refs_0_
  3.1 0.0 copy-start
  3.1 2.3 %rank.1 = (s32[32,128]{1,0:T(8,128)S(1)}, f32[128,32]{1,0:T(8,128)S(1)}) custom-call(s32[32,128]{1,0:T(8,128)S(1)} %reshape.26.refs_0_), custom_call_target="tpu_custom_call" | custom-call | tf_op jit(solution)/shard_map/rank/pallas_call | solution.py:570
  5.4 0.0 copy-start.4
  5.4 20.8 %all_to_all.33 = f32[128,1,32]{2,1,0:T(1,128)S(1)} all-to-all(f32[128,1,32]{2,1,0:T(1,128)S(1)} %bitcast.25), channel_id=1, replica_groups=mesh['views'=4,'tiles'=32] {'views','tiles'}, dimensions={0} | all-to-all | bytes 32768 | tf_op jit(solution)/shard_map/all_to_all | solution.py:576
  26.2 0.0 copy-done
  26.2 0.0 copy-done.4
  26.2 1.8 %answer.1 = f32[128,384]{1,0:T(8,128)S(1)} custom-call(f32[59,512]{1,0:T(8,128)S(1)} %copy-done, f32[4,6]{1,0:T(4,128)S(1)} %copy-done.4, f32[128,32]{1,0:T(8,128)S(1)} %bitcast.22), custom_call_target="tpu_custom_call" | custom-call | tf_op jit(solution)/shard_map/answer/pallas_call | solution.py:577
  28.0 0.9 copy.17
  28.9 4.6 %all-to-all-start.1 = ((f32[128,1,384]{2,1,0:T(1,128)}), f32[128,1,384]{2,1,0:T(1,128)S(1)}, u32[]{:S(2)}, u32[]{:S(2)}) async-start(f32[128,1,384]{2,1,0:T(1,128)} %copy.17), calls=%async_computation.1 | async-start | bytes 393216 | tf_op jit(solution)/shard_map/all_to_all | solution.py:583
  33.5 0.0 copy-done.5
  33.6 10.3 %all-to-all-done.1 = f32[128,1,384]{2,1,0:T(1,128)S(1)} async-done(((f32[128,1,384]{2,1,0:T(1,128)}), f32[128,1,384]{2,1,0:T(1,128)S(1)}, u32[]{:S(2)}, u32[]{:S(2)}) %all-to-all-start.1) | async-done | bytes 196640 | tf_op jit(solution)/shard_map/all_to_all | solution.py:583
  43.9 29.6 %tiles.1 = f32[128,384]{1,0:T(8,128)S(1)} custom-call(s32[32,128]{1,0:T(8,128)S(1)} %reshape.26.refs_0_, s32[32,128]{1,0:T(8,128)S(1)} %get-tuple-element.6.refs_1_, f32[128,384]{1,0:T(8,128)S(1)} %bitcast.20, f32[16,3,256]{2,1,0:T(4,128)S(1)} %bitcast.24), custom_call_target="tpu_custom_call" | custom-call | tf_op jit(solution)/shard_map/tiles/pallas_call | solution.py:584
  73.6 0.2 copy.19
  73.8 14.7 %all_to_all.34 = f32[128,1,384]{2,1,0:T(1,128)S(1)} all-to-all(f32[128,1,384]{2,1,0:T(1,128)S(1)} %copy.19), channel_id=1, replica_groups=mesh['views'=4,'tiles'=32] {'views','tiles'}, dimensions={0} | all-to-all | bytes 393216 | tf_op jit(solution)/shard_map/all_to_all | solution.py:599
  88.5 0.9 copy-done.1
  89.4 0.1 copy-done.2
  89.4 3.0 %update.1 = (f32[59,512]{1,0:T(8,128)}, f32[59,512]{1,0:T(8,128)}, f32[59,512]{1,0:T(8,128)}) custom-call(f32[59,512]{1,0:T(8,128)S(1)} %copy-done, f32[59,512]{1,0:T(8,128)S(1)} %copy-done.1, f32[59,512]{1,0:T(8,128)S(1)} %copy-done.2, f32[4,6]{1,0:T(4,128)S(1)} %copy-done.4, f32[128,32]{1,0:T(8,128)S(1)} %bitcast.23, f32[128,384]{1,0:T(8,128)S(1)} %bitcast.19, ...), custom_call_target="tpu_custom_call" | custom-call | tf_op jit(solution)/shard_map/update/pallas_call | solution.py:600
  (9 shorter events, 0.1 us)
Async XLA Ops:
  0.6 0.7 copy-start.6
  3.1 23.1 %copy-start = (f32[59,512]{1,0:T(8,128)S(1)}, f32[59,512]{1,0:T(8,128)}, u32[]{:S(2)}) copy-start(f32[59,512]{1,0:T(8,128)} %refs_0_.3) | copy-start | bytes 362500
  5.4 20.8 %copy-start.4 = (f32[4,6]{1,0:T(4,128)S(1)}, f32[4,6]{1,0:T(4,128)}, u32[]{:S(2)}) copy-start(f32[4,6]{1,0:T(4,128)} %refs_3_.1) | copy-start | bytes 292
  28.9 4.6 %copy-start.5 = (f32[1,16,3,256]{3,1,2,0:T(8,128)S(1)}, f32[1,16,3,256]{3,1,2,0:T(8,128)}, u32[]{:S(2)}) copy-start(f32[1,16,3,256]{3,1,2,0:T(8,128)} %param.12) | copy-start | bytes 147460
  28.9 15.0 %all-to-all-start.1 = ((f32[128,1,384]{2,1,0:T(1,128)}), f32[128,1,384]{2,1,0:T(1,128)S(1)}, u32[]{:S(2)}, u32[]{:S(2)}) async-start(f32[128,1,384]{2,1,0:T(1,128)} %copy.17), calls=%async_computation.1 | async-start | bytes 393216 | tf_op jit(solution)/shard_map/all_to_all | solution.py:583
  88.5 0.9 copy-start.1
  88.5 1.0 %copy-start.2 = (f32[59,512]{1,0:T(8,128)S(1)}, f32[59,512]{1,0:T(8,128)}, u32[]{:S(2)}) copy-start(f32[59,512]{1,0:T(8,128)} %refs_2_.1) | copy-start | bytes 362500
  88.5 1.0 %copy-start.3 = (f32[59,1]{1,0:T(8,128)S(1)}, f32[59,1]{1,0:T(8,128)}, u32[]{:S(2)}) copy-start(f32[59,1]{1,0:T(8,128)} %constant.6.clone.refs_6_) | copy-start | bytes 712

commit v2 on v1

--- a/solution.py
+++ b/solution.py
@@ -13,6 +13,7 @@
 LANES = 128
 VIEWS = 4
 SLOTS = 32
+HALF = SLOTS // 2
 FEATURES = 9
 AXES = ("views", "tiles")
 
@@ -41,6 +42,7 @@
 beta_one = 0.9
 beta_two = 0.999
 adam_eps = 1e-15
+log2_e = 1.4426950408889634
 
 
 def matmul_three(left, right):
@@ -261,11 +263,20 @@
                 )
                 found = jnp.take_along_axis(source, lane_of, axis=1, mode="promise_in_bounds")
                 chosen[at] = jnp.where(mask, found, chosen[at])
+    stack = [
+        chosen[at][half * HALF : (half + 1) * HALF] for half in range(2) for at in range(FEATURES)
+    ]
+    stack.append(jnp.zeros((3 * LANES - SLOTS * FEATURES, LANES), f32))
+    stack = jnp.concatenate(stack, axis=0)
     for part in range(3):
-        stack = chosen[4 * part : 4 * part + 4]
-        while len(stack) < 4:
-            stack.append(jnp.zeros((SLOTS, LANES), f32))
-        rows_ref[:, part * LANES : (part + 1) * LANES] = jnp.concatenate(stack, axis=0).T
+        rows_ref[:, part * LANES : (part + 1) * LANES] = stack[
+            part * LANES : (part + 1) * LANES
+        ].T
+
+
+def slot_columns(entries, rank, owned):
+    owner = lax.rem(lax.div(entries, owned), LANES)
+    return lax.div(rank, HALF) * LANES + owner, lax.rem(rank, HALF)
 
 
 def tile_kernel(
@@ -275,38 +286,60 @@
     rows_ref,
     target_ref,
     grads_ref,
-    source_ref,
+    hot_ref,
+    picked_ref,
     coef_ref,
     color_ref,
     alpha_ref,
     weight_ref,
+    high_ref,
+    middle_ref,
+    low_ref,
+    pull_ref,
     moment_ref,
     grad_ref,
+    spread_ref,
 ):
     chunks = entries_ref.shape[0]
     groups = 2
     per_group = chunks // groups
     pixels = TILE_SIDE * TILE_SIDE
     steps = LANES // GROUP
+    span = FEATURES * HALF
     first_tile = lax.axis_index("tiles") * (groups * GROUP)
 
-    for part in range(3):
-        source_ref[part * LANES : (part + 1) * LANES, :] = rows_ref[
-            :, part * LANES : (part + 1) * LANES
-        ].T
     entries = entries_ref[...]
-    owner = lax.rem(lax.div(entries, owned), LANES)
     live = entries < owned * LANES
-    rank = rank_ref[...]
+    place, below = slot_columns(entries, rank_ref[...], owned)
+    place = place.astype(f32)
+    place_id = iota((2 * LANES, LANES), 0).astype(f32).astype(bf16)
+    for at in range(chunks):
+        row = jnp.broadcast_to(place[at : at + 1, :], (2 * LANES, LANES)).astype(bf16)
+        hot_ref[:, at * LANES : (at + 1) * LANES] = jnp.where(
+            place_id == row, jnp.ones((), bf16), jnp.zeros((), bf16)
+        )
+
+    flipped = jnp.concatenate(
+        [rows_ref[:, part * LANES : (part + 1) * LANES].T for part in range(3)], axis=0
+    )
+    table = jnp.concatenate([flipped[:span], flipped[span : 2 * span]], axis=1)
+    table = jnp.concatenate(pieces(table, 3), axis=0)
+    half_id = iota((HALF, LANES), 0)
+    for at in range(0, chunks, 2):
+        found = dot(table, hot_ref[:, at * LANES : (at + 2) * LANES], 1, 0)
+        found = found[:span] + (found[span : 2 * span] + found[2 * span :])
+        for side in range(2):
+            mask = half_id == below[at + side : at + side + 1, :]
+            for feature in range(FEATURES):
+                values = found[
+                    feature * HALF : (feature + 1) * HALF, side * LANES : (side + 1) * LANES
+                ]
+                row = feature * chunks + at + side
+                picked_ref[row : row + 1, :] = jnp.sum(
+                    jnp.where(mask, values, 0.0), axis=0, keepdims=True
+                )
     shape = (chunks, LANES)
-    chosen = [jnp.zeros(shape, f32) for _ in range(FEATURES)]
-    for slot in range(SLOTS):
-        mask = rank == slot
-        for at in range(FEATURES):
-            row = at * SLOTS + slot
-            source = jnp.broadcast_to(source_ref[row : row + 1, :], shape)
-            found = jnp.take_along_axis(source, owner, axis=1, mode="promise_in_bounds")
-            chosen[at] = jnp.where(mask, found, chosen[at])
+    chosen = [picked_ref[at * chunks : (at + 1) * chunks, :] for at in range(FEATURES)]
 
     tile = first_tile + lax.div(iota(shape, 0), per_group) * GROUP + lax.rem(iota(shape, 1), GROUP)
     middle_x = (lax.rem(tile, TILE_COLS) * TILE_SIDE + TILE_SIDE // 2).astype(f32)
@@ -317,12 +350,12 @@
     by_u = conic_a * at_u + conic_b * at_v
     by_v = conic_b * at_u + conic_c * at_v
     coefs = [
-        jnp.where(live, chosen[5] - 0.5 * (at_u * by_u + at_v * by_v), -1e4),
-        jnp.where(live, by_u, 0.0),
-        jnp.where(live, by_v, 0.0),
-        jnp.where(live, -0.5 * conic_a, 0.0),
-        jnp.where(live, -conic_b, 0.0),
-        jnp.where(live, -0.5 * conic_c, 0.0),
+        jnp.where(live, log2_e * (chosen[5] - 0.5 * (at_u * by_u + at_v * by_v)), -1e4),
+        jnp.where(live, log2_e * by_u, 0.0),
+        jnp.where(live, log2_e * by_v, 0.0),
+        jnp.where(live, (-0.5 * log2_e) * conic_a, 0.0),
+        jnp.where(live, -log2_e * conic_b, 0.0),
+        jnp.where(live, (-0.5 * log2_e) * conic_c, 0.0),
     ]
     for at in range(8):
         split = pieces(coefs[at], 3) if at < 6 else [jnp.zeros(shape, bf16)] * 3
@@ -342,9 +375,12 @@
     base = jnp.where(row8 == 0, 1.0, 0.0)
     for at, values in enumerate([off_x, off_y, off_x * off_x, off_x * off_y, off_y * off_y]):
         base = jnp.where(row8 == at + 1, values, base)
-    base_one = base.astype(bf16)
+    base_two = jnp.concatenate([base, base], axis=1).astype(bf16)
     base_three = jnp.concatenate([base, base, base], axis=0).astype(bf16)
     same_tile = lax.rem(iota((GROUP, LANES), 1), GROUP) == iota((GROUP, LANES), 0)
+
+    def rows_of(chunk):
+        return pl.ds(pl.multiple_of(chunk * LANES, LANES), LANES)
 
     def color_rows(chunk):
         rows = []
@@ -353,42 +389,63 @@
             rows.append(jnp.where(same_tile, jnp.broadcast_to(row, (GROUP, LANES)), 0.0))
         return jnp.concatenate(rows, axis=0).astype(bf16)
 
-    def forward(at, carry):
+    def shade(at):
+        for group in range(groups):
+            chunk = group * per_group + at
+            coef = coef_ref[pl.ds(chunk, 24, stride=chunks), :].astype(bf16)
+            alpha_ref[rows_of(chunk), :] = jnp.exp2(dot(coef, base_three, 0, 0))
+
+    def weigh(at, clears):
         out = []
         for group in range(groups):
-            clear, render = carry[group]
-            chunk = group * per_group + at
-            coef = coef_ref[pl.ds(chunk, 24, stride=chunks), :].astype(bf16)
-            alpha = jnp.exp(dot(coef, base_three, 0, 0))
-            start = pl.multiple_of(chunk * LANES, LANES)
-            alpha_ref[pl.ds(start, LANES), :] = alpha
+            clear = clears[group]
+            rows = rows_of(group * per_group + at)
+            alpha = alpha_ref[rows, :]
             weights = []
             for step in range(steps):
                 weight = alpha[step * GROUP : (step + 1) * GROUP, :] * clear
                 clear = clear - weight
                 weights.append(weight)
             weight = jnp.concatenate(weights, axis=0)
-            weight_ref[pl.ds(start, LANES), :] = weight
+            weight_ref[rows, :] = weight
+            high_ref[rows, :], middle_ref[rows, :], low_ref[rows, :] = pieces(weight, 3)
+            out.append(clear)
+        return tuple(out)
+
+    def blend(at, renders):
+        out = []
+        for group in range(groups):
+            chunk = group * per_group + at
+            rows = rows_of(chunk)
             colors = color_rows(chunk)
-            high, middle, low = pieces(weight, 3)
-            render = render + (
-                dot(colors, high, 1, 0)
-                + jnp.concatenate(
-                    [dot(colors[:48], middle, 1, 0), jnp.zeros((24, pixels), f32)], axis=0
-                )
+            colors = jnp.concatenate([colors, colors, colors], axis=1)
+            parts = jnp.concatenate(
+                [high_ref[rows, :], middle_ref[rows, :], low_ref[rows, :]], axis=0
             )
-            render = render + jnp.concatenate(
-                [dot(colors[:24], low, 1, 0), jnp.zeros((48, pixels), f32)], axis=0
-            )
-            out.append((clear, render))
+            out.append(renders[group] + dot(colors, parts, 1, 0))
         return tuple(out)
 
-    start_state = (jnp.ones((GROUP, pixels), f32), jnp.zeros((72, pixels), f32))
-    done = lax.fori_loop(0, per_group, forward, (start_state,) * groups)
-
-    signs = []
+    clears = (jnp.ones((GROUP, pixels), f32),) * groups
+    renders = (jnp.zeros((72, pixels), f32),) * groups
+    shade(0)
+    shade(1)
+    clears = weigh(0, clears)
+
+    def forward(at, carry):
+        clears, renders = carry
+        shade(at + 1)
+        renders = blend(at - 1, renders)
+        clears = weigh(at, clears)
+        return clears, renders
+
+    clears, renders = lax.fori_loop(1, per_group - 1, forward, (clears, renders))
+    renders = blend(per_group - 2, renders)
+    clears = weigh(per_group - 1, clears)
+    renders = blend(per_group - 1, renders)
+
+    signs, sign_twos, sign_threes = [], [], []
     for group in range(groups):
-        render = done[group][1]
+        render = renders[group]
         render = render[:24] + (render[24:48] + render[48:])
         rows = []
         for at in range(3):
@@ -397,42 +454,62 @@
                 - target_ref[group * GROUP : (group + 1) * GROUP, at, :]
             )
             rows.append(jnp.where(gap > 0.0, 1.0, jnp.where(gap < 0.0, -1.0, 0.0)))
-        signs.append(jnp.concatenate(rows, axis=0))
-
-    def backward(back, carry):
-        at = per_group - 1 - back
+        sign = jnp.concatenate(rows, axis=0)
+        sign_twos.append(jnp.concatenate([sign, sign], axis=1).astype(bf16))
+        sign_threes.append(jnp.concatenate([sign, sign, sign], axis=0).astype(bf16))
+
+    def draw(at):
+        for group in range(groups):
+            chunk = group * per_group + at
+            pull_ref[rows_of(chunk), :] = dot(color_rows(chunk), sign_threes[group], 0, 0)
+
+    def unweigh(at, behinds):
         out = []
         for group in range(groups):
-            behind = carry[group]
-            chunk = group * per_group + at
-            start = pl.multiple_of(chunk * LANES, LANES)
-            sign = signs[group].astype(bf16)
-            sign_three = jnp.concatenate([signs[group]] * 3, axis=0).astype(bf16)
-            pull = dot(color_rows(chunk), sign_three, 0, 0)
-            alpha = alpha_ref[pl.ds(start, LANES), :]
-            weight = weight_ref[pl.ds(start, LANES), :]
+            behind = behinds[group]
+            rows = rows_of(group * per_group + at)
+            pull, alpha, weight = pull_ref[rows, :], alpha_ref[rows, :], weight_ref[rows, :]
             by_alpha = [None] * steps
             for step in reversed(range(steps)):
-                rows = slice(step * GROUP, (step + 1) * GROUP)
-                gap = pull[rows, :] - behind
-                by_alpha[step] = weight[rows, :] * gap
-                behind = behind + alpha[rows, :] * gap
-            high, low = pieces(jnp.concatenate(by_alpha, axis=0), 2)
-            moments = dot(base_one, high, 1, 1) + dot(base_one, low, 1, 1)
-            high, low = pieces(weight, 2)
-            by_color = dot(sign, high, 1, 1) + dot(sign, low, 1, 1)
+                part = slice(step * GROUP, (step + 1) * GROUP)
+                gap = pull[part, :] - behind
+                by_alpha[step] = weight[part, :] * gap
+                behind = behind + alpha[part, :] * gap
+            low_ref[rows, :], spread_ref[rows, :] = pieces(jnp.concatenate(by_alpha, axis=0), 2)
+            out.append(behind)
+        return tuple(out)
+
+    def total(at):
+        for group in range(groups):
+            chunk = group * per_group + at
+            rows = rows_of(chunk)
             row = pl.multiple_of(chunk * 16, 16)
-            moment_ref[pl.ds(row, 8), :] = moments
+            parts = jnp.concatenate([low_ref[rows, :], spread_ref[rows, :]], axis=1)
+            moment_ref[pl.ds(row, 8), :] = dot(base_two, parts, 1, 1)
+            parts = jnp.concatenate([high_ref[rows, :], middle_ref[rows, :]], axis=1)
+            by_color = dot(sign_twos[group], parts, 1, 1)
             for channel in range(3):
                 moment_ref[pl.ds(row + 8 + channel, 1), :] = jnp.sum(
                     jnp.where(same_tile, by_color[channel * GROUP : (channel + 1) * GROUP], 0.0),
                     axis=0,
                     keepdims=True,
                 )
-            out.append(behind)
-        return tuple(out)
-
-    lax.fori_loop(0, per_group, backward, (jnp.zeros((GROUP, pixels), f32),) * groups)
+
+    behinds = (jnp.zeros((GROUP, pixels), f32),) * groups
+    draw(per_group - 1)
+    draw(per_group - 2)
+    behinds = unweigh(per_group - 1, behinds)
+
+    def backward(back, behinds):
+        at = per_group - 1 - back
+        draw(at - 1)
+        total(at + 1)
+        return unweigh(at, behinds)
+
+    behinds = lax.fori_loop(1, per_group - 1, backward, behinds)
+    total(1)
+    behinds = unweigh(0, behinds)
+    total(0)
 
     sums = [moment_ref[pl.ds(at, chunks, stride=16), :] for at in range(6)]
     sum_x = sums[1] - at_u * sums[0]
@@ -448,27 +525,64 @@
         -0.5 * sum_yy,
         sums[0],
     ] + [moment_ref[pl.ds(8 + at, chunks, stride=16), :] for at in range(3)]
-    for at in range(FEATURES):
-        grad_ref[at * chunks : (at + 1) * chunks, :] = jnp.where(live, grads[at], 0.0)
-
-    owner_id = iota((LANES, LANES), 0)
-    slot_id = iota((SLOTS, LANES), 0)
-
-    def scatter(chunk, total):
-        own = lax.rem(lax.div(entries_ref[pl.ds(chunk, 1), :], owned), LANES)
-        hot = jnp.where(owner_id == own, 1.0, 0.0).astype(bf16)
-        slot = slot_id == rank_ref[pl.ds(chunk, 1), :]
-        rows = []
-        for at in range(FEATURES):
-            row = grad_ref[pl.ds(at * chunks + chunk, 1), :]
-            rows.append(jnp.where(slot, jnp.broadcast_to(row, (SLOTS, LANES)), 0.0))
-        high, low = pieces(jnp.concatenate(rows, axis=0), 2)
-        return total + (dot(hot, high, 1, 1) + dot(hot, low, 1, 1))
-
-    total = lax.fori_loop(0, chunks, scatter, jnp.zeros((LANES, FEATURES * SLOTS), f32))
-    grads_ref[...] = jnp.concatenate(
-        [total, jnp.zeros((LANES, 3 * LANES - FEATURES * SLOTS), f32)], axis=1
-    )
+
+    half_one = half_id.astype(f32).astype(bf16)
+    below = below.astype(f32)
+    grads = [pieces(jnp.where(live, grad, 0.0), 2) for grad in grads]
+    grads = [[part.astype(f32) for part in split] for split in grads]
+    for at in range(chunks):
+        mask = half_one == jnp.broadcast_to(below[at : at + 1, :], (HALF, LANES)).astype(bf16)
+        for part in range(2):
+            for feature in range(FEATURES):
+                row = grads[feature][part][at : at + 1, :]
+                grad_ref[
+                    part * span + feature * HALF : part * span + (feature + 1) * HALF,
+                    at * LANES : (at + 1) * LANES,
+                ] = jnp.where(
+                    mask,
+                    jnp.broadcast_to(row, (HALF, LANES)).astype(bf16),
+                    jnp.zeros((), bf16),
+                )
+    sent = dot(grad_ref[...], hot_ref[...], 1, 1)
+    sent = sent[:span] + sent[span:]
+    sent = jnp.concatenate(
+        [sent[:, :LANES], sent[:, LANES:], jnp.zeros((3 * LANES - 2 * span, LANES), f32)], axis=0
+    )
+    for part in range(3):
+        grads_ref[:, part * LANES : (part + 1) * LANES] = sent[
+            part * LANES : (part + 1) * LANES, :
+        ].T
+
+
+def tiles_call(entries, rank, rows, target, owned):
+    chunks = entries.shape[0]
+    pixels = TILE_SIDE * TILE_SIDE
+    count = chunks * LANES
+
+    def plane(dtype):
+        return pltpu.VMEM((count, pixels), dtype)
+
+    return pl.pallas_call(
+        lambda *refs: tile_kernel(owned, *refs),
+        out_shape=jax.ShapeDtypeStruct((LANES, 3 * LANES), f32),
+        scratch_shapes=[
+            pltpu.VMEM((2 * LANES, count), bf16),
+            pltpu.VMEM((FEATURES * chunks, LANES), f32),
+            pltpu.VMEM((24 * chunks, LANES), f32),
+            pltpu.VMEM((9 * chunks, LANES), f32),
+            plane(f32),
+            plane(f32),
+            plane(bf16),
+            plane(bf16),
+            plane(bf16),
+            plane(f32),
+            pltpu.VMEM((16 * chunks, LANES), f32),
+            pltpu.VMEM((2 * FEATURES * HALF, count), bf16),
+            plane(bf16),
+        ],
+        compiler_params=pltpu.CompilerParams(vmem_limit_bytes=48 * 1024 * 1024),
+        name="tiles",
+    )(entries, rank, rows, target)
 
 
 def update_kernel(
@@ -499,7 +613,8 @@
     dense = jnp.zeros((2 * VIEWS * 16, owned), f32)
     for slot in range(SLOTS):
         hot = jnp.where(column_id == asked[slot : slot + 1, :], 1.0, 0.0).astype(bf16)
-        values = source_ref[pl.ds(slot, 16, stride=SLOTS), :]
+        first = slot // HALF * FEATURES * HALF + slot % HALF
+        values = source_ref[pl.ds(first, 16, stride=HALF), :]
         values = jnp.concatenate(
             [jnp.where(view_of == view, values, 0.0) for view in range(VIEWS)], axis=0
         )
@@ -581,21 +696,7 @@
         name="answer",
     )(params, cameras, asked)
     rows = lax.all_to_all(answers, AXES, 0, 0, tiled=True)
-    row_grads = pl.pallas_call(
-        lambda *refs: tile_kernel(owned, *refs),
-        out_shape=full((LANES, 3 * LANES)),
-        scratch_shapes=[
-            pltpu.VMEM((3 * LANES, LANES), f32),
-            pltpu.VMEM((24 * chunks, LANES), f32),
-            pltpu.VMEM((9 * chunks, LANES), f32),
-            pltpu.VMEM((entry_count, TILE_SIDE * TILE_SIDE), f32),
-            pltpu.VMEM((entry_count, TILE_SIDE * TILE_SIDE), f32),
-            pltpu.VMEM((16 * chunks, LANES), f32),
-            pltpu.VMEM((FEATURES * chunks, LANES), f32),
-        ],
-        compiler_params=limits,
-        name="tiles",
-    )(entries, rank, rows, target[0])
+    row_grads = tiles_call(entries, rank, rows, target[0], owned)
     shares = lax.all_to_all(row_grads, AXES, 0, 0, tiled=True)
     return pl.pallas_call(
         lambda *refs: update_kernel(frame, *refs),

time: 92.7 us -> 76.2 us (0.82)
  Pallas kernels: 36.7 us -> 20.2 us
    pallas_call x1, Pallas kernels: 29.6 us -> 13.1 us  [tiles_call(): pl.pallas_call(lambda *refs: tile_kernel(owned, *refs), out_shape=jax.Sha...]
where the time goes in v2:
time: 76.2 us; the launch traced here: 75.9 us
  blocking collectives  35.5 us (47%)
  Pallas kernels  20.2 us (27%)
  waiting for transfers between devices  10.3 us (14%)
  starting transfers between devices  4.62 us (6%)
  local copies, waits for them, and re-layouts  3.83 us (5%)
    all_to_all x1, blocking collectives, per_device(): asked = lax.all_to_all(requests, AXES, 0, 0, tiled=True)  20.8 us
    all_to_all x1, blocking collectives, per_device(): shares = lax.all_to_all(row_grads, AXES, 0, 0, tiled=True)  14.7 us
    pallas_call x1, Pallas kernels, tiles_call(): pl.pallas_call(lambda *refs: tile_kernel(owned, *refs), out_shape=jax.Sha...  13.1 us
    all_to_all x1, waiting for transfers between devices, per_device(): rows = lax.all_to_all(answers, AXES, 0, 0, tiled=True)  10.3 us
    all_to_all x1, starting transfers between devices, per_device(): rows = lax.all_to_all(answers, AXES, 0, 0, tiled=True)  4.62 us
    pallas_call x1, Pallas kernels, per_device(): pl.pallas_call(lambda *refs: update_kernel(frame, *refs), out_shape=(full...  2.93 us
    pallas_call x1, Pallas kernels, per_device(): pl.pallas_call(lambda *refs: rank_kernel(owned, *refs), out_shape=(full((...  2.29 us
    pallas_call x1, Pallas kernels, per_device(): pl.pallas_call(lambda *refs: answer_kernel(frame, *refs), out_shape=full(...  1.83 us
  transfers between devices with their start and end apart: 1, of which 1 were waited for; matrix products, arithmetic and copies ran while one was open for 0% of the time, Pallas kernels for 0%

profile of v2, /device:TPU:1, one launch (start us, length us, event | category | flops | bytes accessed | tf_op | source)
XLA Modules:
  0.0 75.9 jit_solution(6300068463065435754)
XLA Ops:
  0.6 0.0 copy-start.6
  0.6 0.5 broadcast.10
  1.2 0.1 copy-done.6
  1.3 0.7 reduce.3
  1.9 0.1 ge.17
  2.0 0.8 %copy.15 = s32[2,8,256]{1,2,0:T(8,128)S(1)} copy(s32[2,8,256]{2,1,0:T(8,128)} %bitcast.26) | data formatting | bytes 32768 | tf_op jit(solution)/shard_map/squeeze | solution.py:677
  2.9 0.1 reshape.26.refs_0_
  3.1 0.0 copy-start
  3.1 2.3 %rank.1 = (s32[32,128]{1,0:T(8,128)S(1)}, f32[128,32]{1,0:T(8,128)S(1)}) custom-call(s32[32,128]{1,0:T(8,128)S(1)} %reshape.26.refs_0_), custom_call_target="tpu_custom_call" | custom-call | tf_op jit(solution)/shard_map/rank/pallas_call | solution.py:685
  5.4 0.0 copy-start.4
  5.4 20.8 %all_to_all.33 = f32[128,1,32]{2,1,0:T(1,128)S(1)} all-to-all(f32[128,1,32]{2,1,0:T(1,128)S(1)} %bitcast.25), channel_id=1, replica_groups=mesh['views'=4,'tiles'=32] {'views','tiles'}, dimensions={0} | all-to-all | bytes 32768 | tf_op jit(solution)/shard_map/all_to_all | solution.py:691
  26.2 0.0 copy-done
  26.2 0.0 copy-done.4
  26.2 1.8 %answer.1 = f32[128,384]{1,0:T(8,128)S(1)} custom-call(f32[59,512]{1,0:T(8,128)S(1)} %copy-done, f32[4,6]{1,0:T(4,128)S(1)} %copy-done.4, f32[128,32]{1,0:T(8,128)S(1)} %bitcast.22), custom_call_target="tpu_custom_call" | custom-call | tf_op jit(solution)/shard_map/answer/pallas_call | solution.py:692
  28.0 0.9 %copy.17 = f32[128,1,384]{2,1,0:T(1,128)} copy(f32[128,1,384]{2,0,1:T(8,128)S(1)} %bitcast.18) | data formatting | bytes 393216 | tf_op jit(solution)/shard_map/all_to_all | solution.py:698
  28.9 4.6 %all-to-all-start.1 = ((f32[128,1,384]{2,1,0:T(1,128)}), f32[128,1,384]{2,1,0:T(1,128)S(1)}, u32[]{:S(2)}, u32[]{:S(2)}) async-start(f32[128,1,384]{2,1,0:T(1,128)} %copy.17), calls=%async_computation.1 | async-start | bytes 393216 | tf_op jit(solution)/shard_map/all_to_all | solution.py:698
  33.5 0.0 copy-done.5
  33.6 10.3 %all-to-all-done.1 = f32[128,1,384]{2,1,0:T(1,128)S(1)} async-done(((f32[128,1,384]{2,1,0:T(1,128)}), f32[128,1,384]{2,1,0:T(1,128)S(1)}, u32[]{:S(2)}, u32[]{:S(2)}) %all-to-all-start.1) | async-done | bytes 196640 | tf_op jit(solution)/shard_map/all_to_all | solution.py:698
  43.9 13.1 %tiles.1 = f32[128,384]{1,0:T(8,128)S(1)} custom-call(s32[32,128]{1,0:T(8,128)S(1)} %reshape.26.refs_0_, s32[32,128]{1,0:T(8,128)S(1)} %get-tuple-element.6.refs_1_, f32[128,384]{1,0:T(8,128)S(1)} %bitcast.20, f32[16,3,256]{2,1,0:T(4,128)S(1)} %bitcast.24), custom_call_target="tpu_custom_call" | custom-call | tf_op jit(solution)/shard_map/tiles/pallas_call | solution.py:565
  57.0 0.2 copy.19
  57.3 14.7 %all_to_all.34 = f32[128,1,384]{2,1,0:T(1,128)S(1)} all-to-all(f32[128,1,384]{2,1,0:T(1,128)S(1)} %copy.19), channel_id=1, replica_groups=mesh['views'=4,'tiles'=32] {'views','tiles'}, dimensions={0} | all-to-all | bytes 393216 | tf_op jit(solution)/shard_map/all_to_all | solution.py:700
  72.0 0.9 %copy-done.1 = f32[59,512]{1,0:T(8,128)S(1)} copy-done((f32[59,512]{1,0:T(8,128)S(1)}, f32[59,512]{1,0:T(8,128)}, u32[]{:S(2)}) %copy-start.1) | copy-done | bytes 120856
  72.9 0.1 copy-done.2
  72.9 2.9 %update.1 = (f32[59,512]{1,0:T(8,128)}, f32[59,512]{1,0:T(8,128)}, f32[59,512]{1,0:T(8,128)}) custom-call(f32[59,512]{1,0:T(8,128)S(1)} %copy-done, f32[59,512]{1,0:T(8,128)S(1)} %copy-done.1, f32[59,512]{1,0:T(8,128)S(1)} %copy-done.2, f32[4,6]{1,0:T(4,128)S(1)} %copy-done.4, f32[128,32]{1,0:T(8,128)S(1)} %bitcast.23, f32[128,384]{1,0:T(8,128)S(1)} %bitcast.19, ...), custom_call_target="tpu_custom_call" | custom-call | tf_op jit(solution)/shard_map/update/pallas_call | solution.py:701
  (9 shorter events, 0.1 us)
Async XLA Ops:
  0.6 0.7 copy-start.6
  3.1 23.1 %copy-start = (f32[59,512]{1,0:T(8,128)S(1)}, f32[59,512]{1,0:T(8,128)}, u32[]{:S(2)}) copy-start(f32[59,512]{1,0:T(8,128)} %refs_0_.3) | copy-start | bytes 362500
  5.4 20.8 %copy-start.4 = (f32[4,6]{1,0:T(4,128)S(1)}, f32[4,6]{1,0:T(4,128)}, u32[]{:S(2)}) copy-start(f32[4,6]{1,0:T(4,128)} %refs_3_.1) | copy-start | bytes 292
  28.9 4.6 %copy-start.5 = (f32[1,16,3,256]{3,1,2,0:T(8,128)S(1)}, f32[1,16,3,256]{3,1,2,0:T(8,128)}, u32[]{:S(2)}) copy-start(f32[1,16,3,256]{3,1,2,0:T(8,128)} %param.12) | copy-start | bytes 147460
  28.9 15.0 %all-to-all-start.1 = ((f32[128,1,384]{2,1,0:T(1,128)}), f32[128,1,384]{2,1,0:T(1,128)S(1)}, u32[]{:S(2)}, u32[]{:S(2)}) async-start(f32[128,1,384]{2,1,0:T(1,128)} %copy.17), calls=%async_computation.1 | async-start | bytes 393216 | tf_op jit(solution)/shard_map/all_to_all | solution.py:698
  72.0 0.9 %copy-start.1 = (f32[59,512]{1,0:T(8,128)S(1)}, f32[59,512]{1,0:T(8,128)}, u32[]{:S(2)}) copy-start(f32[59,512]{1,0:T(8,128)} %refs_1_.3) | copy-start | bytes 362500
  72.0 1.0 %copy-start.2 = (f32[59,512]{1,0:T(8,128)S(1)}, f32[59,512]{1,0:T(8,128)}, u32[]{:S(2)}) copy-start(f32[59,512]{1,0:T(8,128)} %refs_2_.1) | copy-start | bytes 362500
  72.0 1.0 %copy-start.3 = (f32[59,1]{1,0:T(8,128)S(1)}, f32[59,1]{1,0:T(8,128)}, u32[]{:S(2)}) copy-start(f32[59,1]{1,0:T(8,128)} %constant.6.clone.refs_6_) | copy-start | bytes 712

commit v3 on v2

--- a/solution.py
+++ b/solution.py
@@ -1,6 +1,5 @@
 import jax
 import jax.numpy as jnp
-import numpy as np
 from jax import lax
 from jax.experimental import pallas as pl
 from jax.experimental.pallas import tpu as pltpu
@@ -14,6 +13,7 @@
 VIEWS = 4
 SLOTS = 32
 HALF = SLOTS // 2
+BLOCK = 8
 FEATURES = 9
 AXES = ("views", "tiles")
 
@@ -203,37 +203,78 @@
     return out
 
 
-def rank_kernel(owned, entries_ref, rank_ref, request_ref):
+def one_hot(ids, row):
+    row = jnp.broadcast_to(row, (16, row.shape[1])).astype(bf16)
+    row = jnp.concatenate([row] * (ids.shape[0] // 16), axis=0)
+    return jnp.where(ids == row, jnp.ones((), bf16), jnp.zeros((), bf16))
+
+
+def small_ids(count):
+    return iota((count, LANES), 0).astype(f32).astype(bf16)
+
+
+def rank_kernel(
+    owned, lists_ref, lengths_ref, entries_ref, rank_ref, request_ref, hot_ref, wanted_ref
+):
     chunks = entries_ref.shape[0]
+    per_group = chunks // 2
+    steps = LANES // GROUP
+    lengths = jnp.concatenate(
+        [lengths_ref[...], jnp.zeros((1, LANES - lengths_ref.shape[1]), i32)], axis=1
+    )
+    lengths = jnp.broadcast_to(lengths, (GROUP, LANES))
+    lane = iota((GROUP, LANES), 1)
+    tile = lax.rem(lane, GROUP)
+    spot = iota((GROUP, LANES), 0) * steps + lax.div(lane, GROUP)
+    for group in range(2):
+        length = jnp.take_along_axis(
+            lengths, group * GROUP + tile, axis=1, mode="promise_in_bounds"
+        )
+        for half in range(per_group // GROUP):
+            made = jnp.zeros((GROUP, LANES), i32)
+            for at in range(GROUP):
+                row = group * GROUP + at
+                source = jnp.broadcast_to(
+                    lists_ref[row : row + 1, half * LANES : (half + 1) * LANES], (GROUP, LANES)
+                )
+                found = jnp.take_along_axis(source, spot, axis=1, mode="promise_in_bounds")
+                made = jnp.where(tile == at, found, made)
+            dead = spot + half * LANES >= length
+            row = group * per_group + half * GROUP
+            entries_ref[row : row + GROUP, :] = jnp.where(dead, made + owned * LANES, made)
     entries = entries_ref[...]
     owner = lax.rem(lax.div(entries, owned), LANES)
+    owner_row = owner.astype(f32)
     column = lax.rem(entries, owned)
     low = lax.rem(column, 256).astype(f32)
     high = lax.div(column, 256).astype(f32)
     before = jnp.where(iota((LANES, LANES), 0) < iota((LANES, LANES), 1), 1.0, 0.0)
     adder = jnp.concatenate([before, jnp.ones((LANES, LANES), f32)], axis=1).astype(bf16)
     owner_id = iota((LANES, LANES), 0)
-    slot_id = iota((SLOTS, LANES), 0)
+    owner_one = small_ids(LANES)
+    slot_one = small_ids(SLOTS)
     base = jnp.zeros((LANES, LANES), f32)
-    requests = jnp.zeros((LANES, 2 * SLOTS), f32)
     for at in range(chunks):
-        hot = owner_id == owner[at : at + 1, :]
-        hot_one = jnp.where(hot, 1.0, 0.0).astype(bf16)
-        counts = dot(hot_one, adder, 1, 0)
+        lanes = slice(at * LANES, (at + 1) * LANES)
+        hot = one_hot(owner_one, owner_row[at : at + 1, :])
+        hot_ref[:, lanes] = hot
+        counts = dot(hot, adder, 1, 0)
         rank = jnp.sum(
-            jnp.where(hot, counts[:, :LANES] + base, 0.0), axis=0, keepdims=True
-        ).astype(i32)
+            jnp.where(owner_id == owner[at : at + 1, :], counts[:, :LANES] + base, 0.0),
+            axis=0,
+            keepdims=True,
+        )
         base = base + counts[:, LANES:]
-        rank_ref[at : at + 1, :] = rank
-        slot = slot_id == rank
-        wanted = jnp.concatenate(
+        rank_ref[at : at + 1, :] = rank.astype(i32)
+        slot = one_hot(slot_one, rank)
+        wanted_ref[:, lanes] = jnp.concatenate(
             [
-                jnp.where(slot, low[at : at + 1, :], 0.0),
-                jnp.where(slot, high[at : at + 1, :], 0.0),
+                slot * jnp.broadcast_to(part[at : at + 1, :], (SLOTS, LANES)).astype(bf16)
+                for part in (low, high)
             ],
             axis=0,
-        ).astype(bf16)
-        requests = requests + dot(hot_one, wanted, 1, 1)
+        )
+    requests = dot(hot_ref[...], wanted_ref[...], 1, 1)
     request_ref[...] = requests[:, :SLOTS] + 256.0 * requests[:, SLOTS:]
 
 
@@ -243,11 +284,27 @@
     return wide.T[:SLOTS, :].astype(i32)
 
 
-def answer_kernel(frame, params_ref, cameras_ref, asked_ref, rows_ref):
+def project_kernel(frame, params_ref, cameras_ref, table_ref):
     owned = params_ref.shape[1]
     rotation, shift = camera_terms(cameras_ref, owned)
     params = [jnp.broadcast_to(params_ref[at : at + 1, :], (VIEWS, owned)) for at in range(59)]
-    projected = project(params, rotation, shift, *frame)
+    for at, values in enumerate(project(params, rotation, shift, *frame)):
+        table_ref[at * VIEWS : (at + 1) * VIEWS, :] = values
+
+
+def spread_rows(stack, out_ref):
+    for part in range(3):
+        out_ref[pl.ds(part, LANES, stride=3), :] = stack[part * LANES : (part + 1) * LANES].T
+
+
+def gathered_rows(rows_ref):
+    return jnp.concatenate(
+        [rows_ref[pl.ds(part, LANES, stride=3), :].T for part in range(3)], axis=0
+    )
+
+
+def answer_kernel(table_ref, asked_ref, rows_ref):
+    owned = table_ref.shape[1]
     asked = flipped_requests(asked_ref)
     chunk_of = lax.div(asked, LANES)
     lane_of = lax.rem(asked, LANES)
@@ -257,9 +314,9 @@
         for chunk in range(owned // LANES):
             mask = (view_of == view) & (chunk_of == chunk)
             for at in range(FEATURES):
+                row = at * VIEWS + view
                 source = jnp.broadcast_to(
-                    projected[at][view : view + 1, chunk * LANES : (chunk + 1) * LANES],
-                    (SLOTS, LANES),
+                    table_ref[row : row + 1, chunk * LANES : (chunk + 1) * LANES], (SLOTS, LANES)
                 )
                 found = jnp.take_along_axis(source, lane_of, axis=1, mode="promise_in_bounds")
                 chosen[at] = jnp.where(mask, found, chosen[at])
@@ -267,11 +324,18 @@
         chosen[at][half * HALF : (half + 1) * HALF] for half in range(2) for at in range(FEATURES)
     ]
     stack.append(jnp.zeros((3 * LANES - SLOTS * FEATURES, LANES), f32))
-    stack = jnp.concatenate(stack, axis=0)
-    for part in range(3):
-        rows_ref[:, part * LANES : (part + 1) * LANES] = stack[
-            part * LANES : (part + 1) * LANES
-        ].T
+    spread_rows(jnp.concatenate(stack, axis=0), rows_ref)
+
+
+def prepare_kernel(owned, entries_ref, rank_ref, asked_ref, hot_ref, column_ref):
+    ids = small_ids(2 * LANES)
+    place, _ = slot_columns(entries_ref[...], rank_ref[...], owned)
+    place = place.astype(f32)
+    for at in range(entries_ref.shape[0]):
+        hot_ref[:, at * LANES : (at + 1) * LANES] = one_hot(ids, place[at : at + 1, :])
+    low = lax.rem(flipped_requests(asked_ref), 2 * LANES).astype(f32)
+    for at in range(SLOTS):
+        column_ref[:, at * LANES : (at + 1) * LANES] = one_hot(ids, low[at : at + 1, :])
 
 
 def slot_columns(entries, rank, owned):
@@ -283,10 +347,10 @@
     owned,
     entries_ref,
     rank_ref,
+    hot_ref,
     rows_ref,
     target_ref,
     grads_ref,
-    hot_ref,
     picked_ref,
     coef_ref,
     color_ref,
@@ -299,6 +363,7 @@
     moment_ref,
     grad_ref,
     spread_ref,
+    paint_ref,
 ):
     chunks = entries_ref.shape[0]
     groups = 2
@@ -310,34 +375,29 @@
 
     entries = entries_ref[...]
     live = entries < owned * LANES
-    place, below = slot_columns(entries, rank_ref[...], owned)
-    place = place.astype(f32)
-    place_id = iota((2 * LANES, LANES), 0).astype(f32).astype(bf16)
-    for at in range(chunks):
-        row = jnp.broadcast_to(place[at : at + 1, :], (2 * LANES, LANES)).astype(bf16)
-        hot_ref[:, at * LANES : (at + 1) * LANES] = jnp.where(
-            place_id == row, jnp.ones((), bf16), jnp.zeros((), bf16)
-        )
-
-    flipped = jnp.concatenate(
-        [rows_ref[:, part * LANES : (part + 1) * LANES].T for part in range(3)], axis=0
-    )
+    _, below = slot_columns(entries, rank_ref[...], owned)
+
+    flipped = gathered_rows(rows_ref)
     table = jnp.concatenate([flipped[:span], flipped[span : 2 * span]], axis=1)
     table = jnp.concatenate(pieces(table, 3), axis=0)
-    half_id = iota((HALF, LANES), 0)
     for at in range(0, chunks, 2):
         found = dot(table, hot_ref[:, at * LANES : (at + 2) * LANES], 1, 0)
         found = found[:span] + (found[span : 2 * span] + found[2 * span :])
         for side in range(2):
-            mask = half_id == below[at + side : at + side + 1, :]
+            row = jnp.broadcast_to(below[at + side : at + side + 1, :], (8, LANES))
+            index, upper = lax.rem(row, 8), row >= 8
             for feature in range(FEATURES):
-                values = found[
-                    feature * HALF : (feature + 1) * HALF, side * LANES : (side + 1) * LANES
+                first, second = [
+                    jnp.take_along_axis(
+                        found[part : part + 8, side * LANES : (side + 1) * LANES],
+                        index,
+                        axis=0,
+                        mode="promise_in_bounds",
+                    )
+                    for part in (feature * HALF, feature * HALF + 8)
                 ]
                 row = feature * chunks + at + side
-                picked_ref[row : row + 1, :] = jnp.sum(
-                    jnp.where(mask, values, 0.0), axis=0, keepdims=True
-                )
+                picked_ref[row : row + 1, :] = jnp.where(upper, second, first)[:1, :]
     shape = (chunks, LANES)
     chosen = [picked_ref[at * chunks : (at + 1) * chunks, :] for at in range(FEATURES)]
 
@@ -379,71 +439,72 @@
     base_three = jnp.concatenate([base, base, base], axis=0).astype(bf16)
     same_tile = lax.rem(iota((GROUP, LANES), 1), GROUP) == iota((GROUP, LANES), 0)
 
-    def rows_of(chunk):
-        return pl.ds(pl.multiple_of(chunk * LANES, LANES), LANES)
-
-    def color_rows(chunk):
+    for at in range(chunks):
         rows = []
         for part in range(9):
-            row = color_ref[pl.ds(part * chunks + chunk, 1), :]
+            row = color_ref[part * chunks + at : part * chunks + at + 1, :]
             rows.append(jnp.where(same_tile, jnp.broadcast_to(row, (GROUP, LANES)), 0.0))
-        return jnp.concatenate(rows, axis=0).astype(bf16)
-
-    def shade(at):
+        rows.append(jnp.zeros((GROUP, LANES), f32))
+        paint_ref[:, at * LANES : (at + 1) * LANES] = jnp.concatenate(rows, axis=0).astype(bf16)
+
+    def rows_of(chunk, count=1):
+        return pl.ds(pl.multiple_of(chunk * LANES, LANES), count * LANES)
+
+    def shade(at, carry):
+        coef = jnp.concatenate(
+            [coef_ref[pl.ds(at * BLOCK + off, 24, stride=chunks), :] for off in range(BLOCK)], axis=1
+        )
+        alpha_ref[rows_of(at * BLOCK, BLOCK), :] = jnp.exp2(dot(coef.astype(bf16), base_three, 0, 0))
+        return carry
+
+    lax.fori_loop(0, chunks // BLOCK, shade, 0)
+
+    def load(ref, at):
+        return [ref[rows_of(group * per_group + at), :] for group in range(groups)]
+
+    def keep(refs, at, made):
         for group in range(groups):
-            chunk = group * per_group + at
-            coef = coef_ref[pl.ds(chunk, 24, stride=chunks), :].astype(bf16)
-            alpha_ref[rows_of(chunk), :] = jnp.exp2(dot(coef, base_three, 0, 0))
+            for ref, values in zip(refs, made[group]):
+                ref[rows_of(group * per_group + at), :] = values
 
     def weigh(at, clears):
-        out = []
+        alphas = load(alpha_ref, at)
+        out, made = [], []
         for group in range(groups):
-            clear = clears[group]
-            rows = rows_of(group * per_group + at)
-            alpha = alpha_ref[rows, :]
+            clear, alpha = clears[group], alphas[group]
             weights = []
             for step in range(steps):
                 weight = alpha[step * GROUP : (step + 1) * GROUP, :] * clear
                 clear = clear - weight
                 weights.append(weight)
             weight = jnp.concatenate(weights, axis=0)
-            weight_ref[rows, :] = weight
-            high_ref[rows, :], middle_ref[rows, :], low_ref[rows, :] = pieces(weight, 3)
+            made.append((weight, *pieces(weight, 3)))
             out.append(clear)
+        keep((weight_ref, high_ref, middle_ref, low_ref), at, made)
         return tuple(out)
+
+    lax.fori_loop(0, per_group, weigh, (jnp.ones((GROUP, pixels), f32),) * groups)
 
     def blend(at, renders):
         out = []
         for group in range(groups):
-            chunk = group * per_group + at
-            rows = rows_of(chunk)
-            colors = color_rows(chunk)
-            colors = jnp.concatenate([colors, colors, colors], axis=1)
-            parts = jnp.concatenate(
-                [high_ref[rows, :], middle_ref[rows, :], low_ref[rows, :]], axis=0
+            chunk = group * per_group + at * BLOCK
+            rows = rows_of(chunk, BLOCK)
+            paint = paint_ref[:72, rows]
+            out.append(
+                renders[group]
+                + (
+                    dot(paint, high_ref[rows, :], 1, 0)
+                    + (dot(paint, middle_ref[rows, :], 1, 0) + dot(paint, low_ref[rows, :], 1, 0))
+                )
             )
-            out.append(renders[group] + dot(colors, parts, 1, 0))
         return tuple(out)
 
-    clears = (jnp.ones((GROUP, pixels), f32),) * groups
-    renders = (jnp.zeros((72, pixels), f32),) * groups
-    shade(0)
-    shade(1)
-    clears = weigh(0, clears)
-
-    def forward(at, carry):
-        clears, renders = carry
-        shade(at + 1)
-        renders = blend(at - 1, renders)
-        clears = weigh(at, clears)
-        return clears, renders
-
-    clears, renders = lax.fori_loop(1, per_group - 1, forward, (clears, renders))
-    renders = blend(per_group - 2, renders)
-    clears = weigh(per_group - 1, clears)
-    renders = blend(per_group - 1, renders)
-
-    signs, sign_twos, sign_threes = [], [], []
+    renders = lax.fori_loop(
+        0, per_group // BLOCK, blend, (jnp.zeros((72, pixels), f32),) * groups
+    )
+
+    signs, sign_twos = [], []
     for group in range(groups):
         render = renders[group]
         render = render[:24] + (render[24:48] + render[48:])
@@ -451,65 +512,63 @@
         for at in range(3):
             gap = (
                 render[at * GROUP : (at + 1) * GROUP, :]
-                - target_ref[group * GROUP : (group + 1) * GROUP, at, :]
+                - target_ref[at, group * GROUP : (group + 1) * GROUP, :]
             )
             rows.append(jnp.where(gap > 0.0, 1.0, jnp.where(gap < 0.0, -1.0, 0.0)))
         sign = jnp.concatenate(rows, axis=0)
-        sign_twos.append(jnp.concatenate([sign, sign], axis=1).astype(bf16))
-        sign_threes.append(jnp.concatenate([sign, sign, sign], axis=0).astype(bf16))
-
-    def draw(at):
+        signs.append(sign.astype(bf16))
+        sign_twos.append(jnp.concatenate([sign, sign], axis=0).astype(bf16))
+
+    def draw(at, carry):
         for group in range(groups):
-            chunk = group * per_group + at
-            pull_ref[rows_of(chunk), :] = dot(color_rows(chunk), sign_threes[group], 0, 0)
-
-    def unweigh(at, behinds):
-        out = []
+            rows = rows_of(group * per_group + at * BLOCK, BLOCK)
+            pull_ref[rows, :] = dot(paint_ref[:48, rows], sign_twos[group], 0, 0)
+        return carry
+
+    lax.fori_loop(0, per_group // BLOCK, draw, 0)
+
+    def unweigh(back, behinds):
+        at = per_group - 1 - back
+        pulls, alphas, weights = [load(ref, at) for ref in (pull_ref, alpha_ref, weight_ref)]
+        out, made = [], []
         for group in range(groups):
+            pull, alpha, weight = pulls[group], alphas[group], weights[group]
             behind = behinds[group]
-            rows = rows_of(group * per_group + at)
-            pull, alpha, weight = pull_ref[rows, :], alpha_ref[rows, :], weight_ref[rows, :]
             by_alpha = [None] * steps
             for step in reversed(range(steps)):
                 part = slice(step * GROUP, (step + 1) * GROUP)
                 gap = pull[part, :] - behind
                 by_alpha[step] = weight[part, :] * gap
                 behind = behind + alpha[part, :] * gap
-            low_ref[rows, :], spread_ref[rows, :] = pieces(jnp.concatenate(by_alpha, axis=0), 2)
+            made.append(pieces(jnp.concatenate(by_alpha, axis=0), 2))
             out.append(behind)
+        keep((low_ref, spread_ref), at, made)
         return tuple(out)
 
-    def total(at):
+    lax.fori_loop(0, per_group, unweigh, (jnp.zeros((GROUP, pixels), f32),) * groups)
+
+    def total(at, carry):
         for group in range(groups):
-            chunk = group * per_group + at
-            rows = rows_of(chunk)
-            row = pl.multiple_of(chunk * 16, 16)
+            chunk = group * per_group + at * BLOCK
+            rows = rows_of(chunk, BLOCK)
             parts = jnp.concatenate([low_ref[rows, :], spread_ref[rows, :]], axis=1)
-            moment_ref[pl.ds(row, 8), :] = dot(base_two, parts, 1, 1)
-            parts = jnp.concatenate([high_ref[rows, :], middle_ref[rows, :]], axis=1)
-            by_color = dot(sign_twos[group], parts, 1, 1)
-            for channel in range(3):
-                moment_ref[pl.ds(row + 8 + channel, 1), :] = jnp.sum(
-                    jnp.where(same_tile, by_color[channel * GROUP : (channel + 1) * GROUP], 0.0),
-                    axis=0,
-                    keepdims=True,
-                )
-
-    behinds = (jnp.zeros((GROUP, pixels), f32),) * groups
-    draw(per_group - 1)
-    draw(per_group - 2)
-    behinds = unweigh(per_group - 1, behinds)
-
-    def backward(back, behinds):
-        at = per_group - 1 - back
-        draw(at - 1)
-        total(at + 1)
-        return unweigh(at, behinds)
-
-    behinds = lax.fori_loop(1, per_group - 1, backward, behinds)
-    total(1)
-    behinds = unweigh(0, behinds)
-    total(0)
+            moments = dot(base_two, parts, 1, 1)
+            by_color = dot(signs[group], high_ref[rows, :], 1, 1)
+            for off in range(BLOCK):
+                row = pl.multiple_of((chunk + off) * 16, 16)
+                lanes = slice(off * LANES, (off + 1) * LANES)
+                moment_ref[pl.ds(row, 8), :] = moments[:, lanes]
+                for channel in range(3):
+                    moment_ref[pl.ds(row + 8 + channel, 1), :] = jnp.sum(
+                        jnp.where(
+                            same_tile, by_color[channel * GROUP : (channel + 1) * GROUP, lanes], 0.0
+                        ),
+                        axis=0,
+                        keepdims=True,
+                    )
+        return carry
+
+    lax.fori_loop(0, per_group // BLOCK, total, 0)
 
     sums = [moment_ref[pl.ds(at, chunks, stride=16), :] for at in range(6)]
     sum_x = sums[1] - at_u * sums[0]
@@ -526,35 +585,28 @@
         sums[0],
     ] + [moment_ref[pl.ds(8 + at, chunks, stride=16), :] for at in range(3)]
 
-    half_one = half_id.astype(f32).astype(bf16)
+    half_one = small_ids(HALF)
     below = below.astype(f32)
     grads = [pieces(jnp.where(live, grad, 0.0), 2) for grad in grads]
     grads = [[part.astype(f32) for part in split] for split in grads]
     for at in range(chunks):
-        mask = half_one == jnp.broadcast_to(below[at : at + 1, :], (HALF, LANES)).astype(bf16)
+        mask = one_hot(half_one, below[at : at + 1, :])
         for part in range(2):
             for feature in range(FEATURES):
                 row = grads[feature][part][at : at + 1, :]
                 grad_ref[
                     part * span + feature * HALF : part * span + (feature + 1) * HALF,
                     at * LANES : (at + 1) * LANES,
-                ] = jnp.where(
-                    mask,
-                    jnp.broadcast_to(row, (HALF, LANES)).astype(bf16),
-                    jnp.zeros((), bf16),
-                )
+                ] = mask * jnp.broadcast_to(row, (HALF, LANES)).astype(bf16)
     sent = dot(grad_ref[...], hot_ref[...], 1, 1)
     sent = sent[:span] + sent[span:]
     sent = jnp.concatenate(
         [sent[:, :LANES], sent[:, LANES:], jnp.zeros((3 * LANES - 2 * span, LANES), f32)], axis=0
     )
-    for part in range(3):
-        grads_ref[:, part * LANES : (part + 1) * LANES] = sent[
-            part * LANES : (part + 1) * LANES, :
-        ].T
-
-
-def tiles_call(entries, rank, rows, target, owned):
+    spread_rows(sent, grads_ref)
+
+
+def tiles_call(entries, rank, hot, rows, target, owned):
     chunks = entries.shape[0]
     pixels = TILE_SIDE * TILE_SIDE
     count = chunks * LANES
@@ -564,9 +616,8 @@
 
     return pl.pallas_call(
         lambda *refs: tile_kernel(owned, *refs),
-        out_shape=jax.ShapeDtypeStruct((LANES, 3 * LANES), f32),
+        out_shape=jax.ShapeDtypeStruct((3 * LANES, LANES), f32),
         scratch_shapes=[
-            pltpu.VMEM((2 * LANES, count), bf16),
             pltpu.VMEM((FEATURES * chunks, LANES), f32),
             pltpu.VMEM((24 * chunks, LANES), f32),
             pltpu.VMEM((9 * chunks, LANES), f32),
@@ -579,53 +630,80 @@
             pltpu.VMEM((16 * chunks, LANES), f32),
             pltpu.VMEM((2 * FEATURES * HALF, count), bf16),
             plane(bf16),
+            pltpu.VMEM((80, count), bf16),
         ],
         compiler_params=pltpu.CompilerParams(vmem_limit_bytes=48 * 1024 * 1024),
         name="tiles",
-    )(entries, rank, rows, target)
+    )(entries, rank, hot, rows, target)
+
+
+def learning_rates(shape):
+    row = iota(shape, 0)
+    rates = jnp.full(shape, 0.000125, f32)
+    for stop, rate in ((14, 0.0025), (11, 0.05), (10, 0.001), (6, 0.005), (3, 0.00016)):
+        rates = jnp.where(row < stop, rate, rates)
+    return rates
 
 
 def update_kernel(
     frame,
     params_ref,
-    first_ref,
-    second_ref,
+    first_hbm,
+    second_hbm,
     cameras_ref,
     asked_ref,
+    column_ref,
     grads_ref,
-    rates_ref,
     new_params_ref,
     new_first_ref,
     new_second_ref,
     source_ref,
+    spread_ref,
     dense_ref,
     gradient_ref,
+    first_ref,
+    second_ref,
+    arrived,
 ):
     owned = params_ref.shape[1]
-    asked = flipped_requests(asked_ref)
-    for part in range(3):
-        source_ref[part * LANES : (part + 1) * LANES, :] = grads_ref[
-            :, part * LANES : (part + 1) * LANES
-        ].T
-    source_ref[3 * LANES :, :] = jnp.zeros((LANES, LANES), f32)
-    view_of = lax.div(iota((16, LANES), 1), LANES // VIEWS)
-    column_id = iota((owned, LANES), 0)
-    dense = jnp.zeros((2 * VIEWS * 16, owned), f32)
+    copies = [
+        pltpu.make_async_copy(source, target, arrived.at[at])
+        for at, (source, target) in enumerate(((first_hbm, first_ref), (second_hbm, second_ref)))
+    ]
+    for copy in copies:
+        copy.start()
+    upper = lax.div(flipped_requests(asked_ref), 2 * LANES)
+    key = (lax.div(iota((SLOTS, LANES), 1), LANES // VIEWS) * 2 + upper).astype(f32)
+    flipped = gathered_rows(grads_ref)
+    for part, values in enumerate(pieces(flipped, 2)):
+        source_ref[part * 3 * LANES : (part + 1) * 3 * LANES, :] = values.astype(f32)
+    source_ref[6 * LANES :, :] = jnp.zeros((LANES, LANES), f32)
+    keys = [jnp.full((16, LANES), at, f32).astype(bf16) for at in range(2 * VIEWS)]
     for slot in range(SLOTS):
-        hot = jnp.where(column_id == asked[slot : slot + 1, :], 1.0, 0.0).astype(bf16)
         first = slot // HALF * FEATURES * HALF + slot % HALF
-        values = source_ref[pl.ds(first, 16, stride=HALF), :]
-        values = jnp.concatenate(
-            [jnp.where(view_of == view, values, 0.0) for view in range(VIEWS)], axis=0
+        mine = jnp.broadcast_to(key[slot : slot + 1, :], (16, LANES)).astype(bf16)
+        parts = [
+            source_ref[pl.ds(part * 3 * LANES + first, 16, stride=HALF), :].astype(bf16)
+            for part in range(2)
+        ]
+        spread_ref[:, slot * LANES : (slot + 1) * LANES] = jnp.concatenate(
+            [
+                jnp.where(mine == keys[at], values, jnp.zeros((), bf16))
+                for values in parts
+                for at in range(2 * VIEWS)
+            ],
+            axis=0,
         )
-        high, low = pieces(values, 2)
-        dense = dense + dot(jnp.concatenate([high, low], axis=0), hot, 1, 1)
-    dense = dense[: VIEWS * 16] + dense[VIEWS * 16 :]
+    dense = dot(spread_ref[...], column_ref[...], 1, 1)
+    dense = dense[:LANES] + dense[LANES:]
     spans = range(owned // LANES)
     for span in spans:
-        dense_ref[span * VIEWS * 16 : (span + 1) * VIEWS * 16, :] = dense[
-            :, span * LANES : (span + 1) * LANES
-        ]
+        side, lanes = span // 2, slice(span % 2 * LANES, (span % 2 + 1) * LANES)
+        for view in range(VIEWS):
+            row = (view * 2 + side) * 16
+            dense_ref[(span * VIEWS + view) * 16 : (span * VIEWS + view + 1) * 16, :] = dense[
+                row : row + 16, lanes
+            ]
     cotangents = [
         jnp.concatenate(
             [dense_ref[pl.ds(span * VIEWS * 16 + at, VIEWS, stride=16), :] for span in spans], axis=1
@@ -640,26 +718,16 @@
     for at in range(59):
         gradient_ref[at : at + 1, :] = jnp.sum(by_params[at], axis=0, keepdims=True)
     gradient = gradient_ref[:59, :]
+    for copy in copies:
+        copy.wait()
     new_first = beta_one * first_ref[...] + (1.0 - beta_one) * gradient
     new_second = beta_two * second_ref[...] + (1.0 - beta_two) * gradient * gradient
     new_first_ref[...] = new_first
     new_second_ref[...] = new_second
-    step_size = rates_ref[...] * (new_first / (1.0 - beta_one**ADAM_STEP))
+    step_size = learning_rates((59, owned)) * (new_first / (1.0 - beta_one**ADAM_STEP))
     new_params_ref[...] = params_ref[...] - step_size / (
         jnp.sqrt(new_second / (1.0 - beta_two**ADAM_STEP)) + adam_eps
     )
-
-
-learning = np.concatenate(
-    [
-        np.full(3, 0.00016),
-        np.full(3, 0.005),
-        np.full(4, 0.001),
-        np.full(1, 0.05),
-        np.full(3, 0.0025),
-        np.full(45, 0.000125),
-    ]
-).astype(np.float32)[:, None]
 
 
 def per_device(params, first_moment, second_moment, cameras, target, lists, lengths):
@@ -673,42 +741,65 @@
     frame = (float(width), 0.5 * width, 0.5 * height)
     limits = pltpu.CompilerParams(vmem_limit_bytes=48 * 1024 * 1024)
 
-    dead = jnp.arange(list_size, dtype=i32)[None, :] >= lengths[0][:, None]
-    entries = lists[0] + jnp.where(dead, owned * LANES, 0)
-    entries = (
-        entries.reshape(tile_dev // GROUP, GROUP, list_size).transpose(0, 2, 1).reshape(chunks, LANES)
-    )
-
     def full(shape, dtype=f32):
         return jax.ShapeDtypeStruct(shape, dtype)
 
-    rank, requests = pl.pallas_call(
+    def sent(rows):
+        rows = lax.all_to_all(rows.reshape(LANES, 3 * LANES), AXES, 0, 0, tiled=True)
+        return rows.reshape(3 * LANES, LANES)
+
+    entries, rank, requests = pl.pallas_call(
         lambda *refs: rank_kernel(owned, *refs),
-        out_shape=(full((chunks, LANES), i32), full((LANES, SLOTS))),
+        out_shape=(full((chunks, LANES), i32), full((chunks, LANES), i32), full((LANES, SLOTS))),
+        scratch_shapes=[
+            pltpu.VMEM((LANES, entry_count), bf16),
+            pltpu.VMEM((2 * SLOTS, entry_count), bf16),
+        ],
         compiler_params=limits,
         name="rank",
-    )(entries)
+    )(lists[0], lengths)
     asked = lax.all_to_all(requests, AXES, 0, 0, tiled=True)
+    table = pl.pallas_call(
+        lambda *refs: project_kernel(frame, *refs),
+        out_shape=full((FEATURES * VIEWS, owned)),
+        compiler_params=limits,
+        cost_estimate=pl.CostEstimate(flops=4000000, bytes_accessed=200000, transcendentals=20000),
+        name="project",
+    )(params, cameras)
     answers = pl.pallas_call(
-        lambda *refs: answer_kernel(frame, *refs),
-        out_shape=full((LANES, 3 * LANES)),
+        answer_kernel,
+        out_shape=full((3 * LANES, LANES)),
         compiler_params=limits,
         name="answer",
-    )(params, cameras, asked)
-    rows = lax.all_to_all(answers, AXES, 0, 0, tiled=True)
-    row_grads = tiles_call(entries, rank, rows, target[0], owned)
-    shares = lax.all_to_all(row_grads, AXES, 0, 0, tiled=True)
+    )(table, asked)
+    rows = sent(answers)
+    hot, column = pl.pallas_call(
+        lambda *refs: prepare_kernel(owned, *refs),
+        out_shape=(full((2 * LANES, entry_count), bf16),) * 2,
+        compiler_params=limits,
+        cost_estimate=pl.CostEstimate(flops=4000000, bytes_accessed=4200000, transcendentals=0),
+        name="prepare",
+    )(entries, rank, asked)
+    row_grads = tiles_call(entries, rank, hot, rows, target[0].transpose(1, 0, 2), owned)
+    shares = sent(row_grads)
+    whole = pl.BlockSpec(memory_space=pltpu.VMEM)
+    away = pl.BlockSpec(memory_space=pl.ANY)
     return pl.pallas_call(
         lambda *refs: update_kernel(frame, *refs),
         out_shape=(full(params.shape),) * 3,
+        in_specs=[whole, away, away, whole, whole, whole, whole],
         scratch_shapes=[
-            pltpu.VMEM((4 * LANES, LANES), f32),
+            pltpu.VMEM((7 * LANES, LANES), f32),
+            pltpu.VMEM((2 * LANES, SLOTS * LANES), bf16),
             pltpu.VMEM((VIEWS * 16 * (owned // LANES), LANES), f32),
             pltpu.VMEM((64, owned), f32),
+            pltpu.VMEM(params.shape, f32),
+            pltpu.VMEM(params.shape, f32),
+            pltpu.SemaphoreType.DMA((2,)),
         ],
         compiler_params=limits,
         name="update",
-    )(params, first_moment, second_moment, cameras, asked, shares, jnp.asarray(learning))
+    )(params, first_moment, second_moment, cameras, asked, column, shares)
 
 
 def solution(mesh):

time: 76.2 us -> 72 us (0.945)
  blocking collectives: 35.5 us -> 14.7 us
  starting transfers between devices: 4.62 us -> 16.1 us
  waiting for transfers between devices: 10.3 us -> 15.4 us
  local copies, waits for them, and re-layouts: 3.83 us -> 5.28 us
    all_to_all x2 -> x1, blocking collectives: 35.5 us -> 14.7 us  [sent(): lax.all_to_all(rows.reshape(LANES, 3 * LANES), AXES, 0, 0, tiled=True)]
    all_to_all x1 -> x2, starting transfers between devices: 4.62 us -> 16.1 us  [the longest x1 11.5 us: per_device(): asked = lax.all_to_all(requests, AXES, 0, 0, tiled=True)]
    all_to_all x1 -> x2, waiting for transfers between devices: 10.3 us -> 15.4 us  [the longest x1 7.92 us: sent(): lax.all_to_all(rows.reshape(LANES, 3 * LANES), AXES, 0, 0, tiled=True)]
    unnamed x18 -> x22, local copies, waits for them, and re-layouts: 1.68 us -> 5.28 us
    pallas_call x1, Pallas kernels: 13.1 us -> 10.6 us  [tiles_call(): pl.pallas_call(lambda *refs: tile_kernel(owned, *refs), out_shape=jax.Sha...]
    pallas_call x1 -> x3, Pallas kernels: 1.83 us -> 3.89 us  [the longest x1 2.48 us: per_device(): pl.pallas_call(answer_kernel, out_shape=full((3 * LANES, LANES)), compile...]
    all_to_all x2 -> x0, local copies, waits for them, and re-layouts: 1.08 us -> none  [the longest x1 0.88 us: per_device(): rows = lax.all_to_all(answers, AXES, 0, 0, tiled=True)]
    squeeze x1 -> x0, local copies, waits for them, and re-layouts: 0.84 us -> none  [per_device(): entries = lists[0] + jnp.where(dead, owned * LANES, 0)]
  transfers between devices with their start and end apart: 1 -> 2, of which waited for: 1 -> 2; matrix products, arithmetic and copies ran while one was open for 0% -> 0% of each run, Pallas kernels for 0% -> 2%
where the time goes in v3:
time: 72 us; the launch traced here: 71.7 us
  Pallas kernels  19.5 us (27%)
  starting transfers between devices  16.1 us (22%)
  waiting for transfers between devices  15.4 us (21%)
  blocking collectives  14.7 us (20%)
  local copies, waits for them, and re-layouts  5.28 us (7%)
  between operations  0.73 us (1%)
    all_to_all x1, blocking collectives, sent(): lax.all_to_all(rows.reshape(LANES, 3 * LANES), AXES, 0, 0, tiled=True)  14.7 us
    all_to_all x1, starting transfers between devices, per_device(): asked = lax.all_to_all(requests, AXES, 0, 0, tiled=True)  11.5 us
    pallas_call x1, Pallas kernels, tiles_call(): pl.pallas_call(lambda *refs: tile_kernel(owned, *refs), out_shape=jax.Sha...  10.6 us
    all_to_all x1, waiting for transfers between devices, sent(): lax.all_to_all(rows.reshape(LANES, 3 * LANES), AXES, 0, 0, tiled=True)  7.92 us
    all_to_all x1, waiting for transfers between devices, per_device(): asked = lax.all_to_all(requests, AXES, 0, 0, tiled=True)  7.52 us
    unnamed x22, local copies, waits for them, and re-layouts  5.28 us
    all_to_all x1, starting transfers between devices, sent(): lax.all_to_all(rows.reshape(LANES, 3 * LANES), AXES, 0, 0, tiled=True)  4.62 us
    pallas_call x1, Pallas kernels, per_device(): pl.pallas_call(lambda *refs: update_kernel(frame, *refs), out_shape=(full...  2.86 us
  transfers between devices with their start and end apart: 2, of which 2 were waited for; matrix products, arithmetic and copies ran while one was open for 0% of the time, Pallas kernels for 2%

profile of v3, /device:TPU:1, one launch (start us, length us, event | category | flops | bytes accessed | tf_op | source)
XLA Modules:
  0.0 71.7 jit_solution(8656851480166162347)
XLA Ops:
  0.6 0.0 copy-start.3
  0.6 0.0 copy-start.7
  0.7 0.7 %copy-done.7 = s32[1,16,256]{2,1,0:T(8,128)S(1)} copy-done((s32[1,16,256]{2,1,0:T(8,128)S(1)}, s32[1,16,256]{2,1,0:T(8,128)}, u32[]{:S(2)}) %copy-start.7) | copy-done | bytes 16408
  1.4 0.7 copy-done.10
  2.1 2.1 %rank.1 = (s32[32,128]{1,0:T(8,128)S(1)}, s32[32,128]{1,0:T(8,128)S(1)}, f32[128,32]{1,0:T(8,128)}) custom-call(s32[16,256]{1,0:T(8,128)S(1)} %bitcast.19, s32[1,16]{1,0:T(1,128)S(1)} %copy-done.10), custom_call_target="tpu_custom_call" | custom-call | tf_op jit(solution)/shard_map/rank/pallas_call | solution.py:751
  4.1 11.5 %all-to-all-start = ((f32[128,1,32]{2,1,0:T(1,128)}), f32[128,1,32]{2,1,0:T(1,128)S(1)}, u32[]{:S(2)}, u32[]{:S(2)}) async-start(f32[128,1,32]{2,1,0:T(1,128)} %bitcast.2), calls=%async_computation | async-start | bytes 131072 | tf_op jit(solution)/shard_map/all_to_all | solution.py:761
  15.6 0.0 copy-start.2
  15.6 0.9 %copy-done.2 = f32[59,512]{1,0:T(8,128)S(1)} copy-done((f32[59,512]{1,0:T(8,128)S(1)}, f32[59,512]{1,0:T(8,128)}, u32[]{:S(2)}) %copy-start.2) | copy-done | bytes 120856
  16.5 0.7 copy-done.8
  17.2 0.3 project.1.table_ref
  17.5 7.5 %all-to-all-done = f32[128,1,32]{2,1,0:T(1,128)S(1)} async-done(((f32[128,1,32]{2,1,0:T(1,128)}), f32[128,1,32]{2,1,0:T(1,128)S(1)}, u32[]{:S(2)}, u32[]{:S(2)}) %all-to-all-start) | async-done | bytes 16416 | tf_op jit(solution)/shard_map/all_to_all | solution.py:761
  25.1 2.5 %answer.1 = f32[384,128]{1,0:T(8,128)} custom-call(f32[36,512]{1,0:T(8,128)S(1)} %project.1.table_ref, f32[128,32]{1,0:T(8,128)S(1)} %bitcast.12), custom_call_target="tpu_custom_call" | custom-call | tf_op jit(solution)/shard_map/answer/pallas_call | solution.py:769
  27.5 4.6 %all-to-all-start.1 = ((f32[128,1,384]{2,1,0:T(1,128)}), f32[128,1,384]{2,1,0:T(1,128)S(1)}, u32[]{:S(2)}, u32[]{:S(2)}) async-start(f32[128,1,384]{2,1,0:T(1,128)} %bitcast.4), calls=%async_computation.1 | async-start | bytes 393216 | tf_op jit(solution)/shard_map/all_to_all | solution.py:748
  32.2 1.1 %prepare.1 = (bf16[256,4096]{1,0:T(8,128)(2,1)S(1)}, bf16[256,4096]{1,0:T(8,128)(2,1)S(1)}) custom-call(s32[32,128]{1,0:T(8,128)S(1)} %get-tuple-element.9.refs_0_, s32[32,128]{1,0:T(8,128)S(1)} %get-tuple-element.10.refs_1_, f32[128,32]{1,0:T(8,128)S(1)} %bitcast.13), custom_call_target="tpu_custom_call" | custom-call | flops 4000000 | bytes 4200000 | tf_op jit(solution)/shard_map/prepare/pallas_call | solution.py:776
  33.3 0.0 copy-start
  33.3 1.3 %copy-done = bf16[256,4096]{1,0:T(8,128)(2,1)} copy-done((bf16[256,4096]{1,0:T(8,128)(2,1)}, bf16[256,4096]{1,0:T(8,128)(2,1)S(1)}, u32[]{:S(2)}) %copy-start) | copy-done | bytes 2097176
  34.6 7.9 %all-to-all-done.1 = f32[128,1,384]{2,1,0:T(1,128)S(1)} async-done(((f32[128,1,384]{2,1,0:T(1,128)}), f32[128,1,384]{2,1,0:T(1,128)S(1)}, u32[]{:S(2)}, u32[]{:S(2)}) %all-to-all-start.1) | async-done | bytes 196640 | tf_op jit(solution)/shard_map/all_to_all | solution.py:748
  42.5 0.9 %copy-done.6 = f32[1,16,3,256]{3,1,2,0:T(8,128)S(1)} copy-done((f32[1,16,3,256]{3,1,2,0:T(8,128)S(1)}, f32[1,16,3,256]{3,1,2,0:T(8,128)}, u32[]{:S(2)}) %copy-start.6) | copy-done | bytes 49176
  43.5 10.6 %tiles.1 = f32[384,128]{1,0:T(8,128)S(1)} custom-call(s32[32,128]{1,0:T(8,128)S(1)} %get-tuple-element.9.refs_0_, s32[32,128]{1,0:T(8,128)S(1)} %get-tuple-element.10.refs_1_, bf16[256,4096]{1,0:T(8,128)(2,1)S(1)} %get-tuple-element.12.refs_2_, f32[384,128]{1,0:T(8,128)S(1)} %bitcast.15, f32[3,16,256]{2,1,0:T(8,128)S(1)} %bitcast.18), custom_call_target="tpu_custom_call" | custom-call | tf_op jit(solution)/shard_map/tiles/pallas_call | solution.py:617
  54.1 14.7 %all_to_all.29 = f32[128,1,384]{2,1,0:T(1,128)S(1)} all-to-all(f32[128,1,384]{2,1,0:T(1,128)S(1)} %bitcast.17), channel_id=1, replica_groups=mesh['views'=4,'tiles'=32] {'views','tiles'}, dimensions={0} | all-to-all | bytes 393216 | tf_op jit(solution)/shard_map/all_to_all | solution.py:748
  68.8 0.0 copy-done.3
  68.8 0.0 copy-done.9
  68.8 0.0 copy-done.4
  68.9 2.9 %update.1 = (f32[59,512]{1,0:T(8,128)}, f32[59,512]{1,0:T(8,128)}, f32[59,512]{1,0:T(8,128)}) custom-call(f32[59,512]{1,0:T(8,128)S(1)} %copy-done.3, f32[59,512]{1,0:T(8,128)S(1)} %copy-done.4, f32[59,512]{1,0:T(8,128)S(1)} %copy-done.5, f32[4,6]{1,0:T(4,128)S(1)} %copy-done.9, f32[128,32]{1,0:T(8,128)S(1)} %bitcast.14, bf16[256,4096]{1,0:T(8,128)(2,1)S(1)} %copy-done.1, ...), custom_call_target="tpu_custom_call" | custom-call | tf_op jit(solution)/shard_map/update/pallas_call | solution.py:787
  (9 shorter events, 0.0 us)
Async XLA Ops:
  0.6 68.2 %copy-start.3 = (f32[59,512]{1,0:T(8,128)S(1)}, f32[59,512]{1,0:T(8,128)}, u32[]{:S(2)}) copy-start(f32[59,512]{1,0:T(8,128)} %refs_0_.3) | copy-start | bytes 362500
  0.6 0.8 %copy-start.7 = (s32[1,16,256]{2,1,0:T(8,128)S(1)}, s32[1,16,256]{2,1,0:T(8,128)}, u32[]{:S(2)}) copy-start(s32[1,16,256]{2,1,0:T(8,128)} %param.12) | copy-start | bytes 49156
  1.4 0.7 copy-start.10
  2.1 66.8 %copy-start.9 = (f32[4,6]{1,0:T(4,128)S(1)}, f32[4,6]{1,0:T(4,128)}, u32[]{:S(2)}) copy-start(f32[4,6]{1,0:T(4,128)} %refs_3_.1) | copy-start | bytes 292
  4.1 20.9 %all-to-all-start = ((f32[128,1,32]{2,1,0:T(1,128)}), f32[128,1,32]{2,1,0:T(1,128)S(1)}, u32[]{:S(2)}, u32[]{:S(2)}) async-start(f32[128,1,32]{2,1,0:T(1,128)} %bitcast.2), calls=%async_computation | async-start | bytes 131072 | tf_op jit(solution)/shard_map/all_to_all | solution.py:761
  15.6 0.9 %copy-start.2 = (f32[59,512]{1,0:T(8,128)S(1)}, f32[59,512]{1,0:T(8,128)}, u32[]{:S(2)}) copy-start(f32[59,512]{1,0:T(8,128)} %refs_0_.3) | copy-start | bytes 362500
  16.5 0.7 copy-start.8
  17.2 51.6 %copy-start.4 = (f32[59,512]{1,0:T(8,128)S(1)}, f32[59,512]{1,0:T(8,128)}, u32[]{:S(2)}) copy-start(f32[59,512]{1,0:T(8,128)} %refs_1_.5) | copy-start | bytes 362500
  17.2 51.6 %copy-start.5 = (f32[59,512]{1,0:T(8,128)S(1)}, f32[59,512]{1,0:T(8,128)}, u32[]{:S(2)}) copy-start(f32[59,512]{1,0:T(8,128)} %refs_2_.1) | copy-start | bytes 362500
  27.5 15.0 %all-to-all-start.1 = ((f32[128,1,384]{2,1,0:T(1,128)}), f32[128,1,384]{2,1,0:T(1,128)S(1)}, u32[]{:S(2)}, u32[]{:S(2)}) async-start(f32[128,1,384]{2,1,0:T(1,128)} %bitcast.4), calls=%async_computation.1 | async-start | bytes 393216 | tf_op jit(solution)/shard_map/all_to_all | solution.py:748
  33.3 1.3 %copy-start = (bf16[256,4096]{1,0:T(8,128)(2,1)}, bf16[256,4096]{1,0:T(8,128)(2,1)S(1)}, u32[]{:S(2)}) copy-start(bf16[256,4096]{1,0:T(8,128)(2,1)S(1)} %get-tuple-element.11.refs_5_) | copy-start | bytes 6291460
  42.5 26.3 %copy-start.1 = (bf16[256,4096]{1,0:T(8,128)(2,1)S(1)}, bf16[256,4096]{1,0:T(8,128)(2,1)}, u32[]{:S(2)}) copy-start(bf16[256,4096]{1,0:T(8,128)(2,1)} %copy-done) | copy-start | bytes 6291460
  42.5 0.9 %copy-start.6 = (f32[1,16,3,256]{3,1,2,0:T(8,128)S(1)}, f32[1,16,3,256]{3,1,2,0:T(8,128)}, u32[]{:S(2)}) copy-start(f32[1,16,3,256]{3,1,2,0:T(8,128)} %param.11) | copy-start | bytes 147460

commit v4 on v3

--- a/solution.py
+++ b/solution.py
@@ -13,7 +13,10 @@
 VIEWS = 4
 SLOTS = 32
 HALF = SLOTS // 2
-BLOCK = 8
+KEYS = 2 * VIEWS
+PARAMS = 59
+TABLE = 80
+BLOCK = 4
 FEATURES = 9
 AXES = ("views", "tiles")
 
@@ -170,17 +173,32 @@
     ]
 
 
-def camera_terms(cameras_ref, owned):
+def both_halves(upper, lower):
+    return jnp.concatenate([upper, lower], axis=0)
+
+
+def camera_terms(cameras_ref, half):
     cameras = cameras_ref[...]
     cos, sin = jnp.cos(cameras), jnp.sin(cameras)
 
     def column(values, at):
-        return jnp.broadcast_to(values[:, at : at + 1], (VIEWS, owned))
+        values = values[:, at : at + 1]
+        return jnp.broadcast_to(both_halves(values, values), (KEYS, half))
 
     rotation = rotation_entries(
         [column(cos, at) for at in range(3)], [column(sin, at) for at in range(3)]
     )
     return rotation, [column(cameras, 3 + at) for at in range(3)]
+
+
+def spread_params(params_ref, half):
+    return [
+        both_halves(
+            jnp.broadcast_to(params_ref[at : at + 1, :half], (VIEWS, half)),
+            jnp.broadcast_to(params_ref[at : at + 1, half:], (VIEWS, half)),
+        )
+        for at in range(PARAMS)
+    ]
 
 
 def iota(shape, dim):
@@ -214,22 +232,15 @@
 
 
 def rank_kernel(
-    owned, lists_ref, lengths_ref, entries_ref, rank_ref, request_ref, hot_ref, wanted_ref
+    owned, lists_ref, entries_ref, rank_ref, request_ref, hot_ref, wanted_ref
 ):
     chunks = entries_ref.shape[0]
     per_group = chunks // 2
     steps = LANES // GROUP
-    lengths = jnp.concatenate(
-        [lengths_ref[...], jnp.zeros((1, LANES - lengths_ref.shape[1]), i32)], axis=1
-    )
-    lengths = jnp.broadcast_to(lengths, (GROUP, LANES))
     lane = iota((GROUP, LANES), 1)
     tile = lax.rem(lane, GROUP)
     spot = iota((GROUP, LANES), 0) * steps + lax.div(lane, GROUP)
     for group in range(2):
-        length = jnp.take_along_axis(
-            lengths, group * GROUP + tile, axis=1, mode="promise_in_bounds"
-        )
         for half in range(per_group // GROUP):
             made = jnp.zeros((GROUP, LANES), i32)
             for at in range(GROUP):
@@ -239,11 +250,10 @@
                 )
                 found = jnp.take_along_axis(source, spot, axis=1, mode="promise_in_bounds")
                 made = jnp.where(tile == at, found, made)
-            dead = spot + half * LANES >= length
             row = group * per_group + half * GROUP
-            entries_ref[row : row + GROUP, :] = jnp.where(dead, made + owned * LANES, made)
+            entries_ref[row : row + GROUP, :] = made
     entries = entries_ref[...]
-    owner = lax.rem(lax.div(entries, owned), LANES)
+    owner = lax.div(entries, owned)
     owner_row = owner.astype(f32)
     column = lax.rem(entries, owned)
     low = lax.rem(column, 256).astype(f32)
@@ -285,11 +295,17 @@
 
 
 def project_kernel(frame, params_ref, cameras_ref, table_ref):
-    owned = params_ref.shape[1]
-    rotation, shift = camera_terms(cameras_ref, owned)
-    params = [jnp.broadcast_to(params_ref[at : at + 1, :], (VIEWS, owned)) for at in range(59)]
-    for at, values in enumerate(project(params, rotation, shift, *frame)):
-        table_ref[at * VIEWS : (at + 1) * VIEWS, :] = values
+    half = params_ref.shape[1] // 2
+    rotation, shift = camera_terms(cameras_ref, half)
+    rows = project(spread_params(params_ref, half), rotation, shift, *frame)
+    rows.append(jnp.zeros((TABLE - FEATURES * KEYS, half), f32))
+    for part, values in enumerate(pieces(jnp.concatenate(rows, axis=0), 3)):
+        table_ref[part * TABLE : (part + 1) * TABLE, :] = values
+
+
+def request_keys(asked):
+    half = 2 * LANES
+    return lax.div(asked, half) * VIEWS + lax.div(iota(asked.shape, 1), LANES // VIEWS)
 
 
 def spread_rows(stack, out_ref):
@@ -303,49 +319,84 @@
     )
 
 
-def answer_kernel(table_ref, asked_ref, rows_ref):
-    owned = table_ref.shape[1]
+def pick_sublane(values, row):
+    index = jnp.broadcast_to(row, (8, values.shape[1]))
+    return jnp.take_along_axis(values, index, axis=0, mode="promise_in_bounds")
+
+
+def fill_columns(asked, column_ref):
+    low = lax.rem(asked, 2 * LANES).astype(f32)
+    ids = small_ids(2 * LANES)
+    for at in range(SLOTS):
+        column_ref[:, at * LANES : (at + 1) * LANES] = one_hot(ids, low[at : at + 1, :])
+
+
+def answer_kernel(table_ref, asked_ref, rows_ref, column_ref, stack_ref):
     asked = flipped_requests(asked_ref)
-    chunk_of = lax.div(asked, LANES)
-    lane_of = lax.rem(asked, LANES)
-    view_of = lax.div(iota((SLOTS, LANES), 1), LANES // VIEWS)
-    chosen = [jnp.zeros((SLOTS, LANES), f32) for _ in range(FEATURES)]
-    for view in range(VIEWS):
-        for chunk in range(owned // LANES):
-            mask = (view_of == view) & (chunk_of == chunk)
-            for at in range(FEATURES):
-                row = at * VIEWS + view
-                source = jnp.broadcast_to(
-                    table_ref[row : row + 1, chunk * LANES : (chunk + 1) * LANES], (SLOTS, LANES)
-                )
-                found = jnp.take_along_axis(source, lane_of, axis=1, mode="promise_in_bounds")
-                chosen[at] = jnp.where(mask, found, chosen[at])
-    stack = [
-        chosen[at][half * HALF : (half + 1) * HALF] for half in range(2) for at in range(FEATURES)
-    ]
-    stack.append(jnp.zeros((3 * LANES - SLOTS * FEATURES, LANES), f32))
-    spread_rows(jnp.concatenate(stack, axis=0), rows_ref)
-
-
-def prepare_kernel(owned, entries_ref, rank_ref, asked_ref, hot_ref, column_ref):
+    key = request_keys(asked)
+    fill_columns(asked, column_ref)
+    table = table_ref[...]
+    for at in range(0, SLOTS, 2):
+        found = dot(table, column_ref[:, at * LANES : (at + 2) * LANES], 1, 0)
+        found = found[:TABLE] + (found[TABLE : 2 * TABLE] + found[2 * TABLE :])
+        for side in range(2):
+            slot = at + side
+            for feature in range(FEATURES):
+                row = slot // HALF * FEATURES * HALF + feature * HALF + slot % HALF
+                stack_ref[row : row + 1, :] = pick_sublane(
+                    found[feature * KEYS : (feature + 1) * KEYS, side * LANES : (side + 1) * LANES],
+                    key[slot : slot + 1, :],
+                )[:1, :]
+    stack_ref[SLOTS * FEATURES :, :] = jnp.zeros((3 * LANES - SLOTS * FEATURES, LANES), f32)
+    spread_rows(stack_ref[...], rows_ref)
+
+
+def prepare_kernel(
+    owned,
+    entries_ref,
+    rank_ref,
+    lengths_ref,
+    target_ref,
+    first_ref,
+    second_ref,
+    asked_ref,
+    hot_ref,
+    column_ref,
+    live_ref,
+    aim_ref,
+    old_first_ref,
+    old_second_ref,
+):
+    fill_columns(flipped_requests(asked_ref), column_ref)
+    old_first_ref[...] = beta_one * first_ref[...]
+    old_second_ref[...] = beta_two * second_ref[...]
     ids = small_ids(2 * LANES)
     place, _ = slot_columns(entries_ref[...], rank_ref[...], owned)
     place = place.astype(f32)
     for at in range(entries_ref.shape[0]):
         hot_ref[:, at * LANES : (at + 1) * LANES] = one_hot(ids, place[at : at + 1, :])
-    low = lax.rem(flipped_requests(asked_ref), 2 * LANES).astype(f32)
-    for at in range(SLOTS):
-        column_ref[:, at * LANES : (at + 1) * LANES] = one_hot(ids, low[at : at + 1, :])
+    lengths = jnp.concatenate(
+        [lengths_ref[...], jnp.zeros((1, LANES - lengths_ref.shape[1]), i32)], axis=1
+    )
+    shape = entries_ref.shape
+    per_group = shape[0] // 2
+    tile = lax.div(iota(shape, 0), per_group) * GROUP + lax.rem(iota(shape, 1), GROUP)
+    length = jnp.take_along_axis(
+        jnp.broadcast_to(lengths, shape), tile, axis=1, mode="promise_in_bounds"
+    )
+    steps = LANES // GROUP
+    spot = lax.rem(iota(shape, 0), per_group) * steps + lax.div(iota(shape, 1), GROUP)
+    live_ref[...] = jnp.where(spot < length, 1, 0)
+    aim_ref[...] = target_ref[...]
 
 
 def slot_columns(entries, rank, owned):
-    owner = lax.rem(lax.div(entries, owned), LANES)
+    owner = lax.div(entries, owned)
     return lax.div(rank, HALF) * LANES + owner, lax.rem(rank, HALF)
 
 
 def tile_kernel(
-    owned,
-    entries_ref,
+    live_ref,
     rank_ref,
     hot_ref,
     rows_ref,
@@ -365,7 +416,7 @@
     spread_ref,
     paint_ref,
 ):
-    chunks = entries_ref.shape[0]
+    chunks = live_ref.shape[0]
     groups = 2
     per_group = chunks // groups
     pixels = TILE_SIDE * TILE_SIDE
@@ -373,9 +424,8 @@
     span = FEATURES * HALF
     first_tile = lax.axis_index("tiles") * (groups * GROUP)
 
-    entries = entries_ref[...]
-    live = entries < owned * LANES
-    _, below = slot_columns(entries, rank_ref[...], owned)
+    live = live_ref[...] > 0
+    below = lax.rem(rank_ref[...], HALF)
 
     flipped = gathered_rows(rows_ref)
     table = jnp.concatenate([flipped[:span], flipped[span : 2 * span]], axis=1)
@@ -384,15 +434,12 @@
         found = dot(table, hot_ref[:, at * LANES : (at + 2) * LANES], 1, 0)
         found = found[:span] + (found[span : 2 * span] + found[2 * span :])
         for side in range(2):
-            row = jnp.broadcast_to(below[at + side : at + side + 1, :], (8, LANES))
-            index, upper = lax.rem(row, 8), row >= 8
+            row = below[at + side : at + side + 1, :]
+            index, upper = lax.rem(row, 8), jnp.broadcast_to(row, (8, LANES)) >= 8
             for feature in range(FEATURES):
                 first, second = [
-                    jnp.take_along_axis(
-                        found[part : part + 8, side * LANES : (side + 1) * LANES],
-                        index,
-                        axis=0,
-                        mode="promise_in_bounds",
+                    pick_sublane(
+                        found[part : part + 8, side * LANES : (side + 1) * LANES], index
                     )
                     for part in (feature * HALF, feature * HALF + 8)
                 ]
@@ -448,16 +495,19 @@
         paint_ref[:, at * LANES : (at + 1) * LANES] = jnp.concatenate(rows, axis=0).astype(bf16)
 
     def rows_of(chunk, count=1):
-        return pl.ds(pl.multiple_of(chunk * LANES, LANES), count * LANES)
-
-    def shade(at, carry):
-        coef = jnp.concatenate(
-            [coef_ref[pl.ds(at * BLOCK + off, 24, stride=chunks), :] for off in range(BLOCK)], axis=1
-        )
-        alpha_ref[rows_of(at * BLOCK, BLOCK), :] = jnp.exp2(dot(coef.astype(bf16), base_three, 0, 0))
-        return carry
-
-    lax.fori_loop(0, chunks // BLOCK, shade, 0)
+        return slice(chunk * LANES, (chunk + count) * LANES)
+
+    blocks = per_group // BLOCK
+
+    def shade(at):
+        for group in range(groups):
+            chunk = group * per_group + at * BLOCK
+            coef = jnp.concatenate(
+                [coef_ref[pl.ds(chunk + off, 24, stride=chunks), :] for off in range(BLOCK)], axis=1
+            )
+            alpha_ref[rows_of(chunk, BLOCK), :] = jnp.exp2(
+                dot(coef.astype(bf16), base_three, 0, 0)
+            )
 
     def load(ref, at):
         return [ref[rows_of(group * per_group + at), :] for group in range(groups)]
@@ -483,8 +533,6 @@
         keep((weight_ref, high_ref, middle_ref, low_ref), at, made)
         return tuple(out)
 
-    lax.fori_loop(0, per_group, weigh, (jnp.ones((GROUP, pixels), f32),) * groups)
-
     def blend(at, renders):
         out = []
         for group in range(groups):
@@ -500,9 +548,15 @@
             )
         return tuple(out)
 
-    renders = lax.fori_loop(
-        0, per_group // BLOCK, blend, (jnp.zeros((72, pixels), f32),) * groups
-    )
+    clears = (jnp.ones((GROUP, pixels), f32),) * groups
+    renders = (jnp.zeros((72, pixels), f32),) * groups
+    shade(0)
+    for block in range(blocks):
+        if block + 1 < blocks:
+            shade(block + 1)
+        for at in range(block * BLOCK, (block + 1) * BLOCK):
+            clears = weigh(at, clears)
+        renders = blend(block, renders)
 
     signs, sign_twos = [], []
     for group in range(groups):
@@ -519,16 +573,12 @@
         signs.append(sign.astype(bf16))
         sign_twos.append(jnp.concatenate([sign, sign], axis=0).astype(bf16))
 
-    def draw(at, carry):
+    def draw(at):
         for group in range(groups):
             rows = rows_of(group * per_group + at * BLOCK, BLOCK)
             pull_ref[rows, :] = dot(paint_ref[:48, rows], sign_twos[group], 0, 0)
-        return carry
-
-    lax.fori_loop(0, per_group // BLOCK, draw, 0)
-
-    def unweigh(back, behinds):
-        at = per_group - 1 - back
+
+    def unweigh(at, behinds):
         pulls, alphas, weights = [load(ref, at) for ref in (pull_ref, alpha_ref, weight_ref)]
         out, made = [], []
         for group in range(groups):
@@ -545,9 +595,7 @@
         keep((low_ref, spread_ref), at, made)
         return tuple(out)
 
-    lax.fori_loop(0, per_group, unweigh, (jnp.zeros((GROUP, pixels), f32),) * groups)
-
-    def total(at, carry):
+    def total(at):
         for group in range(groups):
             chunk = group * per_group + at * BLOCK
             rows = rows_of(chunk, BLOCK)
@@ -555,7 +603,7 @@
             moments = dot(base_two, parts, 1, 1)
             by_color = dot(signs[group], high_ref[rows, :], 1, 1)
             for off in range(BLOCK):
-                row = pl.multiple_of((chunk + off) * 16, 16)
+                row = (chunk + off) * 16
                 lanes = slice(off * LANES, (off + 1) * LANES)
                 moment_ref[pl.ds(row, 8), :] = moments[:, lanes]
                 for channel in range(3):
@@ -566,9 +614,15 @@
                         axis=0,
                         keepdims=True,
                     )
-        return carry
-
-    lax.fori_loop(0, per_group // BLOCK, total, 0)
+
+    behinds = (jnp.zeros((GROUP, pixels), f32),) * groups
+    draw(blocks - 1)
+    for block in reversed(range(blocks)):
+        if block:
+            draw(block - 1)
+        for at in reversed(range(block * BLOCK, (block + 1) * BLOCK)):
+            behinds = unweigh(at, behinds)
+        total(block)
 
     sums = [moment_ref[pl.ds(at, chunks, stride=16), :] for at in range(6)]
     sum_x = sums[1] - at_u * sums[0]
@@ -606,8 +660,8 @@
     spread_rows(sent, grads_ref)
 
 
-def tiles_call(entries, rank, hot, rows, target, owned):
-    chunks = entries.shape[0]
+def tiles_call(live, rank, hot, rows, target):
+    chunks = live.shape[0]
     pixels = TILE_SIDE * TILE_SIDE
     count = chunks * LANES
 
@@ -615,7 +669,7 @@
         return pltpu.VMEM((count, pixels), dtype)
 
     return pl.pallas_call(
-        lambda *refs: tile_kernel(owned, *refs),
+        tile_kernel,
         out_shape=jax.ShapeDtypeStruct((3 * LANES, LANES), f32),
         scratch_shapes=[
             pltpu.VMEM((FEATURES * chunks, LANES), f32),
@@ -632,9 +686,9 @@
             plane(bf16),
             pltpu.VMEM((80, count), bf16),
         ],
-        compiler_params=pltpu.CompilerParams(vmem_limit_bytes=48 * 1024 * 1024),
+        compiler_params=pltpu.CompilerParams(vmem_limit_bytes=32 * 1024 * 1024),
         name="tiles",
-    )(entries, rank, hot, rows, target)
+    )(live, rank, hot, rows, target)
 
 
 def learning_rates(shape):
@@ -648,8 +702,8 @@
 def update_kernel(
     frame,
     params_ref,
-    first_hbm,
-    second_hbm,
+    old_first_ref,
+    old_second_ref,
     cameras_ref,
     asked_ref,
     column_ref,
@@ -659,72 +713,44 @@
     new_second_ref,
     source_ref,
     spread_ref,
-    dense_ref,
     gradient_ref,
-    first_ref,
-    second_ref,
-    arrived,
 ):
     owned = params_ref.shape[1]
-    copies = [
-        pltpu.make_async_copy(source, target, arrived.at[at])
-        for at, (source, target) in enumerate(((first_hbm, first_ref), (second_hbm, second_ref)))
-    ]
-    for copy in copies:
-        copy.start()
-    upper = lax.div(flipped_requests(asked_ref), 2 * LANES)
-    key = (lax.div(iota((SLOTS, LANES), 1), LANES // VIEWS) * 2 + upper).astype(f32)
+    half = owned // 2
+    key = request_keys(flipped_requests(asked_ref))
     flipped = gathered_rows(grads_ref)
     for part, values in enumerate(pieces(flipped, 2)):
         source_ref[part * 3 * LANES : (part + 1) * 3 * LANES, :] = values.astype(f32)
-    source_ref[6 * LANES :, :] = jnp.zeros((LANES, LANES), f32)
-    keys = [jnp.full((16, LANES), at, f32).astype(bf16) for at in range(2 * VIEWS)]
+    key_id = iota((KEYS, LANES), 0)
     for slot in range(SLOTS):
         first = slot // HALF * FEATURES * HALF + slot % HALF
-        mine = jnp.broadcast_to(key[slot : slot + 1, :], (16, LANES)).astype(bf16)
-        parts = [
-            source_ref[pl.ds(part * 3 * LANES + first, 16, stride=HALF), :].astype(bf16)
-            for part in range(2)
-        ]
-        spread_ref[:, slot * LANES : (slot + 1) * LANES] = jnp.concatenate(
-            [
-                jnp.where(mine == keys[at], values, jnp.zeros((), bf16))
-                for values in parts
-                for at in range(2 * VIEWS)
-            ],
-            axis=0,
-        )
+        mine = key_id == key[slot : slot + 1, :]
+        rows = []
+        for part in range(2):
+            for feature in range(FEATURES):
+                at = part * 3 * LANES + first + feature * HALF
+                row = jnp.broadcast_to(source_ref[at : at + 1, :], (KEYS, LANES))
+                rows.append(jnp.where(mine, row, 0.0))
+        spread_ref[:, slot * LANES : (slot + 1) * LANES] = jnp.concatenate(rows, axis=0).astype(bf16)
     dense = dot(spread_ref[...], column_ref[...], 1, 1)
-    dense = dense[:LANES] + dense[LANES:]
-    spans = range(owned // LANES)
-    for span in spans:
-        side, lanes = span // 2, slice(span % 2 * LANES, (span % 2 + 1) * LANES)
-        for view in range(VIEWS):
-            row = (view * 2 + side) * 16
-            dense_ref[(span * VIEWS + view) * 16 : (span * VIEWS + view + 1) * 16, :] = dense[
-                row : row + 16, lanes
-            ]
-    cotangents = [
-        jnp.concatenate(
-            [dense_ref[pl.ds(span * VIEWS * 16 + at, VIEWS, stride=16), :] for span in spans], axis=1
-        )
-        for at in range(FEATURES)
-    ]
-
-    rotation, shift = camera_terms(cameras_ref, owned)
-    params = [jnp.broadcast_to(params_ref[at : at + 1, :], (VIEWS, owned)) for at in range(59)]
+    dense = dense[: FEATURES * KEYS] + dense[FEATURES * KEYS :]
+    cotangents = [dense[at * KEYS : (at + 1) * KEYS] for at in range(FEATURES)]
+
+    rotation, shift = camera_terms(cameras_ref, half)
+    params = spread_params(params_ref, half)
     _, pullback = jax.vjp(lambda values: project(values, rotation, shift, *frame), params)
     by_params = pullback(cotangents)[0]
-    for at in range(59):
-        gradient_ref[at : at + 1, :] = jnp.sum(by_params[at], axis=0, keepdims=True)
-    gradient = gradient_ref[:59, :]
-    for copy in copies:
-        copy.wait()
-    new_first = beta_one * first_ref[...] + (1.0 - beta_one) * gradient
-    new_second = beta_two * second_ref[...] + (1.0 - beta_two) * gradient * gradient
+    for at in range(PARAMS):
+        pair = by_params[at] + pltpu.roll(by_params[at], 1, 0)
+        four = pair + pltpu.roll(pair, 2, 0)
+        gradient_ref[at : at + 1, :half] = four[VIEWS - 1 : VIEWS]
+        gradient_ref[at : at + 1, half:] = four[KEYS - 1 :]
+    gradient = gradient_ref[:PARAMS, :]
+    new_first = old_first_ref[...] + (1.0 - beta_one) * gradient
+    new_second = old_second_ref[...] + (1.0 - beta_two) * gradient * gradient
     new_first_ref[...] = new_first
     new_second_ref[...] = new_second
-    step_size = learning_rates((59, owned)) * (new_first / (1.0 - beta_one**ADAM_STEP))
+    step_size = learning_rates((PARAMS, owned)) * (new_first / (1.0 - beta_one**ADAM_STEP))
     new_params_ref[...] = params_ref[...] - step_size / (
         jnp.sqrt(new_second / (1.0 - beta_two**ADAM_STEP)) + adam_eps
     )
@@ -739,7 +765,7 @@
     width = TILE_COLS * TILE_SIDE
     height = tile_dev * lax.axis_size("tiles") // TILE_COLS * TILE_SIDE
     frame = (float(width), 0.5 * width, 0.5 * height)
-    limits = pltpu.CompilerParams(vmem_limit_bytes=48 * 1024 * 1024)
+    limits = pltpu.CompilerParams(vmem_limit_bytes=16 * 1024 * 1024)
 
     def full(shape, dtype=f32):
         return jax.ShapeDtypeStruct(shape, dtype)
@@ -757,49 +783,52 @@
         ],
         compiler_params=limits,
         name="rank",
-    )(lists[0], lengths)
+    )(lists[0])
     asked = lax.all_to_all(requests, AXES, 0, 0, tiled=True)
     table = pl.pallas_call(
         lambda *refs: project_kernel(frame, *refs),
-        out_shape=full((FEATURES * VIEWS, owned)),
+        out_shape=full((3 * TABLE, owned // 2), bf16),
         compiler_params=limits,
         cost_estimate=pl.CostEstimate(flops=4000000, bytes_accessed=200000, transcendentals=20000),
         name="project",
     )(params, cameras)
+    columns = (owned // 2, SLOTS * LANES)
     answers = pl.pallas_call(
         answer_kernel,
         out_shape=full((3 * LANES, LANES)),
+        scratch_shapes=[pltpu.VMEM(columns, bf16), pltpu.VMEM((3 * LANES, LANES), f32)],
         compiler_params=limits,
         name="answer",
     )(table, asked)
     rows = sent(answers)
-    hot, column = pl.pallas_call(
+    aim = target[0].transpose(1, 0, 2)
+    hot, column, live, aim, old_first, old_second = pl.pallas_call(
         lambda *refs: prepare_kernel(owned, *refs),
-        out_shape=(full((2 * LANES, entry_count), bf16),) * 2,
+        out_shape=(
+            full((2 * LANES, entry_count), bf16),
+            full(columns, bf16),
+            full((chunks, LANES), i32),
+            full(aim.shape),
+            full(params.shape),
+            full(params.shape),
+        ),
         compiler_params=limits,
-        cost_estimate=pl.CostEstimate(flops=4000000, bytes_accessed=4200000, transcendentals=0),
+        cost_estimate=pl.CostEstimate(flops=4000000, bytes_accessed=2200000, transcendentals=0),
         name="prepare",
-    )(entries, rank, asked)
-    row_grads = tiles_call(entries, rank, hot, rows, target[0].transpose(1, 0, 2), owned)
+    )(entries, rank, lengths, aim, first_moment, second_moment, asked)
+    row_grads = tiles_call(live, rank, hot, rows, aim)
     shares = sent(row_grads)
-    whole = pl.BlockSpec(memory_space=pltpu.VMEM)
-    away = pl.BlockSpec(memory_space=pl.ANY)
     return pl.pallas_call(
         lambda *refs: update_kernel(frame, *refs),
         out_shape=(full(params.shape),) * 3,
-        in_specs=[whole, away, away, whole, whole, whole, whole],
         scratch_shapes=[
-            pltpu.VMEM((7 * LANES, LANES), f32),
-            pltpu.VMEM((2 * LANES, SLOTS * LANES), bf16),
-            pltpu.VMEM((VIEWS * 16 * (owned // LANES), LANES), f32),
+            pltpu.VMEM((6 * LANES, LANES), f32),
+            pltpu.VMEM((2 * FEATURES * KEYS, SLOTS * LANES), bf16),
             pltpu.VMEM((64, owned), f32),
-            pltpu.VMEM(params.shape, f32),
-            pltpu.VMEM(params.shape, f32),
-            pltpu.SemaphoreType.DMA((2,)),
         ],
         compiler_params=limits,
         name="update",
-    )(params, first_moment, second_moment, cameras, asked, column, shares)
+    )(params, old_first, old_second, cameras, asked, column, shares)
 
 
 def solution(mesh):

time: 72 us -> 65.9 us (0.915)
  Pallas kernels: 19.5 us -> 14.2 us
  waiting for transfers between devices: 15.4 us -> 12.2 us
  local copies, waits for them, and re-layouts: 5.28 us -> 6.89 us
    pallas_call x2, Pallas kernels: 13.1 us -> 8.77 us  [the longest x1 7.14 us: tiles_call(): pl.pallas_call(tile_kernel, out_shape=jax.ShapeDtypeStruct((3 * LANES, LA...]
    all_to_all x1, waiting for transfers between devices: 7.92 us -> 4.61 us  [sent(): lax.all_to_all(rows.reshape(LANES, 3 * LANES), AXES, 0, 0, tiled=True)]
    unnamed x22, local copies, waits for them, and re-layouts: 5.28 us -> 6.89 us
    pallas_call x1, Pallas kernels: 2.86 us -> 1.98 us  [per_device(): pl.pallas_call(lambda *refs: update_kernel(frame, *refs), out_shape=(full...]
where the time goes in v4:
time: 65.9 us; the launch traced here: 65.5 us
  starting transfers between devices  16.1 us (24%)
  blocking collectives  15.4 us (23%)
  Pallas kernels  14.2 us (22%)
  waiting for transfers between devices  12.2 us (19%)
  local copies, waits for them, and re-layouts  6.89 us (10%)
  between operations  0.73 us (1%)
    all_to_all x1, blocking collectives, sent(): lax.all_to_all(rows.reshape(LANES, 3 * LANES), AXES, 0, 0, tiled=True)  15.4 us
    all_to_all x1, starting transfers between devices, per_device(): asked = lax.all_to_all(requests, AXES, 0, 0, tiled=True)  11.5 us
    all_to_all x1, waiting for transfers between devices, per_device(): asked = lax.all_to_all(requests, AXES, 0, 0, tiled=True)  7.58 us
    pallas_call x1, Pallas kernels, tiles_call(): pl.pallas_call(tile_kernel, out_shape=jax.ShapeDtypeStruct((3 * LANES, LA...  7.14 us
    unnamed x22, local copies, waits for them, and re-layouts  6.89 us
    all_to_all x1, starting transfers between devices, sent(): lax.all_to_all(rows.reshape(LANES, 3 * LANES), AXES, 0, 0, tiled=True)  4.62 us
    all_to_all x1, waiting for transfers between devices, sent(): lax.all_to_all(rows.reshape(LANES, 3 * LANES), AXES, 0, 0, tiled=True)  4.61 us
    pallas_call x1, Pallas kernels, per_device(): pl.pallas_call(lambda *refs: rank_kernel(owned, *refs), out_shape=(full((...  2.06 us
  transfers between devices with their start and end apart: 2, of which 2 were waited for; matrix products, arithmetic and copies ran while one was open for 0% of the time, Pallas kernels for 2%

profile of v4, /device:TPU:1, one launch (start us, length us, event | category | flops | bytes accessed | tf_op | source)
XLA Modules:
  0.0 65.5 jit_solution(12762447052147872950)
XLA Ops:
  0.6 0.7 %copy-done.7 = s32[1,16,256]{2,1,0:T(8,128)S(1)} copy-done((s32[1,16,256]{2,1,0:T(8,128)S(1)}, s32[1,16,256]{2,1,0:T(8,128)}, u32[]{:S(2)}) %copy-start.7) | copy-done | bytes 16408
  1.3 2.1 %rank.1 = (s32[32,128]{1,0:T(8,128)S(1)}, s32[32,128]{1,0:T(8,128)S(1)}, f32[128,32]{1,0:T(8,128)}) custom-call(s32[16,256]{1,0:T(8,128)S(1)} %bitcast.19), custom_call_target="tpu_custom_call" | custom-call | tf_op jit(solution)/shard_map/rank/pallas_call | solution.py:777
  3.4 11.5 %all-to-all-start = ((f32[128,1,32]{2,1,0:T(1,128)}), f32[128,1,32]{2,1,0:T(1,128)S(1)}, u32[]{:S(2)}, u32[]{:S(2)}) async-start(f32[128,1,32]{2,1,0:T(1,128)} %bitcast.4), calls=%async_computation | async-start | bytes 131072 | tf_op jit(solution)/shard_map/all_to_all | solution.py:787
  14.9 0.0 copy-start.2
  14.9 0.9 %copy-done.2 = f32[59,512]{1,0:T(8,128)S(1)} copy-done((f32[59,512]{1,0:T(8,128)S(1)}, f32[59,512]{1,0:T(8,128)}, u32[]{:S(2)}) %copy-start.2) | copy-done | bytes 120856
  15.8 0.7 %copy-done.8 = f32[4,6]{1,0:T(4,128)S(1)} copy-done((f32[4,6]{1,0:T(4,128)S(1)}, f32[4,6]{1,0:T(4,128)}, u32[]{:S(2)}) %copy-start.8) | copy-done | bytes 120
  16.5 0.2 project.1.table_ref
  16.7 0.0 copy-start.3
  16.7 0.0 copy-start.9
  16.8 7.6 %all-to-all-done = f32[128,1,32]{2,1,0:T(1,128)S(1)} async-done(((f32[128,1,32]{2,1,0:T(1,128)}), f32[128,1,32]{2,1,0:T(1,128)S(1)}, u32[]{:S(2)}, u32[]{:S(2)}) %all-to-all-start) | async-done | bytes 16416 | tf_op jit(solution)/shard_map/all_to_all | solution.py:787
  24.3 1.6 %answer.1 = f32[384,128]{1,0:T(8,128)} custom-call(bf16[240,256]{1,0:T(8,128)(2,1)S(1)} %project.1.table_ref, f32[128,32]{1,0:T(8,128)S(1)} %bitcast.12), custom_call_target="tpu_custom_call" | custom-call | tf_op jit(solution)/shard_map/answer/pallas_call | solution.py:796
  26.0 4.6 %all-to-all-start.1 = ((f32[128,1,384]{2,1,0:T(1,128)}), f32[128,1,384]{2,1,0:T(1,128)S(1)}, u32[]{:S(2)}, u32[]{:S(2)}) async-start(f32[128,1,384]{2,1,0:T(1,128)} %bitcast.6), calls=%async_computation.1 | async-start | bytes 393216 | tf_op jit(solution)/shard_map/all_to_all | solution.py:774
  30.6 0.0 copy-start.4
  30.6 0.9 %copy-done.4 = f32[59,512]{1,0:T(8,128)S(1)} copy-done((f32[59,512]{1,0:T(8,128)S(1)}, f32[59,512]{1,0:T(8,128)}, u32[]{:S(2)}) %copy-start.4) | copy-done | bytes 120856
  31.5 0.9 %copy-done.5 = f32[59,512]{1,0:T(8,128)S(1)} copy-done((f32[59,512]{1,0:T(8,128)S(1)}, f32[59,512]{1,0:T(8,128)}, u32[]{:S(2)}) %copy-start.5) | copy-done | bytes 120856
  32.4 0.8 %copy-done.6 = f32[1,16,3,256]{3,1,2,0:T(8,128)S(1)} copy-done((f32[1,16,3,256]{3,1,2,0:T(8,128)S(1)}, f32[1,16,3,256]{3,1,2,0:T(8,128)}, u32[]{:S(2)}) %copy-start.6) | copy-done | bytes 49176
  33.2 0.7 copy-done.10
  33.9 1.2 %prepare.1 = (bf16[256,4096]{1,0:T(8,128)(2,1)S(1)}, bf16[256,4096]{1,0:T(8,128)(2,1)S(1)}, s32[32,128]{1,0:T(8,128)S(1)}, f32[3,16,256]{2,1,0:T(8,128)S(1)}, f3...) custom-call(s32[32,128]{1,0:T(8,128)S(1)} %get-tuple-element.12.refs_0_, s32[32,128]{1,0:T(8,128)S(1)} %get-tuple-element.13.refs_1_.rank_ref, ...), custom_call_target="tpu_custom_call" | custom-call | flops 4000000 | bytes 2200000 | tf_op jit(solution)/shard_map/prepare/pallas_call | solution.py:805
  35.0 1.3 %copy-done = bf16[256,4096]{1,0:T(8,128)(2,1)} copy-done((bf16[256,4096]{1,0:T(8,128)(2,1)}, bf16[256,4096]{1,0:T(8,128)(2,1)S(1)}, u32[]{:S(2)}) %copy-start) | copy-done | bytes 2097176
  36.3 4.6 %all-to-all-done.1 = f32[128,1,384]{2,1,0:T(1,128)S(1)} async-done(((f32[128,1,384]{2,1,0:T(1,128)}), f32[128,1,384]{2,1,0:T(1,128)S(1)}, u32[]{:S(2)}, u32[]{:S(2)}) %all-to-all-start.1) | async-done | bytes 196640 | tf_op jit(solution)/shard_map/all_to_all | solution.py:774
  41.0 7.1 %tiles.1 = f32[384,128]{1,0:T(8,128)S(1)} custom-call(s32[32,128]{1,0:T(8,128)S(1)} %get-tuple-element.18.live_ref, s32[32,128]{1,0:T(8,128)S(1)} %get-tuple-element.13.refs_1_.rank_ref, bf16[256,4096]{1,0:T(8,128)(2,1)S(1)} %get-tuple-element.19.hot_ref, f32[384,128]{1,0:T(8,128)S(1)} %bitcast.15, f32[3,16,256]{2,1,0:T(8,128)S(1)} %get-tuple-element.20.target_ref), custom_call_target="tpu_custom_call" | custom-call | tf_op jit(solution)/shard_map/tiles/pallas_call | solution.py:671
  48.1 15.4 %all_to_all.29 = f32[128,1,384]{2,1,0:T(1,128)S(1)} all-to-all(f32[128,1,384]{2,1,0:T(1,128)S(1)} %bitcast.17), channel_id=1, replica_groups=mesh['views'=4,'tiles'=32] {'views','tiles'}, dimensions={0} | all-to-all | bytes 393216 | tf_op jit(solution)/shard_map/all_to_all | solution.py:774
  63.5 0.0 copy-done.3
  63.5 2.0 %update.1 = (f32[59,512]{1,0:T(8,128)}, f32[59,512]{1,0:T(8,128)}, f32[59,512]{1,0:T(8,128)}) custom-call(f32[59,512]{1,0:T(8,128)S(1)} %copy-done.3, f32[59,512]{1,0:T(8,128)S(1)} %get-tuple-element.15.refs_1_, f32[59,512]{1,0:T(8,128)S(1)} %get-tuple-element.16.refs_2_, f32[4,6]{1,0:T(4,128)S(1)} %copy-done.9, f32[128,32]{1,0:T(8,128)S(1)} %bitcast.14, ...), custom_call_target="tpu_custom_call" | custom-call | tf_op jit(solution)/shard_map/update/pallas_call | solution.py:821
  (9 shorter events, 0.0 us)
Async XLA Ops:
  0.6 0.7 %copy-start.7 = (s32[1,16,256]{2,1,0:T(8,128)S(1)}, s32[1,16,256]{2,1,0:T(8,128)}, u32[]{:S(2)}) copy-start(s32[1,16,256]{2,1,0:T(8,128)} %param.12) | copy-start | bytes 49156
  3.4 20.9 %all-to-all-start = ((f32[128,1,32]{2,1,0:T(1,128)}), f32[128,1,32]{2,1,0:T(1,128)S(1)}, u32[]{:S(2)}, u32[]{:S(2)}) async-start(f32[128,1,32]{2,1,0:T(1,128)} %bitcast.4), calls=%async_computation | async-start | bytes 131072 | tf_op jit(solution)/shard_map/all_to_all | solution.py:787
  14.9 0.9 %copy-start.2 = (f32[59,512]{1,0:T(8,128)S(1)}, f32[59,512]{1,0:T(8,128)}, u32[]{:S(2)}) copy-start(f32[59,512]{1,0:T(8,128)} %refs_0_.3) | copy-start | bytes 362500
  15.8 0.7 %copy-start.8 = (f32[4,6]{1,0:T(4,128)S(1)}, f32[4,6]{1,0:T(4,128)}, u32[]{:S(2)}) copy-start(f32[4,6]{1,0:T(4,128)} %refs_3_.1) | copy-start | bytes 292
  16.7 46.8 %copy-start.3 = (f32[59,512]{1,0:T(8,128)S(1)}, f32[59,512]{1,0:T(8,128)}, u32[]{:S(2)}) copy-start(f32[59,512]{1,0:T(8,128)} %refs_0_.3) | copy-start | bytes 362500
  16.7 46.7 %copy-start.9 = (f32[4,6]{1,0:T(4,128)S(1)}, f32[4,6]{1,0:T(4,128)}, u32[]{:S(2)}) copy-start(f32[4,6]{1,0:T(4,128)} %refs_3_.1) | copy-start | bytes 292
  26.0 15.0 %all-to-all-start.1 = ((f32[128,1,384]{2,1,0:T(1,128)}), f32[128,1,384]{2,1,0:T(1,128)S(1)}, u32[]{:S(2)}, u32[]{:S(2)}) async-start(f32[128,1,384]{2,1,0:T(1,128)} %bitcast.6), calls=%async_computation.1 | async-start | bytes 393216 | tf_op jit(solution)/shard_map/all_to_all | solution.py:774
  30.6 0.9 %copy-start.4 = (f32[59,512]{1,0:T(8,128)S(1)}, f32[59,512]{1,0:T(8,128)}, u32[]{:S(2)}) copy-start(f32[59,512]{1,0:T(8,128)} %refs_4_.1) | copy-start | bytes 362500
  31.5 0.9 %copy-start.5 = (f32[59,512]{1,0:T(8,128)S(1)}, f32[59,512]{1,0:T(8,128)}, u32[]{:S(2)}) copy-start(f32[59,512]{1,0:T(8,128)} %refs_5_.1) | copy-start | bytes 362500
  32.4 0.8 %copy-start.6 = (f32[1,16,3,256]{3,1,2,0:T(8,128)S(1)}, f32[1,16,3,256]{3,1,2,0:T(8,128)}, u32[]{:S(2)}) copy-start(f32[1,16,3,256]{3,1,2,0:T(8,128)} %param.11) | copy-start | bytes 147460
  33.2 0.7 %copy-start.10 = (s32[1,16]{1,0:T(1,128)S(1)}, s32[1,16]{1,0:T(1,128)}, u32[]{:S(2)}) copy-start(s32[1,16]{1,0:T(1,128)} %refs_2_.1) | copy-start | bytes 196
  35.0 1.3 %copy-start = (bf16[256,4096]{1,0:T(8,128)(2,1)}, bf16[256,4096]{1,0:T(8,128)(2,1)S(1)}, u32[]{:S(2)}) copy-start(bf16[256,4096]{1,0:T(8,128)(2,1)S(1)} %get-tuple-element.17.refs_5_) | copy-start | bytes 6291460
  41.0 22.5 %copy-start.1 = (bf16[256,4096]{1,0:T(8,128)(2,1)S(1)}, bf16[256,4096]{1,0:T(8,128)(2,1)}, u32[]{:S(2)}) copy-start(bf16[256,4096]{1,0:T(8,128)(2,1)} %copy-done) | copy-start | bytes 6291460

commit v5 on v4

--- a/solution.py
+++ b/solution.py
@@ -16,7 +16,7 @@
 KEYS = 2 * VIEWS
 PARAMS = 59
 TABLE = 80
-BLOCK = 4
+BLOCKS = ((0, 4), (4, 4), (8, 4), (12, 4))
 FEATURES = 9
 AXES = ("views", "tiles")
 
@@ -208,6 +208,13 @@
 def dot(left, right, left_dim, right_dim):
     return lax.dot_general(
         left, right, (((left_dim,), (right_dim,)), ((), ())), preferred_element_type=f32
+    )
+
+
+def halved_dot(left_ref, right_ref):
+    half = left_ref.shape[1] // 2
+    return dot(left_ref[:, :half], right_ref[:, :half], 1, 1) - dot(
+        left_ref[:, half:], right_ref[:, half:], 1, 1
     )
 
 
@@ -256,8 +263,9 @@
     owner = lax.div(entries, owned)
     owner_row = owner.astype(f32)
     column = lax.rem(entries, owned)
-    low = lax.rem(column, 256).astype(f32)
-    high = lax.div(column, 256).astype(f32)
+    turn = jnp.where(iota(entries.shape, 0) < per_group, 1.0, -1.0)
+    low = turn * lax.rem(column, 256).astype(f32)
+    high = turn * lax.div(column, 256).astype(f32)
     before = jnp.where(iota((LANES, LANES), 0) < iota((LANES, LANES), 1), 1.0, 0.0)
     adder = jnp.concatenate([before, jnp.ones((LANES, LANES), f32)], axis=1).astype(bf16)
     owner_id = iota((LANES, LANES), 0)
@@ -284,7 +292,7 @@
             ],
             axis=0,
         )
-    requests = dot(hot_ref[...], wanted_ref[...], 1, 1)
+    requests = halved_dot(hot_ref, wanted_ref)
     request_ref[...] = requests[:, :SLOTS] + 256.0 * requests[:, SLOTS:]
 
 
@@ -359,15 +367,12 @@
     target_ref,
     first_ref,
     second_ref,
-    asked_ref,
     hot_ref,
-    column_ref,
     live_ref,
     aim_ref,
     old_first_ref,
     old_second_ref,
 ):
-    fill_columns(flipped_requests(asked_ref), column_ref)
     old_first_ref[...] = beta_one * first_ref[...]
     old_second_ref[...] = beta_two * second_ref[...]
     ids = small_ids(2 * LANES)
@@ -497,47 +502,39 @@
     def rows_of(chunk, count=1):
         return slice(chunk * LANES, (chunk + count) * LANES)
 
-    blocks = per_group // BLOCK
-
-    def shade(at):
+    def shade(first, count):
         for group in range(groups):
-            chunk = group * per_group + at * BLOCK
+            chunk = group * per_group + first
             coef = jnp.concatenate(
-                [coef_ref[pl.ds(chunk + off, 24, stride=chunks), :] for off in range(BLOCK)], axis=1
+                [coef_ref[pl.ds(chunk + off, 24, stride=chunks), :] for off in range(count)], axis=1
             )
-            alpha_ref[rows_of(chunk, BLOCK), :] = jnp.exp2(
+            alpha_ref[rows_of(chunk, count), :] = jnp.exp2(
                 dot(coef.astype(bf16), base_three, 0, 0)
             )
 
-    def load(ref, at):
-        return [ref[rows_of(group * per_group + at), :] for group in range(groups)]
-
-    def keep(refs, at, made):
-        for group in range(groups):
-            for ref, values in zip(refs, made[group]):
-                ref[rows_of(group * per_group + at), :] = values
+    def pairs_of(at, group):
+        start = (group * per_group + at) * LANES
+        return [slice(start + off, start + off + 2 * GROUP) for off in range(0, LANES, 2 * GROUP)]
 
     def weigh(at, clears):
-        alphas = load(alpha_ref, at)
-        out, made = [], []
-        for group in range(groups):
-            clear, alpha = clears[group], alphas[group]
-            weights = []
-            for step in range(steps):
-                weight = alpha[step * GROUP : (step + 1) * GROUP, :] * clear
-                clear = clear - weight
-                weights.append(weight)
-            weight = jnp.concatenate(weights, axis=0)
-            made.append((weight, *pieces(weight, 3)))
-            out.append(clear)
-        keep((weight_ref, high_ref, middle_ref, low_ref), at, made)
-        return tuple(out)
-
-    def blend(at, renders):
+        clears = list(clears)
+        for pair in range(steps // 2):
+            for group in range(groups):
+                rows = pairs_of(at, group)[pair]
+                alpha = alpha_ref[rows, :]
+                weights = []
+                for part in (alpha[:GROUP], alpha[GROUP:]):
+                    weights.append(part * clears[group])
+                    clears[group] = clears[group] - weights[-1]
+                weight = jnp.concatenate(weights, axis=0)
+                weight_ref[rows, :] = weight
+                high_ref[rows, :], middle_ref[rows, :], low_ref[rows, :] = pieces(weight, 3)
+        return tuple(clears)
+
+    def blend(first, count, renders):
         out = []
         for group in range(groups):
-            chunk = group * per_group + at * BLOCK
-            rows = rows_of(chunk, BLOCK)
+            rows = rows_of(group * per_group + first, count)
             paint = paint_ref[:72, rows]
             out.append(
                 renders[group]
@@ -550,13 +547,13 @@
 
     clears = (jnp.ones((GROUP, pixels), f32),) * groups
     renders = (jnp.zeros((72, pixels), f32),) * groups
-    shade(0)
-    for block in range(blocks):
-        if block + 1 < blocks:
-            shade(block + 1)
-        for at in range(block * BLOCK, (block + 1) * BLOCK):
+    shade(*BLOCKS[0])
+    for block, (first, count) in enumerate(BLOCKS):
+        if block + 1 < len(BLOCKS):
+            shade(*BLOCKS[block + 1])
+        for at in range(first, first + count):
             clears = weigh(at, clears)
-        renders = blend(block, renders)
+        renders = blend(first, count, renders)
 
     signs, sign_twos = [], []
     for group in range(groups):
@@ -573,36 +570,33 @@
         signs.append(sign.astype(bf16))
         sign_twos.append(jnp.concatenate([sign, sign], axis=0).astype(bf16))
 
-    def draw(at):
+    def draw(first, count):
         for group in range(groups):
-            rows = rows_of(group * per_group + at * BLOCK, BLOCK)
+            rows = rows_of(group * per_group + first, count)
             pull_ref[rows, :] = dot(paint_ref[:48, rows], sign_twos[group], 0, 0)
 
     def unweigh(at, behinds):
-        pulls, alphas, weights = [load(ref, at) for ref in (pull_ref, alpha_ref, weight_ref)]
-        out, made = [], []
+        behinds = list(behinds)
+        for pair in reversed(range(steps // 2)):
+            for group in range(groups):
+                rows = pairs_of(at, group)[pair]
+                pull, alpha, weight = pull_ref[rows, :], alpha_ref[rows, :], weight_ref[rows, :]
+                by_alpha = []
+                for part in (slice(GROUP, 2 * GROUP), slice(0, GROUP)):
+                    gap = pull[part] - behinds[group]
+                    by_alpha.insert(0, weight[part] * gap)
+                    behinds[group] = behinds[group] + alpha[part] * gap
+                low_ref[rows, :], spread_ref[rows, :] = pieces(jnp.concatenate(by_alpha, axis=0), 2)
+        return tuple(behinds)
+
+    def total(first, count):
         for group in range(groups):
-            pull, alpha, weight = pulls[group], alphas[group], weights[group]
-            behind = behinds[group]
-            by_alpha = [None] * steps
-            for step in reversed(range(steps)):
-                part = slice(step * GROUP, (step + 1) * GROUP)
-                gap = pull[part, :] - behind
-                by_alpha[step] = weight[part, :] * gap
-                behind = behind + alpha[part, :] * gap
-            made.append(pieces(jnp.concatenate(by_alpha, axis=0), 2))
-            out.append(behind)
-        keep((low_ref, spread_ref), at, made)
-        return tuple(out)
-
-    def total(at):
-        for group in range(groups):
-            chunk = group * per_group + at * BLOCK
-            rows = rows_of(chunk, BLOCK)
+            chunk = group * per_group + first
+            rows = rows_of(chunk, count)
             parts = jnp.concatenate([low_ref[rows, :], spread_ref[rows, :]], axis=1)
             moments = dot(base_two, parts, 1, 1)
             by_color = dot(signs[group], high_ref[rows, :], 1, 1)
-            for off in range(BLOCK):
+            for off in range(count):
                 row = (chunk + off) * 16
                 lanes = slice(off * LANES, (off + 1) * LANES)
                 moment_ref[pl.ds(row, 8), :] = moments[:, lanes]
@@ -616,13 +610,14 @@
                     )
 
     behinds = (jnp.zeros((GROUP, pixels), f32),) * groups
-    draw(blocks - 1)
-    for block in reversed(range(blocks)):
+    draw(*BLOCKS[-1])
+    for block in reversed(range(len(BLOCKS))):
         if block:
-            draw(block - 1)
-        for at in reversed(range(block * BLOCK, (block + 1) * BLOCK)):
+            draw(*BLOCKS[block - 1])
+        first, count = BLOCKS[block]
+        for at in reversed(range(first, first + count)):
             behinds = unweigh(at, behinds)
-        total(block)
+        total(first, count)
 
     sums = [moment_ref[pl.ds(at, chunks, stride=16), :] for at in range(6)]
     sum_x = sums[1] - at_u * sums[0]
@@ -641,7 +636,8 @@
 
     half_one = small_ids(HALF)
     below = below.astype(f32)
-    grads = [pieces(jnp.where(live, grad, 0.0), 2) for grad in grads]
+    turn = jnp.where(live, jnp.where(iota(shape, 0) < per_group, 1.0, -1.0), 0.0)
+    grads = [pieces(turn * grad, 2) for grad in grads]
     grads = [[part.astype(f32) for part in split] for split in grads]
     for at in range(chunks):
         mask = one_hot(half_one, below[at : at + 1, :])
@@ -652,7 +648,7 @@
                     part * span + feature * HALF : part * span + (feature + 1) * HALF,
                     at * LANES : (at + 1) * LANES,
                 ] = mask * jnp.broadcast_to(row, (HALF, LANES)).astype(bf16)
-    sent = dot(grad_ref[...], hot_ref[...], 1, 1)
+    sent = halved_dot(grad_ref, hot_ref)
     sent = sent[:span] + sent[span:]
     sent = jnp.concatenate(
         [sent[:, :LANES], sent[:, LANES:], jnp.zeros((3 * LANES - 2 * span, LANES), f32)], axis=0
@@ -706,21 +702,25 @@
     old_second_ref,
     cameras_ref,
     asked_ref,
-    column_ref,
     grads_ref,
     new_params_ref,
     new_first_ref,
     new_second_ref,
     source_ref,
     spread_ref,
+    column_ref,
     gradient_ref,
 ):
     owned = params_ref.shape[1]
     half = owned // 2
-    key = request_keys(flipped_requests(asked_ref))
+    asked = flipped_requests(asked_ref)
+    key = request_keys(asked)
+    fill_columns(asked, column_ref)
     flipped = gathered_rows(grads_ref)
+    first_half = iota(flipped.shape, 0) < FEATURES * HALF
     for part, values in enumerate(pieces(flipped, 2)):
-        source_ref[part * 3 * LANES : (part + 1) * 3 * LANES, :] = values.astype(f32)
+        values = values.astype(f32)
+        source_ref[part * 3 * LANES : (part + 1) * 3 * LANES, :] = jnp.where(first_half, values, -values)
     key_id = iota((KEYS, LANES), 0)
     for slot in range(SLOTS):
         first = slot // HALF * FEATURES * HALF + slot % HALF
@@ -732,7 +732,7 @@
                 row = jnp.broadcast_to(source_ref[at : at + 1, :], (KEYS, LANES))
                 rows.append(jnp.where(mine, row, 0.0))
         spread_ref[:, slot * LANES : (slot + 1) * LANES] = jnp.concatenate(rows, axis=0).astype(bf16)
-    dense = dot(spread_ref[...], column_ref[...], 1, 1)
+    dense = halved_dot(spread_ref, column_ref)
     dense = dense[: FEATURES * KEYS] + dense[FEATURES * KEYS :]
     cotangents = [dense[at * KEYS : (at + 1) * KEYS] for at in range(FEATURES)]
 
@@ -802,11 +802,10 @@
     )(table, asked)
     rows = sent(answers)
     aim = target[0].transpose(1, 0, 2)
-    hot, column, live, aim, old_first, old_second = pl.pallas_call(
+    hot, live, aim, old_first, old_second = pl.pallas_call(
         lambda *refs: prepare_kernel(owned, *refs),
         out_shape=(
             full((2 * LANES, entry_count), bf16),
-            full(columns, bf16),
             full((chunks, LANES), i32),
             full(aim.shape),
             full(params.shape),
@@ -815,7 +814,7 @@
         compiler_params=limits,
         cost_estimate=pl.CostEstimate(flops=4000000, bytes_accessed=2200000, transcendentals=0),
         name="prepare",
-    )(entries, rank, lengths, aim, first_moment, second_moment, asked)
+    )(entries, rank, lengths, aim, first_moment, second_moment)
     row_grads = tiles_call(live, rank, hot, rows, aim)
     shares = sent(row_grads)
     return pl.pallas_call(
@@ -824,11 +823,12 @@
         scratch_shapes=[
             pltpu.VMEM((6 * LANES, LANES), f32),
             pltpu.VMEM((2 * FEATURES * KEYS, SLOTS * LANES), bf16),
+            pltpu.VMEM(columns, bf16),
             pltpu.VMEM((64, owned), f32),
         ],
         compiler_params=limits,
         name="update",
-    )(params, old_first, old_second, cameras, asked, column, shares)
+    )(params, old_first, old_second, cameras, asked, shares)
 
 
 def solution(mesh):

time: 65.9 us -> 64.9 us (0.985)
  waiting for transfers between devices: 12.2 us -> 14.1 us
  local copies, waits for them, and re-layouts: 6.89 us -> 5.56 us
  Pallas kernels: 14.2 us -> 13.3 us
  blocking collectives: 15.4 us -> 14.7 us
    all_to_all x1, waiting for transfers between devices: 4.61 us -> 6.56 us  [sent(): lax.all_to_all(rows.reshape(LANES, 3 * LANES), AXES, 0, 0, tiled=True)]
    unnamed x22 -> x18, local copies, waits for them, and re-layouts: 6.89 us -> 5.56 us
    all_to_all x1, blocking collectives: 15.4 us -> 14.7 us  [sent(): lax.all_to_all(rows.reshape(LANES, 3 * LANES), AXES, 0, 0, tiled=True)]
  transfers between devices with their start and end apart: 2 -> 2, of which waited for: 2 -> 2; matrix products, arithmetic and copies ran while one was open for 0% -> 0% of each run, Pallas kernels for 2% -> 1%
where the time goes in v5:
time: 64.9 us; the launch traced here: 64.5 us
  starting transfers between devices  16.1 us (25%)
  blocking collectives  14.7 us (23%)
  waiting for transfers between devices  14.1 us (22%)
  Pallas kernels  13.3 us (20%)
  local copies, waits for them, and re-layouts  5.56 us (9%)
  between operations  0.72 us (1%)
    all_to_all x1, blocking collectives, sent(): lax.all_to_all(rows.reshape(LANES, 3 * LANES), AXES, 0, 0, tiled=True)  14.7 us
    all_to_all x1, starting transfers between devices, per_device(): asked = lax.all_to_all(requests, AXES, 0, 0, tiled=True)  11.5 us
    all_to_all x1, waiting for transfers between devices, per_device(): asked = lax.all_to_all(requests, AXES, 0, 0, tiled=True)  7.58 us
    pallas_call x1, Pallas kernels, tiles_call(): pl.pallas_call(tile_kernel, out_shape=jax.ShapeDtypeStruct((3 * LANES, LA...  6.74 us
    all_to_all x1, waiting for transfers between devices, sent(): lax.all_to_all(rows.reshape(LANES, 3 * LANES), AXES, 0, 0, tiled=True)  6.56 us
    unnamed x18, local copies, waits for them, and re-layouts  5.56 us
    all_to_all x1, starting transfers between devices, sent(): lax.all_to_all(rows.reshape(LANES, 3 * LANES), AXES, 0, 0, tiled=True)  4.62 us
    pallas_call x1, Pallas kernels, per_device(): pl.pallas_call(lambda *refs: update_kernel(frame, *refs), out_shape=(full...  2.3 us
  transfers between devices with their start and end apart: 2, of which 2 were waited for; matrix products, arithmetic and copies ran while one was open for 0% of the time, Pallas kernels for 1%

profile of v5, /device:TPU:1, one launch (start us, length us, event | category | flops | bytes accessed | tf_op | source)
XLA Modules:
  0.0 64.5 jit_solution(1712677327108901272)
XLA Ops:
  0.6 0.0 copy-start.5
  0.6 0.7 %copy-done.5 = s32[1,16,256]{2,1,0:T(8,128)S(1)} copy-done((s32[1,16,256]{2,1,0:T(8,128)S(1)}, s32[1,16,256]{2,1,0:T(8,128)}, u32[]{:S(2)}) %copy-start.5) | copy-done | bytes 16408
  1.3 1.8 %rank.1 = (s32[32,128]{1,0:T(8,128)S(1)}, s32[32,128]{1,0:T(8,128)S(1)}, f32[128,32]{1,0:T(8,128)}) custom-call(s32[16,256]{1,0:T(8,128)S(1)} %bitcast.18), custom_call_target="tpu_custom_call" | custom-call | tf_op jit(solution)/shard_map/rank/pallas_call | solution.py:777
  3.2 11.5 %all-to-all-start = ((f32[128,1,32]{2,1,0:T(1,128)}), f32[128,1,32]{2,1,0:T(1,128)S(1)}, u32[]{:S(2)}, u32[]{:S(2)}) async-start(f32[128,1,32]{2,1,0:T(1,128)} %bitcast.4), calls=%async_computation | async-start | bytes 131072 | tf_op jit(solution)/shard_map/all_to_all | solution.py:787
  14.7 0.0 copy-start
  14.7 0.9 %copy-done = f32[59,512]{1,0:T(8,128)S(1)} copy-done((f32[59,512]{1,0:T(8,128)S(1)}, f32[59,512]{1,0:T(8,128)}, u32[]{:S(2)}) %copy-start) | copy-done | bytes 120856
  15.6 0.7 %copy-done.6 = f32[4,6]{1,0:T(4,128)S(1)} copy-done((f32[4,6]{1,0:T(4,128)S(1)}, f32[4,6]{1,0:T(4,128)}, u32[]{:S(2)}) %copy-start.6) | copy-done | bytes 120
  16.3 0.2 project.1.table_ref
  16.5 0.0 copy-start.1
  16.5 0.0 copy-start.7
  16.5 7.6 %all-to-all-done = f32[128,1,32]{2,1,0:T(1,128)S(1)} async-done(((f32[128,1,32]{2,1,0:T(1,128)}), f32[128,1,32]{2,1,0:T(1,128)S(1)}, u32[]{:S(2)}, u32[]{:S(2)}) %all-to-all-start) | async-done | bytes 16416 | tf_op jit(solution)/shard_map/all_to_all | solution.py:787
  24.1 1.6 %answer.1 = f32[384,128]{1,0:T(8,128)} custom-call(bf16[240,256]{1,0:T(8,128)(2,1)S(1)} %project.1.table_ref, f32[128,32]{1,0:T(8,128)S(1)} %bitcast.15), custom_call_target="tpu_custom_call" | custom-call | tf_op jit(solution)/shard_map/answer/pallas_call | solution.py:796
  25.8 4.6 %all-to-all-start.1 = ((f32[128,1,384]{2,1,0:T(1,128)}), f32[128,1,384]{2,1,0:T(1,128)S(1)}, u32[]{:S(2)}, u32[]{:S(2)}) async-start(f32[128,1,384]{2,1,0:T(1,128)} %bitcast.6), calls=%async_computation.1 | async-start | bytes 393216 | tf_op jit(solution)/shard_map/all_to_all | solution.py:774
  30.4 0.0 copy-start.2
  30.4 0.9 %copy-done.2 = f32[59,512]{1,0:T(8,128)S(1)} copy-done((f32[59,512]{1,0:T(8,128)S(1)}, f32[59,512]{1,0:T(8,128)}, u32[]{:S(2)}) %copy-start.2) | copy-done | bytes 120856
  31.3 0.9 %copy-done.3 = f32[59,512]{1,0:T(8,128)S(1)} copy-done((f32[59,512]{1,0:T(8,128)S(1)}, f32[59,512]{1,0:T(8,128)}, u32[]{:S(2)}) %copy-start.3) | copy-done | bytes 120856
  32.2 0.8 %copy-done.4 = f32[1,16,3,256]{3,1,2,0:T(8,128)S(1)} copy-done((f32[1,16,3,256]{3,1,2,0:T(8,128)S(1)}, f32[1,16,3,256]{3,1,2,0:T(8,128)}, u32[]{:S(2)}) %copy-start.4) | copy-done | bytes 49176
  33.0 0.7 %copy-done.8 = s32[1,16]{1,0:T(1,128)S(1)} copy-done((s32[1,16]{1,0:T(1,128)S(1)}, s32[1,16]{1,0:T(1,128)}, u32[]{:S(2)}) %copy-start.8) | copy-done | bytes 88
  33.6 0.5 prepare.1
  34.2 6.6 %all-to-all-done.1 = f32[128,1,384]{2,1,0:T(1,128)S(1)} async-done(((f32[128,1,384]{2,1,0:T(1,128)}), f32[128,1,384]{2,1,0:T(1,128)S(1)}, u32[]{:S(2)}, u32[]{:S(2)}) %all-to-all-start.1) | async-done | bytes 196640 | tf_op jit(solution)/shard_map/all_to_all | solution.py:774
  40.7 6.7 %tiles.1 = f32[384,128]{1,0:T(8,128)S(1)} custom-call(s32[32,128]{1,0:T(8,128)S(1)} %get-tuple-element.16.live_ref, s32[32,128]{1,0:T(8,128)S(1)} %get-tuple-element.12.refs_1_.rank_ref, bf16[256,4096]{1,0:T(8,128)(2,1)S(1)} %get-tuple-element.17.hot_ref, f32[384,128]{1,0:T(8,128)S(1)} %bitcast.12, f32[3,16,256]{2,1,0:T(8,128)S(1)} %get-tuple-element.18.target_ref), custom_call_target="tpu_custom_call" | custom-call | tf_op jit(solution)/shard_map/tiles/pallas_call | solution.py:667
  47.5 14.7 %all_to_all.29 = f32[128,1,384]{2,1,0:T(1,128)S(1)} all-to-all(f32[128,1,384]{2,1,0:T(1,128)S(1)} %bitcast.13), channel_id=1, replica_groups=mesh['views'=4,'tiles'=32] {'views','tiles'}, dimensions={0} | all-to-all | bytes 393216 | tf_op jit(solution)/shard_map/all_to_all | solution.py:774
  62.2 0.0 copy-done.1
  62.2 2.3 %update.1 = (f32[59,512]{1,0:T(8,128)}, f32[59,512]{1,0:T(8,128)}, f32[59,512]{1,0:T(8,128)}) custom-call(f32[59,512]{1,0:T(8,128)S(1)} %copy-done.1, f32[59,512]{1,0:T(8,128)S(1)} %get-tuple-element.13.refs_1_, f32[59,512]{1,0:T(8,128)S(1)} %get-tuple-element.14.refs_2_, f32[4,6]{1,0:T(4,128)S(1)} %copy-done.7, f32[128,32]{1,0:T(8,128)S(1)} %bitcast.16, ...), custom_call_target="tpu_custom_call" | custom-call | tf_op jit(solution)/shard_map/update/pallas_call | solution.py:820
  (5 shorter events, 0.0 us)
Async XLA Ops:
  0.6 0.7 %copy-start.5 = (s32[1,16,256]{2,1,0:T(8,128)S(1)}, s32[1,16,256]{2,1,0:T(8,128)}, u32[]{:S(2)}) copy-start(s32[1,16,256]{2,1,0:T(8,128)} %param.12) | copy-start | bytes 49156
  3.2 20.9 %all-to-all-start = ((f32[128,1,32]{2,1,0:T(1,128)}), f32[128,1,32]{2,1,0:T(1,128)S(1)}, u32[]{:S(2)}, u32[]{:S(2)}) async-start(f32[128,1,32]{2,1,0:T(1,128)} %bitcast.4), calls=%async_computation | async-start | bytes 131072 | tf_op jit(solution)/shard_map/all_to_all | solution.py:787
  14.7 0.9 %copy-start = (f32[59,512]{1,0:T(8,128)S(1)}, f32[59,512]{1,0:T(8,128)}, u32[]{:S(2)}) copy-start(f32[59,512]{1,0:T(8,128)} %refs_0_.3) | copy-start | bytes 362500
  15.6 0.7 %copy-start.6 = (f32[4,6]{1,0:T(4,128)S(1)}, f32[4,6]{1,0:T(4,128)}, u32[]{:S(2)}) copy-start(f32[4,6]{1,0:T(4,128)} %refs_3_.1) | copy-start | bytes 292
  16.5 45.7 %copy-start.1 = (f32[59,512]{1,0:T(8,128)S(1)}, f32[59,512]{1,0:T(8,128)}, u32[]{:S(2)}) copy-start(f32[59,512]{1,0:T(8,128)} %refs_0_.3) | copy-start | bytes 362500
  16.5 45.7 %copy-start.7 = (f32[4,6]{1,0:T(4,128)S(1)}, f32[4,6]{1,0:T(4,128)}, u32[]{:S(2)}) copy-start(f32[4,6]{1,0:T(4,128)} %refs_3_.1) | copy-start | bytes 292
  25.8 15.0 %all-to-all-start.1 = ((f32[128,1,384]{2,1,0:T(1,128)}), f32[128,1,384]{2,1,0:T(1,128)S(1)}, u32[]{:S(2)}, u32[]{:S(2)}) async-start(f32[128,1,384]{2,1,0:T(1,128)} %bitcast.6), calls=%async_computation.1 | async-start | bytes 393216 | tf_op jit(solution)/shard_map/all_to_all | solution.py:774
  30.4 0.9 %copy-start.2 = (f32[59,512]{1,0:T(8,128)S(1)}, f32[59,512]{1,0:T(8,128)}, u32[]{:S(2)}) copy-start(f32[59,512]{1,0:T(8,128)} %refs_4_.1) | copy-start | bytes 362500
  31.3 0.9 %copy-start.3 = (f32[59,512]{1,0:T(8,128)S(1)}, f32[59,512]{1,0:T(8,128)}, u32[]{:S(2)}) copy-start(f32[59,512]{1,0:T(8,128)} %refs_5_.1) | copy-start | bytes 362500
  32.2 0.8 %copy-start.4 = (f32[1,16,3,256]{3,1,2,0:T(8,128)S(1)}, f32[1,16,3,256]{3,1,2,0:T(8,128)}, u32[]{:S(2)}) copy-start(f32[1,16,3,256]{3,1,2,0:T(8,128)} %param.11) | copy-start | bytes 147460
  33.0 0.7 %copy-start.8 = (s32[1,16]{1,0:T(1,128)S(1)}, s32[1,16]{1,0:T(1,128)}, u32[]{:S(2)}) copy-start(s32[1,16]{1,0:T(1,128)} %refs_2_.1) | copy-start | bytes 196
